TPU v7x, 32 devices: a whole 2x2x4 slice. The times are simulated.
32 devices in a mesh: seq: 4 (over y, core), chan: 8 (over z, x).
Axes of the slice: x: 2, y: 2, z: 4, core: 2. Of those that a mesh axis runs over, the one named last changes fastest.
Arguments:
- queries: bfloat16 [8, 512, 4096], P('chan', 'seq'), may hold values from -256 to 256
- keys: bfloat16 [8, 512, 1024], P('chan', 'seq'), may hold values from -6 to 6
- values: bfloat16 [8, 512, 1024], P('chan', 'seq'), may hold values from -6 to 6
- doc_lengths: int32 [8, 16], P('chan'), may hold values from 1 to 256, 512 in all within a row
- rank_in: bfloat16 [4096, 256], replicated, may hold values from -0.09375 to 0.09375
- bc_weight: bfloat16 [4096, 32], replicated, may hold values from -0.09375 to 0.09375
- rank_out: bfloat16 [256, 4096], replicated, may hold values from -0.375 to 0.375
- dt_bias: float32 [4096], replicated, may hold values from -8 to -6
- a_log: float32 [4096, 16], replicated, may hold values from -10 to 4
- skip_gain: float32 [4096], replicated, may hold values from 0.5 to 1.5
Outputs:
- attn_out: bfloat16 [8, 512, 4096], P('chan', 'seq')
- ssm_out: bfloat16 [8, 512, 4096], P('chan', None, 'seq')
Inputs may be any that keep to these rules, and one draw needn't show every extreme that they name: `doc_lengths`: each row's entries are the lengths of its 16 documents in order and sum to 512; some document of every row is 256 long.
All inputs are finite; a program needn't handle non-finite values.
Results may differ from a plain program's by a relative error of at most 0.0091.
Values may be sent and summed in bfloat16 or wider, within the bound.
No kernel may reach another device: no remote copies, remote signals or barrier semaphores. Data moves between devices by JAX's collectives and lax.ppermute only.
A program may use at most 128 MiB of HBM per device.

v0:
```python
import functools
import math

import jax
import jax.numpy as jnp
from jax import lax
from jax.experimental import pallas as pl
from jax.experimental.pallas import tpu as pltpu
from jax.sharding import PartitionSpec as P

QUERY_HEADS = 32
KEY_VALUE_HEADS = 8
HEAD_SIZE = 128
GROUP = QUERY_HEADS // KEY_VALUE_HEADS
NS = 16
RANK = 256
CORES = 2
LANES = 128
SUBLANES = 8
MAPS = 2 * NS
LOG2E = 1.4426950408889634

masked_fill = -1e30
params = pltpu.CompilerParams(vmem_limit_bytes=60 << 20)


def split(value):
    coarse = value.astype(jnp.bfloat16)
    return coarse, (value - coarse.astype(jnp.float32)).astype(jnp.bfloat16)


def run_copies(pairs, sems):
    copies = [
        pltpu.make_async_copy(source, target, sems.at[i]) for i, (source, target) in enumerate(pairs)
    ]
    for copy in copies:
        copy.start()
    for copy in copies:
        copy.wait()


def columns_of(ref, index, size):
    return ref.at[:, pl.ds(pl.multiple_of(index * size, LANES), size)]


def heads_kernel(key_ref, value_ref, own_ref, their_ref, sems):
    core = lax.rem(lax.axis_index("seq"), CORES)
    wide = own_ref.shape[3]
    halves = key_ref.shape[1] // wide // own_ref.shape[0]
    pairs = []
    for target, which in ((own_ref, core), (their_ref, 1 - core)):
        for chip in range(own_ref.shape[0]):
            index = chip * halves + (which if halves == CORES else 0)
            for kind, source in enumerate((key_ref, value_ref)):
                pairs.append((columns_of(source, index, wide), target.at[chip, kind]))
    run_copies(pairs, sems)


def select_heads(keys, values, chips, wide):
    shape = jax.ShapeDtypeStruct((chips, 2, keys.shape[0], wide), keys.dtype)
    return pl.pallas_call(
        heads_kernel,
        in_specs=[pl.BlockSpec(memory_space=pl.ANY)] * 2,
        out_shape=[shape, shape],
        scratch_shapes=[pltpu.SemaphoreType.DMA((4 * chips,))],
        compiler_params=params,
        name="select_heads",
    )(keys, values)


def join_kernel(sent_ref, stayed_ref, got_sent_ref, got_stayed_ref, out_ref, sems):
    place = lax.axis_index("seq")
    core, chip = lax.rem(place, CORES), place // CORES
    rows = out_ref.shape[0]
    others, _, width = sent_ref.shape
    here = pl.ds(pl.multiple_of(core * rows, rows), rows)
    pairs = []
    for first, rest, which in (
        (stayed_ref, sent_ref, core), (got_stayed_ref, got_sent_ref, 1 - core)
    ):
        for step in range(others + 1):
            source = first.at[0, here, :] if step == 0 else rest.at[step - 1, here, :]
            owner = lax.rem(chip + step, others + 1)
            pairs.append((source, columns_of(out_ref, owner * CORES + which, width)))
    run_copies(pairs, sems)


def join_heads(sent, stayed, got_sent, got_stayed):
    others, rows, width = sent.shape
    return pl.pallas_call(
        join_kernel,
        in_specs=[pl.BlockSpec(memory_space=pl.ANY)] * 4,
        out_shape=jax.ShapeDtypeStruct(
            (rows // CORES, (others + 1) * CORES * width), sent.dtype
        ),
        scratch_shapes=[pltpu.SemaphoreType.DMA((CORES * (others + 1),))],
        compiler_params=params,
        name="join_heads",
    )(sent, stayed, got_sent, got_stayed)


def attend_kernel(
    place_ref, doc_ref, mine_ref, theirs_ref, own_ref, swap_ref, near_ref, far_ref,
    rank_ref, map_ref, *rest, chips,
):
    send_ref, stay_ref, part_ref, mask_ref = rest[-4:]
    step = pl.program_id(0)
    rows = mine_ref.shape[0]
    group = mine_ref.shape[1] // HEAD_SIZE
    chip, core = place_ref[0], place_ref[1]
    first_core = core == 0

    def above(shape):
        row = lax.rem(lax.broadcasted_iota(jnp.int32, shape, 0), rows)
        return lax.broadcasted_iota(jnp.int32, shape, 1) > row

    @pl.when(step == 0)
    def _():
        part_ref[...] = jnp.zeros_like(part_ref)
        own = chip * CORES + core
        swapped = chip * CORES + 1 - core
        near, far = own - CORES, swapped - CORES
        lane = lax.broadcasted_iota(jnp.int32, (rows, rows), 1)
        row = lax.broadcasted_iota(jnp.int32, (rows, rows), 0)
        for item, (place, before, middle) in enumerate(
            (
                (own, near, jnp.where(first_core, far, swapped)),
                (swapped, far, jnp.where(first_core, own, near)),
            )
        ):
            query_pos = place * rows + row
            start = jnp.zeros((rows, rows), jnp.int32)
            bound = jnp.int32(0)
            for doc in range(doc_ref.shape[1]):
                bound = bound + doc_ref[0, doc]
                start = jnp.where(query_pos >= bound, bound, start)
            ends = jnp.where(lane > row, before, place) * rows + lane
            mask_ref[item, :, :rows] = jnp.where(
                (ends >= start) & (ends <= query_pos), 0.0, masked_fill
            )
            mask_ref[item, :, rows:] = jnp.where(
                middle * rows + lane >= start, 0.0, masked_fill
            )

    scale = LOG2E / math.sqrt(HEAD_SIZE)
    ones = jnp.ones((3 * rows, HEAD_SIZE), jnp.bfloat16)

    def windows(kind):
        own, swapped = own_ref[0, kind], swap_ref[0, kind]
        near, far = near_ref[0, kind], far_ref[0, kind]
        return (
            jnp.concatenate([near, own, jnp.where(first_core, far, swapped)], axis=0),
            jnp.concatenate([far, swapped, jnp.where(first_core, own, near)], axis=0),
        )

    scores = []
    for keys, query in zip(windows(0), (mine_ref[...], theirs_ref[...])):
        stacked = jnp.concatenate(
            [query[:, i * HEAD_SIZE : (i + 1) * HEAD_SIZE] for i in range(group)], axis=0
        )
        scores.append(
            lax.dot_general(
                stacked, keys, (((1,), (1,)), ((), ())), preferred_element_type=jnp.float32
            )
        )
    outputs = []
    before = above((group * rows, rows))
    for item, (values, score) in enumerate(zip(windows(1), scores)):
        fill = mask_ref[item]
        ends = jnp.where(before, score[:, :rows], score[:, rows : 2 * rows])
        kept = jnp.concatenate([ends, score[:, 2 * rows :]], axis=1)
        kept = jnp.concatenate(
            [kept[i * rows : (i + 1) * rows, :] + fill for i in range(group)], axis=0
        )
        peak = jnp.max(kept, axis=1, keepdims=True)
        raw = jnp.exp2((kept - peak) * scale).astype(jnp.bfloat16)
        ends = raw[:, :rows]
        none = jnp.zeros_like(ends)
        spread = jnp.concatenate(
            [jnp.where(before, ends, none), jnp.where(before, none, ends), raw[:, rows:]], axis=1
        )
        both = jnp.dot(
            spread, jnp.concatenate([values, ones], axis=1), preferred_element_type=jnp.float32
        )
        mixed = both[:, :HEAD_SIZE] * pl.reciprocal(both[:, HEAD_SIZE:])
        mixed = mixed.astype(jnp.bfloat16)
        outputs.append(
            jnp.concatenate([mixed[i * rows : (i + 1) * rows, :] for i in range(group)], axis=1)
        )
    stream = jnp.concatenate(
        [
            jnp.where(first_core, outputs[0], outputs[1]),
            jnp.where(first_core, outputs[1], outputs[0]),
        ],
        axis=0,
    )
    last = step >= pl.num_programs(0) - pl.num_programs(0) // chips

    @pl.when(last)
    def _():
        stay_ref[0] = stream

    @pl.when(jnp.logical_not(last))
    def _():
        send_ref[0] = stream

    both = CORES * rows
    part_ref[:both, :] += jnp.dot(stream, rank_ref[...], preferred_element_type=jnp.float32)
    part_ref[both:, :] += lax.dot_general(
        map_ref[...], stream, (((1,), (1,)), ((), ())), preferred_element_type=jnp.float32
    )


def attend(place, doc_lengths, queries, blocks, rank_in, map_rows, after):
    mine, theirs = queries
    chips, _, rows, columns = blocks[0].shape
    heads = columns // HEAD_SIZE
    width = mine.shape[1] // (chips * CORES)
    wide = width // heads

    def owner(j, s):
        return lax.rem(s[0] + 1 + j // heads, chips)

    def column(j, s):
        return (owner(j, s) * CORES + s[1]) * heads + lax.rem(j, heads)

    def sent(j, s):
        at = jnp.minimum(j, (chips - 1) * heads - 1)
        return (at // heads, 0, lax.rem(at, heads))

    query = pl.BlockSpec((rows, wide), lambda j, s: (0, column(j, s)))
    block = pl.BlockSpec(
        (1, 2, rows, HEAD_SIZE), lambda j, s: (owner(j, s), 0, 0, lax.rem(j, heads))
    )
    return pl.pallas_call(
        functools.partial(attend_kernel, chips=chips),
        grid_spec=pltpu.PrefetchScalarGridSpec(
            num_scalar_prefetch=1,
            grid=(chips * heads,),
            in_specs=[pl.BlockSpec(memory_space=pltpu.SMEM), query, query]
            + [block] * 4
            + [
                pl.BlockSpec((wide, RANK), lambda j, s: (column(j, s), 0)),
                pl.BlockSpec((2 * NS, wide), lambda j, s: (0, column(j, s))),
            ]
            + [pl.BlockSpec(memory_space=pl.ANY)] * len(after),
            out_specs=[
                pl.BlockSpec((1, CORES * rows, wide), sent),
                pl.BlockSpec(
                    (1, CORES * rows, wide),
                    lambda j, s: (0, 0, jnp.maximum(j - (chips - 1) * heads, 0)),
                ),
                pl.BlockSpec((CORES * rows + 2 * NS, RANK), lambda j, s: (0, 0)),
            ],
            scratch_shapes=[pltpu.VMEM((2, rows, 2 * rows), jnp.float32)],
        ),
        out_shape=[
            jax.ShapeDtypeStruct((chips - 1, CORES * rows, width), jnp.bfloat16),
            jax.ShapeDtypeStruct((1, CORES * rows, width), jnp.bfloat16),
            jax.ShapeDtypeStruct((CORES * rows + 2 * NS, RANK), jnp.float32),
        ],
        compiler_params=params,
        cost_estimate=pl.CostEstimate(flops=5 * 10**9, bytes_accessed=1 << 22, transcendentals=0),
        name="attend",
    )(place, doc_lengths, mine, theirs, *blocks, rank_in, map_rows, *after)


def low_kernel(mine_ref, theirs_ref, out_ref):
    out_ref[...] = (mine_ref[...] + theirs_ref[...]).astype(jnp.bfloat16)


def low_and_maps(mine, theirs):
    return pl.pallas_call(
        low_kernel,
        out_shape=jax.ShapeDtypeStruct(mine.shape, jnp.bfloat16),
        compiler_params=params,
        cost_estimate=pl.CostEstimate(flops=1, bytes_accessed=1, transcendentals=0),
        name="low_and_maps",
    )(mine, theirs)


def softplus(value):
    small = jnp.exp(-jnp.abs(value))
    tail = jnp.where(small < 0.00390625, small * (1.0 - 0.5 * small), jnp.log(1.0 + small))
    return jnp.maximum(value, 0.0) + tail


def add_states(rates_ref, state_ref, total_ref, states, totals):
    state_ref[...] = jnp.exp2(rates_ref[...] * totals) * state_ref[...] + states
    total_ref[...] = total_ref[...] + totals


def sums_within(steps):
    rows = steps.shape[0]
    at = lax.broadcasted_iota(jnp.int32, (rows, rows), 0)
    of = lax.broadcasted_iota(jnp.int32, (rows, rows), 1)
    upto = jnp.where(of <= at, 1.0, 0.0).astype(jnp.bfloat16)
    return jnp.dot(upto, steps, preferred_element_type=jnp.float32)


def step_kernel(
    place_ref, stream_ref, low_ref, map_ref, cols_ref, bias_ref, rates_ref, *rest
):
    own_state_ref, own_total_ref = rest[:2]
    steps_ref, sums_ref, maps_ref, carry_ref, state_ref, total_ref, wide_ref, turn_ref = rest[3:]
    block = pl.program_id(0)
    rows, width = stream_ref.shape[1:]

    @pl.when(block == 0)
    def _():
        state_ref[...] = jnp.zeros_like(state_ref)
        total_ref[...] = jnp.zeros_like(total_ref)
        for n in range(NS):
            wide_ref[n * SUBLANES : (n + 1) * SUBLANES, :] = jnp.broadcast_to(
                rates_ref[n : n + 1, :], (SUBLANES, width)
            )

    @pl.when(block == place_ref[0] * CORES)
    def _():
        add_states(rates_ref, state_ref, total_ref, own_state_ref[...], own_total_ref[...])

    maps = map_ref[0].astype(jnp.float32)
    maps_ref[0] = maps
    logits = jnp.dot(low_ref[0], cols_ref[...], preferred_element_type=jnp.float32)
    steps = softplus(logits + bias_ref[...]).astype(jnp.bfloat16)
    steps_ref[...] = steps
    push = steps * stream_ref[0]
    within = sums_within(steps)
    sums_ref[...] = within.astype(jnp.bfloat16)
    whole = within[rows - 1 :, :]
    left = whole - within
    some, chunk, several = rows // 2, CORES * LANES, 4
    state_row = lax.broadcasted_iota(jnp.int32, (NS, some), 0)
    for first in range(0, rows, some):
        span = slice(first, first + some)
        chosen = [
            jnp.concatenate(
                [
                    jnp.where(state_row == m, maps[:NS, span], 0.0).astype(jnp.bfloat16)
                    for m in range(n, n + several)
                ],
                axis=1,
            )
            for n in range(0, NS, several)
        ]
        for item in range(width // chunk):
            lanes = slice(item * chunk, (item + 1) * chunk)
            left_here = left[span, lanes].reshape(some // SUBLANES, SUBLANES, chunk)
            push_here = push[span, lanes]
            added = state_ref[:, lanes]
            if first == 0:
                added = jnp.exp2(rates_ref[:, lanes] * whole[:, lanes]) * added
            for n in range(0, NS, several):
                pushed = []
                for m in range(n, n + several):
                    rate = wide_ref[m * SUBLANES : (m + 1) * SUBLANES, lanes]
                    decay = jnp.exp2(left_here * rate[None]).reshape(some, chunk)
                    pushed.append(decay.astype(jnp.bfloat16) * push_here)
                added = added + jnp.dot(
                    chosen[n // several],
                    jnp.concatenate(pushed, axis=0),
                    preferred_element_type=jnp.float32,
                )
            state_ref[:, lanes] = added
    total_ref[...] = total_ref[...] + whole

    count = pl.num_programs(0)

    @pl.when(block == count - 1)
    def _():
        @pl.when(place_ref[0] * CORES == count)
        def _():
            add_states(rates_ref, state_ref, total_ref, own_state_ref[...], own_total_ref[...])

        write_carry(carry_ref.at[0], state_ref[...], total_ref[...], turn_ref)
        for target in range(1, carry_ref.shape[0]):
            carry_ref[target] = carry_ref[0]


def step_sizes(place, stream, lows, cols, bias, rates, state, total, targets, after):
    others = stream.shape[0]
    chips = others + 1
    rows, width = stream.shape[1] // CORES, stream.shape[2]
    map_row = CORES * rows // MAPS
    blocks = others * CORES
    carry = (targets, (width // LANES + 1) * NS, LANES)

    def slot(b, s):
        chip = b // CORES
        return lax.rem(s[0] - jnp.where(chip < s[0], chip, chip + 1) + chips, chips) - 1

    def core(b):
        return lax.rem(b, CORES)

    def fixed(*shape):
        return pl.BlockSpec(shape, lambda b, s: (0,) * len(shape))

    return pl.pallas_call(
        step_kernel,
        grid_spec=pltpu.PrefetchScalarGridSpec(
            num_scalar_prefetch=1,
            grid=(blocks,),
            in_specs=[
                pl.BlockSpec((1, rows, width), lambda b, s: (slot(b, s), core(b), 0)),
                pl.BlockSpec((1, rows, RANK), lambda b, s: (slot(b, s), core(b), 0)),
                pl.BlockSpec((1, MAPS, rows), lambda b, s: (slot(b, s), map_row, core(b))),
                fixed(*cols.shape),
                fixed(*bias.shape),
                fixed(*rates.shape),
                fixed(*state.shape),
                fixed(*total.shape),
                pl.BlockSpec(memory_space=pl.ANY),
            ],
            out_specs=[
                pl.BlockSpec((rows, width), lambda b, s: (b, 0)),
                pl.BlockSpec((rows, width), lambda b, s: (b, 0)),
                pl.BlockSpec((1, 2 * NS, rows), lambda b, s: (b, 0, 0)),
                fixed(*carry),
            ],
            scratch_shapes=[
                pltpu.VMEM((NS, width), jnp.float32),
                pltpu.VMEM((1, width), jnp.float32),
                pltpu.VMEM((NS * SUBLANES, width), jnp.float32),
                pltpu.VMEM((SUBLANES, LANES), jnp.float32),
            ],
        ),
        out_shape=[
            jax.ShapeDtypeStruct((blocks * rows, width), jnp.bfloat16),
            jax.ShapeDtypeStruct((blocks * rows, width), jnp.bfloat16),
            jax.ShapeDtypeStruct((blocks, 2 * NS, rows), jnp.float32),
            jax.ShapeDtypeStruct(carry, jnp.bfloat16),
        ],
        compiler_params=params,
        name="step_sizes",
    )(place, stream, lows, lows, cols, bias, rates, state, total, after)


def write_carry(out_ref, state, total, turn_ref):
    tile = state.shape[1] // LANES
    turn_ref[...] = jnp.zeros_like(turn_ref)
    for item in range(tile):
        lanes = slice(item * LANES, (item + 1) * LANES)
        turn_ref[item : item + 1, :] = total[:, lanes]
        out_ref[item * NS : (item + 1) * NS, :] = state[:, lanes].astype(jnp.bfloat16)
    out_ref[tile * NS :, :] = jnp.concatenate(split(turn_ref[...]), axis=0)


def follow(carry_ref, rates_ref, state_ref):
    tile = state_ref.shape[1] // LANES
    sums = carry_ref[tile * NS :, :].astype(jnp.float32)
    sums = sums[:SUBLANES, :] + sums[SUBLANES:, :]
    for item in range(tile):
        lanes = slice(item * LANES, (item + 1) * LANES)
        decay = jnp.exp2(rates_ref[:, lanes] * sums[item : item + 1, :])
        added = carry_ref[item * NS : (item + 1) * NS, :].astype(jnp.float32)
        state_ref[:, lanes] = decay * state_ref[:, lanes] + added
    return sums


def scan_blocks(stream_ref, steps_ref, maps, rates_ref, gain_ref, out_ref, state_ref, work_refs):
    out_of_ref, *hist_refs = work_refs
    rows, width = steps_ref.shape
    source = lax.broadcasted_iota(jnp.int32, (LANES, NS * NS), 0)
    column = lax.rem(lax.broadcasted_iota(jnp.int32, (LANES, NS * NS), 1), NS)
    token = lax.rem(lax.broadcasted_iota(jnp.int32, (rows, NS * NS), 0), NS)
    slot = lax.broadcasted_iota(jnp.int32, (rows, NS * NS), 1) // NS
    turned = jnp.concatenate(
        [maps, jnp.zeros((LANES - 2 * NS, rows), jnp.float32)], axis=0
    ).T.astype(jnp.bfloat16)
    pick = jnp.where(source == NS + column, 1.0, 0.0).astype(jnp.bfloat16)
    spread = jnp.dot(turned, pick, preferred_element_type=jnp.float32)
    out_of_ref[...] = jnp.where(token == slot, spread, 0.0).astype(jnp.bfloat16)
    map_in = maps[:NS, :]
    half = width // 2

    def finish(first, hist_ref):
        here = pl.ds(first, NS)
        mixed = jnp.dot(out_of_ref[here, :], hist_ref[...], preferred_element_type=jnp.float32)
        direct = gain_ref[...] * stream_ref[0, here, :].astype(jnp.float32)
        out_ref[here, :] = (mixed + direct).astype(jnp.bfloat16)

    def advance(first, hist_ref):
        here = pl.ds(first, NS)
        into = pltpu.roll(map_in, lax.rem(rows - first, rows), 1)
        for lanes in (slice(0, half), slice(half, width)):
            state = state_ref[:, lanes]
            rates = rates_ref[:, lanes]
            steps = steps_ref[here, lanes].astype(jnp.float32)
            push = steps * stream_ref[0, here, lanes].astype(jnp.float32)
            for near in range(NS):
                this = slice(near, near + 1)
                state = jnp.exp2(rates * steps[this, :]) * state + into[:, this] * push[this, :]
                hist_ref[near * NS : (near + 1) * NS, lanes] = state.astype(jnp.bfloat16)
            state_ref[:, lanes] = state

    def at(group):
        return pl.multiple_of(group * NS, NS)

    def pair(index, nothing):
        finish(at(2 * index), hist_refs[1])
        advance(at(2 * index + 1), hist_refs[0])
        finish(at(2 * index + 1), hist_refs[0])
        advance(at(2 * index + 2), hist_refs[1])
        return nothing

    groups = rows // NS
    advance(0, hist_refs[1])
    lax.fori_loop(0, groups // 2 - 1, pair, 0)
    finish(rows - 2 * NS, hist_refs[1])
    advance(rows - NS, hist_refs[0])
    finish(rows - NS, hist_refs[0])


def work_shapes(rows, width):
    return [
        pltpu.VMEM((rows, NS * NS), jnp.bfloat16),
        pltpu.VMEM((NS * NS, width), jnp.bfloat16),
        pltpu.VMEM((NS * NS, width), jnp.bfloat16),
    ]


def own_kernel(
    stream_ref, low_ref, map_ref, cols_ref, bias_ref, rates_ref, gain_ref,
    out_ref, sums_ref, maps_ref, state_ref, total_ref, steps_ref, *work_refs
):
    rows = steps_ref.shape[0]

    @pl.when(pl.program_id(0) == 0)
    def _():
        state_ref[...] = jnp.zeros_like(state_ref)
        total_ref[...] = jnp.zeros_like(total_ref)

    maps = map_ref[...].astype(jnp.float32)
    maps_ref[0] = maps
    logits = jnp.dot(low_ref[...], cols_ref[...], preferred_element_type=jnp.float32)
    steps = softplus(logits + bias_ref[...]).astype(jnp.bfloat16)
    steps_ref[...] = steps
    within = sums_within(steps)
    sums_ref[...] = within.astype(jnp.bfloat16)
    total_ref[...] = total_ref[...] + within[rows - 1 :, :]
    scan_blocks(stream_ref, steps_ref, maps, rates_ref, gain_ref, out_ref, state_ref, work_refs)


def scan_own(stream, lows, cols, bias, rates, gain):
    rows, width = stream.shape[1] // CORES, stream.shape[2]
    map_row = CORES * rows // MAPS

    def fixed(*shape):
        return pl.BlockSpec(shape, lambda b: (0,) * len(shape))

    block = pl.BlockSpec((rows, width), lambda b: (b, 0))
    return pl.pallas_call(
        own_kernel,
        grid=(CORES,),
        in_specs=[
            pl.BlockSpec((1, rows, width), lambda b: (0, b, 0)),
            pl.BlockSpec((rows, RANK), lambda b: (b, 0)),
            pl.BlockSpec((MAPS, rows), lambda b: (map_row, b)),
            fixed(*cols.shape),
            fixed(*bias.shape),
            fixed(*rates.shape),
            fixed(*gain.shape),
        ],
        out_specs=[
            block,
            block,
            pl.BlockSpec((1, 2 * NS, rows), lambda b: (b, 0, 0)),
            fixed(NS, width),
            fixed(1, width),
        ],
        out_shape=[
            jax.ShapeDtypeStruct((CORES * rows, width), jnp.bfloat16),
            jax.ShapeDtypeStruct((CORES * rows, width), jnp.bfloat16),
            jax.ShapeDtypeStruct((CORES, 2 * NS, rows), jnp.float32),
            jax.ShapeDtypeStruct((NS, width), jnp.float32),
            jax.ShapeDtypeStruct((1, width), jnp.float32),
        ],
        scratch_shapes=[pltpu.VMEM((rows, width), jnp.bfloat16)] + work_shapes(rows, width),
        compiler_params=params,
        cost_estimate=pl.CostEstimate(flops=4 * 10**9, bytes_accessed=1 << 21, transcendentals=0),
        name="scan_own",
    )(stream, lows, lows, cols, bias, rates, gain)


def others_kernel(
    place_ref, stream_ref, steps_ref, maps_ref, rates_ref, gain_ref, out_ref, last_ref, *work_refs
):
    @pl.when(lax.rem(pl.program_id(0), CORES) == 0)
    def _():
        last_ref[...] = jnp.zeros_like(last_ref)

    scan_blocks(
        stream_ref, steps_ref, maps_ref[0], rates_ref, gain_ref, out_ref, last_ref.at[0], work_refs
    )


def scan_others(place, stream, steps, maps, rates, gain):
    others = stream.shape[0]
    chips = others + 1
    rows, width = stream.shape[1] // CORES, stream.shape[2]

    def slot(b, s):
        chip = b // CORES
        return lax.rem(s[0] - jnp.where(chip < s[0], chip, chip + 1) + chips, chips) - 1

    def fixed(*shape):
        return pl.BlockSpec(shape, lambda b, s: (0,) * len(shape))

    block = pl.BlockSpec((rows, width), lambda b, s: (b, 0))
    return pl.pallas_call(
        others_kernel,
        grid_spec=pltpu.PrefetchScalarGridSpec(
            num_scalar_prefetch=1,
            grid=(others * CORES,),
            in_specs=[
                pl.BlockSpec((1, rows, width), lambda b, s: (slot(b, s), lax.rem(b, CORES), 0)),
                block,
                pl.BlockSpec((1, 2 * NS, rows), lambda b, s: (b, 0, 0)),
                fixed(*rates.shape),
                fixed(*gain.shape),
            ],
            out_specs=[block, pl.BlockSpec((1, NS, width), lambda b, s: (b // CORES, 0, 0))],
            scratch_shapes=work_shapes(rows, width),
        ),
        out_shape=[
            jax.ShapeDtypeStruct((others * CORES * rows, width), jnp.bfloat16),
            jax.ShapeDtypeStruct((others, NS, width), jnp.float32),
        ],
        compiler_params=params,
        cost_estimate=pl.CostEstimate(flops=4 * 10**9, bytes_accessed=1 << 21, transcendentals=0),
        name="scan_others",
    )(place, stream, steps, maps, rates, gain)


def carried_kernel(
    places_ref, part_own_ref, part_come_ref, sums_own_ref, sums_come_ref,
    maps_own_ref, maps_come_ref, last_own_ref, last_come_ref, rates_ref, carries_ref,
    out_ref, state_ref, wide_ref, begin_ref, spread_ref, sums_ref,
):
    block = pl.program_id(0)
    rows, width = out_ref.shape
    chip = block // CORES
    here = chip == places_ref[0]

    @pl.when(block == 0)
    def _():
        state_ref[...] = jnp.zeros_like(state_ref)

        def compose(row, nothing):
            follow(carries_ref.at[row], rates_ref, state_ref)
            return nothing

        lax.fori_loop(0, places_ref[1], compose, 0)
        for n in range(NS):
            wide_ref[n * NS : (n + 1) * NS, :] = jnp.broadcast_to(
                rates_ref[n : n + 1, :], (NS, width)
            ).astype(jnp.bfloat16)

    @pl.when((block > 0) & (lax.rem(block, CORES) == 0))
    def _():
        before = jnp.where(chip - 1 == places_ref[0], last_own_ref[...], last_come_ref[0])
        state_ref[...] = state_ref[...] + before

    state = state_ref[...]
    for n in range(NS):
        begin_ref[n * NS : (n + 1) * NS, :] = jnp.broadcast_to(
            state[n : n + 1, :], (NS, width)
        ).astype(jnp.bfloat16)
    maps = jnp.where(here, maps_own_ref[0], maps_come_ref[0])
    maps = jnp.concatenate([maps, jnp.zeros((LANES - 2 * NS, rows), jnp.float32)], axis=0).T
    for n in range(NS):
        spread_ref[:, n * LANES : (n + 1) * LANES] = jnp.broadcast_to(
            maps[:, NS + n : NS + n + 1], (rows, LANES)
        ).astype(jnp.bfloat16)
    sums = jnp.where(here, sums_own_ref[...], sums_come_ref[...])
    sums_ref[...] = sums
    last = sums[rows - NS :, :].astype(jnp.float32)[NS - 1 :, :]
    state_ref[...] = jnp.exp2(rates_ref[...] * last) * state
    chunk, several = CORES * LANES, 4

    def some(index, nothing):
        near = pl.ds(pl.multiple_of(index * NS, NS), NS)
        for item in range(width // chunk):
            lanes = slice(item * chunk, (item + 1) * chunk)
            part = jnp.where(here, part_own_ref[near, lanes], part_come_ref[near, lanes])
            total = part.astype(jnp.float32)
            sums = sums_ref[near, lanes]
            for first in range(0, NS, several):
                terms = []
                for n in range(first, first + several):
                    decay = jnp.exp2(sums * wide_ref[n * NS : (n + 1) * NS, lanes])
                    out_of = spread_ref[near, n * LANES : (n + 1) * LANES]
                    out_of = jnp.concatenate([out_of] * (chunk // LANES), axis=1)
                    terms.append(decay * begin_ref[n * NS : (n + 1) * NS, lanes] * out_of)
                four = (terms[0] + terms[1]) + (terms[2] + terms[3])
                total = total + four.astype(jnp.float32)
            out_ref[near, lanes] = total.astype(jnp.bfloat16)
        return nothing

    lax.fori_loop(0, rows // NS, some, 0)


def add_carried(places, parts, sums, maps, lasts, rates, carries):
    blocks_come, _, rows = maps[1].shape
    chips = blocks_come // CORES + 1
    width = rates.shape[1]

    def core(b):
        return lax.rem(b, CORES)

    def order(b, s):
        chip = b // CORES
        return jnp.minimum(
            jnp.where(chip < s[0], b, jnp.maximum(b - CORES, 0)), blocks_come - 1
        )

    def before(b, s):
        chip = jnp.maximum(b // CORES - 1, 0)
        return jnp.minimum(jnp.where(chip < s[0], chip, jnp.maximum(chip - 1, 0)), chips - 2)

    def fixed(*shape):
        return pl.BlockSpec(shape, lambda b, s: (0,) * len(shape))

    own = pl.BlockSpec((rows, width), lambda b, s: (core(b), 0))
    come = pl.BlockSpec((rows, width), lambda b, s: (order(b, s), 0))
    return pl.pallas_call(
        carried_kernel,
        grid_spec=pltpu.PrefetchScalarGridSpec(
            num_scalar_prefetch=1,
            grid=(chips * CORES,),
            in_specs=[
                own,
                come,
                own,
                come,
                pl.BlockSpec((1, 2 * NS, rows), lambda b, s: (core(b), 0, 0)),
                pl.BlockSpec((1, 2 * NS, rows), lambda b, s: (order(b, s), 0, 0)),
                fixed(NS, width),
                pl.BlockSpec((1, NS, width), lambda b, s: (before(b, s), 0, 0)),
                fixed(*rates.shape),
                fixed(*carries.shape),
            ],
            out_specs=pl.BlockSpec((rows, width), lambda b, s: (b, 0)),
            scratch_shapes=[
                pltpu.VMEM((NS, width), jnp.float32),
                pltpu.VMEM((NS * NS, width), jnp.bfloat16),
                pltpu.VMEM((NS * NS, width), jnp.bfloat16),
                pltpu.VMEM((rows, NS * LANES), jnp.bfloat16),
                pltpu.VMEM((rows, width), jnp.bfloat16),
            ],
        ),
        out_shape=jax.ShapeDtypeStruct((chips * CORES * rows, width), jnp.bfloat16),
        compiler_params=params,
        name="add_carried",
    )(places, *parts, *sums, *maps, *lasts, rates, carries)


def local(
    queries, keys, values, doc_lengths, rank_in, bc_weight, rank_out, dt_bias, a_log, skip_gain
):
    devices = lax.axis_size("seq")
    chips = devices // CORES
    targets = lax.axis_size("chan")
    seq_place = lax.axis_index("seq").astype(jnp.int32)
    chan_place = lax.axis_index("chan").astype(jnp.int32)
    chip, core = seq_place // CORES, lax.rem(seq_place, CORES)
    place = jnp.stack([chip, core])
    width = queries.shape[2] // devices
    wide = max(HEAD_SIZE, keys.shape[2] // devices)

    def other(device):
        return device + 1 - 2 * (device % CORES)

    swap = [(device, other(device)) for device in range(devices)]
    near = [(device, device + CORES) for device in range(devices - CORES)]
    far = [(device, other(device + CORES)) for device in range(devices - CORES)]

    def onward(chips_on):
        return [(device, (device + chips_on * CORES) % devices) for device in range(devices)]

    own, theirs = select_heads(keys[0], values[0], chips, wide)
    from_near = lax.ppermute(own, "seq", near)
    from_far = lax.ppermute(theirs, "seq", far)
    swapped = lax.ppermute(theirs, "seq", swap)
    queries_after, _ = lax.optimization_barrier((queries[0], own))
    their_queries = lax.ppermute(queries_after, "seq", swap)
    blocks = (own, swapped, from_near, from_far)

    first = seq_place * width
    logs = lax.dynamic_slice_in_dim(a_log, first, width, 0)
    rates = (-LOG2E * jnp.exp(logs)).T
    cols = lax.dynamic_slice_in_dim(rank_out, first, width, 1)
    bias = lax.dynamic_slice_in_dim(dt_bias, first, width, 0)[None]
    gain = lax.dynamic_slice_in_dim(skip_gain, first, width, 0)[None]

    sent, stayed, part = attend(
        place, doc_lengths, (queries[0], their_queries), blocks, rank_in, bc_weight.T,
        (rates, cols, bias, gain),
    )
    come = [lax.ppermute(sent[step], "seq", onward(step + 1)) for step in range(chips - 1)]
    low_own = low_and_maps(part, lax.ppermute(part, "seq", swap))
    low_come = [lax.ppermute(low_own, "seq", onward(step + 1)) for step in range(chips - 1)]
    got_sent = lax.ppermute(sent, "seq", swap)
    got_stayed = lax.ppermute(stayed, "seq", swap)
    attn_rows = join_heads(sent, stayed, got_sent, got_stayed)

    part_own, sums_own, maps_own, state, total = scan_own(stayed, low_own, cols, bias, rates, gain)
    come, low_come = jnp.stack(come), jnp.stack(low_come)
    steps, sums_come, maps_come, carry = step_sizes(
        place, come, low_come, cols, bias, rates, state, total, targets, attn_rows
    )
    carries = lax.all_to_all(carry, "chan", split_axis=0, concat_axis=0, tiled=True)
    part_come, last_come = scan_others(place, come, steps, maps_come, rates, gain)
    ssm_rows = add_carried(
        jnp.stack([chip, chan_place]), (part_own, part_come), (sums_own, sums_come),
        (maps_own, maps_come), (state, last_come), rates, carries,
    )
    return (attn_rows[None], ssm_rows[None])


def solution(mesh):
    return jax.shard_map(
        local,
        mesh=mesh,
        in_specs=(
            P("chan", "seq", None),
            P("chan", "seq", None),
            P("chan", "seq", None),
            P("chan", None),
            P(),
            P(),
            P(),
            P(),
            P(),
            P(),
        ),
        out_specs=(P("chan", "seq", None), P("chan", None, "seq")),
        check_vma=False,
    )
```

profile of v0, /device:TPU:0, one launch (start us, length us, event | category | flops | bytes accessed | tf_op | source)
XLA Modules:
  0.0 81.2 jit_solution(8053398823887040640)
XLA Ops:
  0.6 0.0 copy-start
  0.6 2.1 %select_heads.1 = (bf16[2,2,128,256]{3,2,1,0:T(8,128)(2,1)}, bf16[2,2,128,256]{3,2,1,0:T(8,128)(2,1)}) custom-call(bf16[128,1024]{1,0:T(8,128)(2,1)} %bitcast.23, bf16[128,1024]{1,0:T(8,128)(2,1)} %bitcast.24), custom_call_target="tpu_custom_call" | custom-call | tf_op jit(solution)/shard_map/select_heads/pallas_call | solution.py:61
  2.7 0.5 collective-permute-start
  3.3 4.5 %collective-permute-start.3 = (bf16[2,2,128,256]{3,2,1,0:T(8,128)(2,1)}, bf16[2,2,128,256]{3,2,1,0:T(8,128)(2,1)S(1)}, u32[]{:S(2)}, u32[]{:S(2)}) collective-permute-start(bf16[2,2,128,256]{3,2,1,0:T(8,128)(2,1)} %get-tuple-element.21), channel_id=1, source_target_pairs={{0,24},{8,16},{1,25},{9,17},{2,26},{10,18},{3,27},{11,19},{4,28},{... | collective-permute-start | bytes 786440 | tf_op jit(solution)/shard_map/ppermute | solution.py:783
  7.8 0.1 collective-permute-start.1
  7.9 2.3 %collective-permute-start.2 = (bf16[2,2,128,256]{3,2,1,0:T(8,128)(2,1)}, bf16[2,2,128,256]{3,2,1,0:T(8,128)(2,1)}, u32[]{:S(2)}, u32[]{:S(2)}) collective-permute-start(bf16[2,2,128,256]{3,2,1,0:T(8,128)(2,1)} %get-tuple-element.19.own_ref), channel_id=1, source_target_pairs={{0,16},{8,24},{1,17},{9,25},{2,18},{10,26},{3,19},{11,27},{4,20},{... | collective-permute-start | bytes 786440 | tf_op jit(solution)/shard_map/ppermute | solution.py:782
  10.2 0.6 pad_add_fusion.place_ref
  10.9 1.3 %dynamic_slice.14 = f32[1024]{0:T(1024)} dynamic-slice(f32[4096]{0:T(1024)} %param.17, s32[]{:T(128)S(6)} %select_n.12), dynamic_slice_sizes={1024} | dynamic-slice | bytes 8196 | tf_op jit(solution)/shard_map/dynamic_slice | solution.py:793
  12.2 1.3 %dynamic_slice.15 = f32[1024]{0:T(1024)} dynamic-slice(f32[4096]{0:T(1024)} %param.19, s32[]{:T(128)S(6)} %select_n.12), dynamic_slice_sizes={1024} | dynamic-slice | bytes 8196 | tf_op jit(solution)/shard_map/dynamic_slice | solution.py:794
  13.4 1.5 %multiply_bitcast_fusion.rest_0_.rates_ref = f32[16,1024]{1,0:T(8,128)} fusion(f32[4096,16]{0,1:T(8,128)} %param.18, s32[]{:T(128)S(6)} %select_n.12), kind=kLoop, calls=%fused_computation | loop fusion | flops 16384 | bytes 131076 | tf_op jit(solution)/shard_map/transpose | solution.py:791
  14.9 0.0 copy-done
  14.9 0.8 %constant_dynamic-slice_fusion.rest_1_.cols_ref = bf16[256,1024]{1,0:T(8,128)(2,1)} fusion(bf16[256,4096]{1,0:T(8,128)(2,1)S(1)} %copy-done, s32[]{:T(128)S(6)} %select_n.12), kind=kLoop, calls=%fused_computation.3 | loop fusion | bytes 1048580 | tf_op jit(solution)/shard_map/dynamic_slice | solution.py:792
  15.8 0.0 collective-permute-done.3.far_ref
  15.8 0.0 copy-start.7
  15.8 0.0 collective-permute-done.1.swap_ref
  15.8 4.0 %collective-permute-done.2.near_ref = bf16[2,2,128,256]{3,2,1,0:T(8,128)(2,1)} collective-permute-done((bf16[2,2,128,256]{3,2,1,0:T(8,128)(2,1)}, bf16[2,2,128,256]{3,2,1,0:T(8,128)(2,1)}, u32[]{:S(2)}, u32[]{:S(2)}) %collective-permute-start.2) | collective-permute-done | bytes 262176 | tf_op jit(solution)/shard_map/ppermute | solution.py:782
  19.7 0.0 collective-permute-done.theirs_ref
  19.7 0.0 copy-start.6
  19.7 0.0 copy-done.7
  19.7 1.0 %copy-done.6 = bf16[128,4096]{1,0:T(8,128)(2,1)} copy-done((bf16[128,4096]{1,0:T(8,128)(2,1)}, bf16[128,4096]{1,0:T(8,128)(2,1)S(1)}, u32[]{:S(2)}) %copy-start.6) | copy-done | bytes 1048600
  20.7 8.1 %attend.1 = (bf16[1,256,1024]{2,1,0:T(8,128)(2,1)}, bf16[1,256,1024]{2,1,0:T(8,128)(2,1)}, f32[288,256]{1,0:T(8,128)}) custom-call(s32[2]{0:T(128)} %pad_add_fusion.place_ref, s32[1,16]{1,0:T(1,128)} %doc_ref.1, bf16[128,4096]{1,0:T(8,128)(2,1)} %bitcast.32, bf16[128,4096]{1,0:T(8,128)(2,1)} %copy-done.6, ...), custom_call_target="tpu_custom_call" | custom-call | flops 5000000000 | bytes 4194304 | tf_op jit(solution)/shard_map/attend/pallas_call | solution.py:235
  28.8 0.1 collective-permute-start.6
  28.9 0.5 collective-permute-start.4
  29.4 0.1 collective-permute-start.5
  29.4 2.5 %collective-permute-start.7 = (bf16[256,1024]{1,0:T(8,128)(2,1)}, bf16[256,1024]{1,0:T(8,128)(2,1)S(1)}, u32[]{:S(2)}, u32[]{:S(2)}) collective-permute-start(bf16[256,1024]{1,0:T(8,128)(2,1)} %bitcast.22), channel_id=1, source_target_pairs={{0,16},{8,24},{16,0},{24,8},{1,17},{9,25},{17,1},{25,9},{2,18},{10... | collective-permute-start | bytes 1572872 | tf_op jit(solution)/shard_map/ppermute | solution.py:800
  31.9 0.0 collective-permute-done.6.theirs_ref
  31.9 0.0 copy-start.5
  31.9 0.7 copy-done.5
  32.6 1.7 %low_and_maps.1.low_ref.map_ref = bf16[288,256]{1,0:T(8,128)(2,1)} custom-call(f32[288,256]{1,0:T(8,128)} %get-tuple-element.24.mine_ref, f32[288,256]{1,0:T(8,128)} %copy-done.5), custom_call_target="tpu_custom_call" | custom-call | flops 1 | bytes 1 | tf_op jit(solution)/shard_map/low_and_maps/pallas_call | solution.py:273
  34.4 1.2 %collective-permute-start.8 = (bf16[288,256]{1,0:T(8,128)(2,1)}, bf16[288,256]{1,0:T(8,128)(2,1)S(1)}, u32[]{:S(2)}, u32[]{:S(2)}) collective-permute-start(bf16[288,256]{1,0:T(8,128)(2,1)} %low_and_maps.1.low_ref.map_ref), channel_id=1, source_target_pairs={{0,16},{8,24},{16,0},{24,8},{1,17},{9,25},{17,1},{25,9},{2,18},{10... | collective-permute-start | bytes 442376 | tf_op jit(solution)/shard_map/ppermute | solution.py:802
  35.6 8.4 %scan_own.1 = (bf16[256,1024]{1,0:T(8,128)(2,1)}, bf16[256,1024]{1,0:T(8,128)(2,1)}, f32[2,32,128]{2,1,0:T(8,128)}, f32[16,1024]{1,0:T(8,128)}, f32[1,1024]{1,0:T(1,128)}) custom-call(bf16[1,256,1024]{2,1,0:T(8,128)(2,1)} %get-tuple-element.23.stayed_ref.stream_ref, bf16[288,256]{1,0:T(8,128)(2,1)} %low_and_maps.1.low_ref.map_ref, ...), custom_call_target="tpu_custom_call" | custom-call | flops 4000000000 | bytes 2097152 | tf_op jit(solution)/shard_map/scan_own/pallas_call | solution.py:552
  44.0 0.0 collective-permute-done.4.got_sent_ref
  44.0 0.0 copy-start.4
  44.0 0.0 collective-permute-done.5.got_stayed_ref
  44.0 0.8 copy-done.4
  44.8 2.2 %join_heads.1.rest_2_ = bf16[128,4096]{1,0:T(8,128)(2,1)} custom-call(bf16[1,256,1024]{2,1,0:T(8,128)(2,1)} %get-tuple-element.22.sent_ref, bf16[1,256,1024]{2,1,0:T(8,128)(2,1)} %get-tuple-element.23.stayed_ref.stream_ref, bf16[1,256,1024]{2,1,0:T(8,128)(2,1)} %copy-done.4, bf16[1,256,1024]{2,1,0:T(8,128)(2,1)} %collective-permute-done.5.got_stayed_ref), custom_call_target="tpu_custom_call" | custom-call | tf_op jit(solution)/shard_map/join_heads/pallas_call | solution.py:90
  47.0 0.8 %collective-permute-done.8 = bf16[288,256]{1,0:T(8,128)(2,1)S(1)} collective-permute-done((bf16[288,256]{1,0:T(8,128)(2,1)}, bf16[288,256]{1,0:T(8,128)(2,1)S(1)}, u32[]{:S(2)}, u32[]{:S(2)}) %collective-permute-start.8) | collective-permute-done | bytes 147488 | tf_op jit(solution)/shard_map/ppermute | solution.py:802
  47.8 0.0 copy-start.2
  47.8 0.0 collective-permute-done.7
  47.8 0.6 copy-done.2
  48.5 0.2 copy-done.3
  48.7 6.6 %step_sizes.1 = (bf16[256,1024]{1,0:T(8,128)(2,1)}, bf16[256,1024]{1,0:T(8,128)(2,1)}, f32[2,32,128]{2,1,0:T(8,128)}, bf16[8,144,128]{2,1,0:T(8,128)(2,1)}) custom-call(s32[2]{0:T(128)} %pad_add_fusion.place_ref, bf16[1,256,1024]{2,1,0:T(8,128)(2,1)} %bitcast.20, bf16[1,288,256]{2,1,0:T(8,128)(2,1)} %bitcast.18, bf16[1,288,256]{2,1,0:T(8,128)(2,1)} %bitcast.19, ...), custom_call_target="tpu_custom_call" | custom-call | tf_op jit(solution)/shard_map/step_sizes/pallas_call | solution.py:398
  55.3 5.8 %all-to-all-start = ((bf16[8,144,128]{2,1,0:T(8,128)(2,1)}), bf16[8,144,128]{2,1,0:T(8,128)(2,1)S(1)}, u32[]{:S(2)}, u32[]{:S(2)}) async-start(bf16[8,144,128]{2,1,0:T(8,128)(2,1)} %get-tuple-element.35), calls=%async_computation | async-start | bytes 589824 | tf_op jit(solution)/shard_map/all_to_all | solution.py:812
  61.1 0.6 pad_add_fusion.1.places_ref
  61.7 8.0 %scan_others.1 = (bf16[256,1024]{1,0:T(8,128)(2,1)}, f32[1,16,1024]{2,1,0:T(8,128)}) custom-call(s32[2]{0:T(128)} %pad_add_fusion.place_ref, bf16[1,256,1024]{2,1,0:T(8,128)(2,1)} %bitcast.21, bf16[256,1024]{1,0:T(8,128)(2,1)} %get-tuple-element.28.steps_ref, f32[2,32,128]{2,1,0:T(8,128)} %get-tuple-element.29.maps_ref.maps_come_ref, ...), custom_call_target="tpu_custom_call" | custom-call | flops 4000000000 | bytes 2097152 | tf_op jit(solution)/shard_map/scan_others/pallas_call | solution.py:610
  69.6 1.1 %all-to-all-done.carries_ref = bf16[8,144,128]{2,1,0:T(8,128)(2,1)S(1)} async-done(((bf16[8,144,128]{2,1,0:T(8,128)(2,1)}), bf16[8,144,128]{2,1,0:T(8,128)(2,1)S(1)}, u32[]{:S(2)}, u32[]{:S(2)}) %all-to-all-start) | async-done | bytes 294944 | tf_op jit(solution)/shard_map/all_to_all | solution.py:812
  70.7 0.7 copy-done.1
  71.4 9.7 %add_carried.1 = bf16[512,1024]{1,0:T(8,128)(2,1)} custom-call(s32[2]{0:T(128)} %pad_add_fusion.1.places_ref, bf16[256,1024]{1,0:T(8,128)(2,1)} %get-tuple-element.25.part_own_ref, bf16[256,1024]{1,0:T(8,128)(2,1)} %get-tuple-element.30.part_come_ref, bf16[256,1024]{1,0:T(8,128)(2,1)} %get-tuple-element.31.sums_own_ref, ...), custom_call_target="tpu_custom_call" | custom-call | tf_op jit(solution)/shard_map/add_carried/pallas_call | solution.py:726
  (2 shorter events, 0.0 us)
Async XLA Ops:
  0.6 14.3 %copy-start = (bf16[256,4096]{1,0:T(8,128)(2,1)S(1)}, bf16[256,4096]{1,0:T(8,128)(2,1)}, u32[]{:S(2)}) copy-start(bf16[256,4096]{1,0:T(8,128)(2,1)} %param.16) | copy-start | bytes 6291460
  2.7 17.0 %collective-permute-start = (bf16[128,4096]{1,0:T(8,128)(2,1)}, bf16[128,4096]{1,0:T(8,128)(2,1)S(1)}, u32[]{:S(2)}, u32[]{:S(2)}) collective-permute-start(bf16[128,4096]{1,0:T(8,128)(2,1)} %bitcast.31), channel_id=1, source_target_pairs={{0,8},{8,0},{16,24},{24,16},{1,9},{9,1},{17,25},{25,17},{2,10},{10... | collective-permute-start | bytes 3145736 | tf_op jit(solution)/shard_map/ppermute | solution.py:786
  3.3 12.5 %collective-permute-start.3 = (bf16[2,2,128,256]{3,2,1,0:T(8,128)(2,1)}, bf16[2,2,128,256]{3,2,1,0:T(8,128)(2,1)S(1)}, u32[]{:S(2)}, u32[]{:S(2)}) collective-permute-start(bf16[2,2,128,256]{3,2,1,0:T(8,128)(2,1)} %get-tuple-element.21), channel_id=1, source_target_pairs={{0,24},{8,16},{1,25},{9,17},{2,26},{10,18},{3,27},{11,19},{4,28},{... | collective-permute-start | bytes 786440 | tf_op jit(solution)/shard_map/ppermute | solution.py:783
  7.8 8.0 %collective-permute-start.1 = (bf16[2,2,128,256]{3,2,1,0:T(8,128)(2,1)}, bf16[2,2,128,256]{3,2,1,0:T(8,128)(2,1)}, u32[]{:S(2)}, u32[]{:S(2)}) collective-permute-start(bf16[2,2,128,256]{3,2,1,0:T(8,128)(2,1)} %get-tuple-element.21), channel_id=1, source_target_pairs={{0,8},{8,0},{16,24},{24,16},{1,9},{9,1},{17,25},{25,17},{2,10},{10... | collective-permute-start | bytes 786440 | tf_op jit(solution)/shard_map/ppermute | solution.py:784
  7.9 11.8 %collective-permute-start.2 = (bf16[2,2,128,256]{3,2,1,0:T(8,128)(2,1)}, bf16[2,2,128,256]{3,2,1,0:T(8,128)(2,1)}, u32[]{:S(2)}, u32[]{:S(2)}) collective-permute-start(bf16[2,2,128,256]{3,2,1,0:T(8,128)(2,1)} %get-tuple-element.19.own_ref), channel_id=1, source_target_pairs={{0,16},{8,24},{1,17},{9,25},{2,18},{10,26},{3,19},{11,27},{4,20},{... | collective-permute-start | bytes 786440 | tf_op jit(solution)/shard_map/ppermute | solution.py:782
  15.8 4.0 %copy-start.7 = (bf16[2,2,128,256]{3,2,1,0:T(8,128)(2,1)}, bf16[2,2,128,256]{3,2,1,0:T(8,128)(2,1)S(1)}, u32[]{:S(2)}) copy-start(bf16[2,2,128,256]{3,2,1,0:T(8,128)(2,1)S(1)} %collective-permute-done.3.far_ref) | copy-start | bytes 786436
  19.7 1.0 %copy-start.6 = (bf16[128,4096]{1,0:T(8,128)(2,1)}, bf16[128,4096]{1,0:T(8,128)(2,1)S(1)}, u32[]{:S(2)}) copy-start(bf16[128,4096]{1,0:T(8,128)(2,1)S(1)} %collective-permute-done.theirs_ref) | copy-start | bytes 3145732
  28.8 3.1 %collective-permute-start.6 = (f32[288,256]{1,0:T(8,128)}, f32[288,256]{1,0:T(8,128)S(1)}, u32[]{:S(2)}, u32[]{:S(2)}) collective-permute-start(f32[288,256]{1,0:T(8,128)} %get-tuple-element.24.mine_ref), channel_id=1, source_target_pairs={{0,8},{8,0},{16,24},{24,16},{1,9},{9,1},{17,25},{25,17},{2,10},{10... | collective-permute-start | bytes 884744 | tf_op jit(solution)/shard_map/ppermute | solution.py:801
  28.9 15.1 %collective-permute-start.4 = (bf16[1,256,1024]{2,1,0:T(8,128)(2,1)}, bf16[1,256,1024]{2,1,0:T(8,128)(2,1)S(1)}, u32[]{:S(2)}, u32[]{:S(2)}) collective-permute-start(bf16[1,256,1024]{2,1,0:T(8,128)(2,1)} %get-tuple-element.22.sent_ref), channel_id=1, source_target_pairs={{0,8},{8,0},{16,24},{24,16},{1,9},{9,1},{17,25},{25,17},{2,10},{10... | collective-permute-start | bytes 1572872 | tf_op jit(solution)/shard_map/ppermute | solution.py:803
  29.4 14.7 %collective-permute-start.5 = (bf16[1,256,1024]{2,1,0:T(8,128)(2,1)}, bf16[1,256,1024]{2,1,0:T(8,128)(2,1)}, u32[]{:S(2)}, u32[]{:S(2)}) collective-permute-start(bf16[1,256,1024]{2,1,0:T(8,128)(2,1)} %get-tuple-element.23.stayed_ref.stream_ref), channel_id=1, source_target_pairs={{0,8},{8,0},{16,24},{24,16},{1,9},{9,1},{17,25},{25,17},{2,10},{10... | collective-permute-start | bytes 1572872 | tf_op jit(solution)/shard_map/ppermute | solution.py:804
  29.4 18.4 %collective-permute-start.7 = (bf16[256,1024]{1,0:T(8,128)(2,1)}, bf16[256,1024]{1,0:T(8,128)(2,1)S(1)}, u32[]{:S(2)}, u32[]{:S(2)}) collective-permute-start(bf16[256,1024]{1,0:T(8,128)(2,1)} %bitcast.22), channel_id=1, source_target_pairs={{0,16},{8,24},{16,0},{24,8},{1,17},{9,25},{17,1},{25,9},{2,18},{10... | collective-permute-start | bytes 1572872 | tf_op jit(solution)/shard_map/ppermute | solution.py:800
  31.9 0.7 copy-start.5
  34.4 13.4 %collective-permute-start.8 = (bf16[288,256]{1,0:T(8,128)(2,1)}, bf16[288,256]{1,0:T(8,128)(2,1)S(1)}, u32[]{:S(2)}, u32[]{:S(2)}) collective-permute-start(bf16[288,256]{1,0:T(8,128)(2,1)} %low_and_maps.1.low_ref.map_ref), channel_id=1, source_target_pairs={{0,16},{8,24},{16,0},{24,8},{1,17},{9,25},{17,1},{25,9},{2,18},{10... | collective-permute-start | bytes 442376 | tf_op jit(solution)/shard_map/ppermute | solution.py:802
  44.0 0.8 copy-start.4
  47.8 0.7 copy-start.2
  47.8 0.8 %copy-start.3 = (bf16[256,1024]{1,0:T(8,128)(2,1)}, bf16[256,1024]{1,0:T(8,128)(2,1)S(1)}, u32[]{:S(2)}) copy-start(bf16[256,1024]{1,0:T(8,128)(2,1)S(1)} %collective-permute-done.7) | copy-start | bytes 1572868
  55.3 15.5 %all-to-all-start = ((bf16[8,144,128]{2,1,0:T(8,128)(2,1)}), bf16[8,144,128]{2,1,0:T(8,128)(2,1)S(1)}, u32[]{:S(2)}, u32[]{:S(2)}) async-start(bf16[8,144,128]{2,1,0:T(8,128)(2,1)} %get-tuple-element.35), calls=%async_computation | async-start | bytes 589824 | tf_op jit(solution)/shard_map/all_to_all | solution.py:812
  70.7 0.7 copy-start.1
where the time goes:
time: 81.8 us; the launch traced here: 81.2 us
  Pallas kernels  46.8 us (57%)
  starting transfers between devices  17.6 us (22%)
  local copies, waits for them, and re-layouts  7.41 us (9%)
  waiting for transfers between devices  5.86 us (7%)
  other arithmetic  2.73 us (3%)
    pallas_call x1, Pallas kernels, add_carried(): pl.pallas_call(carried_kernel, grid_spec=pltpu.PrefetchScalarGridSpec(num...  9.75 us
    pallas_call x1, Pallas kernels, scan_own(): pl.pallas_call(own_kernel, grid=(CORES,), in_specs=[pl.BlockSpec((1, rows...  8.42 us
    pallas_call x1, Pallas kernels, attend(): pl.pallas_call(functools.partial(attend_kernel, chips=chips), grid_spec=p...  8.07 us
    pallas_call x1, Pallas kernels, scan_others(): pl.pallas_call(others_kernel, grid_spec=pltpu.PrefetchScalarGridSpec(num_...  7.97 us
    pallas_call x1, Pallas kernels, step_sizes(): pl.pallas_call(step_kernel, grid_spec=pltpu.PrefetchScalarGridSpec(num_sc...  6.6 us
    all_to_all x1, starting transfers between devices, local(): lax.all_to_all(carry, 'chan', split_axis=0, concat_axis=0, tiled=True)  5.82 us
    ppermute x1, starting transfers between devices, local(): from_far = lax.ppermute(theirs, 'seq', far)  4.54 us
    unnamed x16, local copies, waits for them, and re-layouts  4.01 us
  transfers between devices with their start and end apart: 10, of which 3 were waited for; matrix products, arithmetic and copies ran while one was open for 8% of the time, Pallas kernels for 25%

commit v1 on v0

--- a/solution.py
+++ b/solution.py
@@ -298,143 +298,6 @@
     return jnp.dot(upto, steps, preferred_element_type=jnp.float32)
 
 
-def step_kernel(
-    place_ref, stream_ref, low_ref, map_ref, cols_ref, bias_ref, rates_ref, *rest
-):
-    own_state_ref, own_total_ref = rest[:2]
-    steps_ref, sums_ref, maps_ref, carry_ref, state_ref, total_ref, wide_ref, turn_ref = rest[3:]
-    block = pl.program_id(0)
-    rows, width = stream_ref.shape[1:]
-
-    @pl.when(block == 0)
-    def _():
-        state_ref[...] = jnp.zeros_like(state_ref)
-        total_ref[...] = jnp.zeros_like(total_ref)
-        for n in range(NS):
-            wide_ref[n * SUBLANES : (n + 1) * SUBLANES, :] = jnp.broadcast_to(
-                rates_ref[n : n + 1, :], (SUBLANES, width)
-            )
-
-    @pl.when(block == place_ref[0] * CORES)
-    def _():
-        add_states(rates_ref, state_ref, total_ref, own_state_ref[...], own_total_ref[...])
-
-    maps = map_ref[0].astype(jnp.float32)
-    maps_ref[0] = maps
-    logits = jnp.dot(low_ref[0], cols_ref[...], preferred_element_type=jnp.float32)
-    steps = softplus(logits + bias_ref[...]).astype(jnp.bfloat16)
-    steps_ref[...] = steps
-    push = steps * stream_ref[0]
-    within = sums_within(steps)
-    sums_ref[...] = within.astype(jnp.bfloat16)
-    whole = within[rows - 1 :, :]
-    left = whole - within
-    some, chunk, several = rows // 2, CORES * LANES, 4
-    state_row = lax.broadcasted_iota(jnp.int32, (NS, some), 0)
-    for first in range(0, rows, some):
-        span = slice(first, first + some)
-        chosen = [
-            jnp.concatenate(
-                [
-                    jnp.where(state_row == m, maps[:NS, span], 0.0).astype(jnp.bfloat16)
-                    for m in range(n, n + several)
-                ],
-                axis=1,
-            )
-            for n in range(0, NS, several)
-        ]
-        for item in range(width // chunk):
-            lanes = slice(item * chunk, (item + 1) * chunk)
-            left_here = left[span, lanes].reshape(some // SUBLANES, SUBLANES, chunk)
-            push_here = push[span, lanes]
-            added = state_ref[:, lanes]
-            if first == 0:
-                added = jnp.exp2(rates_ref[:, lanes] * whole[:, lanes]) * added
-            for n in range(0, NS, several):
-                pushed = []
-                for m in range(n, n + several):
-                    rate = wide_ref[m * SUBLANES : (m + 1) * SUBLANES, lanes]
-                    decay = jnp.exp2(left_here * rate[None]).reshape(some, chunk)
-                    pushed.append(decay.astype(jnp.bfloat16) * push_here)
-                added = added + jnp.dot(
-                    chosen[n // several],
-                    jnp.concatenate(pushed, axis=0),
-                    preferred_element_type=jnp.float32,
-                )
-            state_ref[:, lanes] = added
-    total_ref[...] = total_ref[...] + whole
-
-    count = pl.num_programs(0)
-
-    @pl.when(block == count - 1)
-    def _():
-        @pl.when(place_ref[0] * CORES == count)
-        def _():
-            add_states(rates_ref, state_ref, total_ref, own_state_ref[...], own_total_ref[...])
-
-        write_carry(carry_ref.at[0], state_ref[...], total_ref[...], turn_ref)
-        for target in range(1, carry_ref.shape[0]):
-            carry_ref[target] = carry_ref[0]
-
-
-def step_sizes(place, stream, lows, cols, bias, rates, state, total, targets, after):
-    others = stream.shape[0]
-    chips = others + 1
-    rows, width = stream.shape[1] // CORES, stream.shape[2]
-    map_row = CORES * rows // MAPS
-    blocks = others * CORES
-    carry = (targets, (width // LANES + 1) * NS, LANES)
-
-    def slot(b, s):
-        chip = b // CORES
-        return lax.rem(s[0] - jnp.where(chip < s[0], chip, chip + 1) + chips, chips) - 1
-
-    def core(b):
-        return lax.rem(b, CORES)
-
-    def fixed(*shape):
-        return pl.BlockSpec(shape, lambda b, s: (0,) * len(shape))
-
-    return pl.pallas_call(
-        step_kernel,
-        grid_spec=pltpu.PrefetchScalarGridSpec(
-            num_scalar_prefetch=1,
-            grid=(blocks,),
-            in_specs=[
-                pl.BlockSpec((1, rows, width), lambda b, s: (slot(b, s), core(b), 0)),
-                pl.BlockSpec((1, rows, RANK), lambda b, s: (slot(b, s), core(b), 0)),
-                pl.BlockSpec((1, MAPS, rows), lambda b, s: (slot(b, s), map_row, core(b))),
-                fixed(*cols.shape),
-                fixed(*bias.shape),
-                fixed(*rates.shape),
-                fixed(*state.shape),
-                fixed(*total.shape),
-                pl.BlockSpec(memory_space=pl.ANY),
-            ],
-            out_specs=[
-                pl.BlockSpec((rows, width), lambda b, s: (b, 0)),
-                pl.BlockSpec((rows, width), lambda b, s: (b, 0)),
-                pl.BlockSpec((1, 2 * NS, rows), lambda b, s: (b, 0, 0)),
-                fixed(*carry),
-            ],
-            scratch_shapes=[
-                pltpu.VMEM((NS, width), jnp.float32),
-                pltpu.VMEM((1, width), jnp.float32),
-                pltpu.VMEM((NS * SUBLANES, width), jnp.float32),
-                pltpu.VMEM((SUBLANES, LANES), jnp.float32),
-            ],
-        ),
-        out_shape=[
-            jax.ShapeDtypeStruct((blocks * rows, width), jnp.bfloat16),
-            jax.ShapeDtypeStruct((blocks * rows, width), jnp.bfloat16),
-            jax.ShapeDtypeStruct((blocks, 2 * NS, rows), jnp.float32),
-            jax.ShapeDtypeStruct(carry, jnp.bfloat16),
-        ],
-        compiler_params=params,
-        name="step_sizes",
-    )(place, stream, lows, lows, cols, bias, rates, state, total, after)
-
-
 def write_carry(out_ref, state, total, turn_ref):
     tile = state.shape[1] // LANES
     turn_ref[...] = jnp.zeros_like(turn_ref)
@@ -519,128 +382,223 @@
     ]
 
 
-def own_kernel(
-    stream_ref, low_ref, map_ref, cols_ref, bias_ref, rates_ref, gain_ref,
-    out_ref, sums_ref, maps_ref, state_ref, total_ref, steps_ref, *work_refs
+def tokens_kernel(
+    place_ref, stream_ref, low_ref, map_ref, cols_ref, bias_ref, rates_ref, gain_ref, *rest, carried
 ):
+    if carried:
+        own_last_ref, own_total_ref, _, *rest = rest
+    out_ref, sums_ref, maps_ref, last_ref, total_ref, *rest = rest
+    if carried:
+        carry_ref, *rest = rest
+    steps_ref, run_state_ref, run_total_ref, turn_ref, *work_refs = rest
+    block = pl.program_id(0)
     rows = steps_ref.shape[0]
-
-    @pl.when(pl.program_id(0) == 0)
-    def _():
-        state_ref[...] = jnp.zeros_like(state_ref)
+    first_core = lax.rem(block, CORES) == 0
+
+    @pl.when(first_core)
+    def _():
+        last_ref[...] = jnp.zeros_like(last_ref)
         total_ref[...] = jnp.zeros_like(total_ref)
 
-    maps = map_ref[...].astype(jnp.float32)
+    def place_own():
+        add_states(rates_ref, run_state_ref, run_total_ref, own_last_ref[0], own_total_ref[0])
+
+    if carried:
+
+        @pl.when(block == 0)
+        def _():
+            run_state_ref[...] = jnp.zeros_like(run_state_ref)
+            run_total_ref[...] = jnp.zeros_like(run_total_ref)
+
+        pl.when(block == place_ref[0] * CORES)(place_own)
+
+    maps = map_ref[0].astype(jnp.float32)
     maps_ref[0] = maps
-    logits = jnp.dot(low_ref[...], cols_ref[...], preferred_element_type=jnp.float32)
+    logits = jnp.dot(low_ref[0], cols_ref[...], preferred_element_type=jnp.float32)
     steps = softplus(logits + bias_ref[...]).astype(jnp.bfloat16)
     steps_ref[...] = steps
     within = sums_within(steps)
     sums_ref[...] = within.astype(jnp.bfloat16)
-    total_ref[...] = total_ref[...] + within[rows - 1 :, :]
-    scan_blocks(stream_ref, steps_ref, maps, rates_ref, gain_ref, out_ref, state_ref, work_refs)
-
-
-def scan_own(stream, lows, cols, bias, rates, gain):
+    total_ref[0] = total_ref[0] + within[rows - 1 :, :]
+    scan_blocks(
+        stream_ref, steps_ref, maps, rates_ref, gain_ref, out_ref, last_ref.at[0], work_refs
+    )
+    if carried:
+        count = pl.num_programs(0)
+
+        @pl.when(jnp.logical_not(first_core))
+        def _():
+            add_states(rates_ref, run_state_ref, run_total_ref, last_ref[0], total_ref[0])
+
+        @pl.when(block == count - 1)
+        def _():
+            pl.when(place_ref[0] * CORES == count)(place_own)
+            write_carry(carry_ref.at[0], run_state_ref[...], run_total_ref[...], turn_ref)
+            for target in range(1, carry_ref.shape[0]):
+                carry_ref[target] = carry_ref[0]
+
+
+def scan_tokens(place, stream, lows, cols, bias, rates, gain, own, targets, after):
+    count = stream.shape[0]
+    chips = count + 1
     rows, width = stream.shape[1] // CORES, stream.shape[2]
     map_row = CORES * rows // MAPS
+    blocks = count * CORES
+    carried = own is not None
+    carry = (targets, (width // LANES + 1) * NS, LANES)
+
+    def slot(b, s):
+        chip = b // CORES
+        if not carried:
+            return chip
+        return lax.rem(s[0] - jnp.where(chip < s[0], chip, chip + 1) + chips, chips) - 1
+
+    def core(b):
+        return lax.rem(b, CORES)
 
     def fixed(*shape):
-        return pl.BlockSpec(shape, lambda b: (0,) * len(shape))
-
-    block = pl.BlockSpec((rows, width), lambda b: (b, 0))
+        return pl.BlockSpec(shape, lambda b, s: (0,) * len(shape))
+
+    block = pl.BlockSpec((rows, width), lambda b, s: (b, 0))
+    in_specs = [
+        pl.BlockSpec((1, rows, width), lambda b, s: (slot(b, s), core(b), 0)),
+        pl.BlockSpec((1, rows, RANK), lambda b, s: (slot(b, s), core(b), 0)),
+        pl.BlockSpec((1, MAPS, rows), lambda b, s: (slot(b, s), map_row, core(b))),
+        fixed(*cols.shape),
+        fixed(*bias.shape),
+        fixed(*rates.shape),
+        fixed(*gain.shape),
+    ]
+    out_specs = [
+        block,
+        block,
+        pl.BlockSpec((1, 2 * NS, rows), lambda b, s: (b, 0, 0)),
+        pl.BlockSpec((1, NS, width), lambda b, s: (b // CORES, 0, 0)),
+        pl.BlockSpec((1, 1, width), lambda b, s: (b // CORES, 0, 0)),
+    ]
+    out_shape = [
+        jax.ShapeDtypeStruct((blocks * rows, width), jnp.bfloat16),
+        jax.ShapeDtypeStruct((blocks * rows, width), jnp.bfloat16),
+        jax.ShapeDtypeStruct((blocks, 2 * NS, rows), jnp.float32),
+        jax.ShapeDtypeStruct((count, NS, width), jnp.float32),
+        jax.ShapeDtypeStruct((count, 1, width), jnp.float32),
+    ]
+    more = []
+    if carried:
+        more = [*own, after]
+        in_specs += [fixed(1, NS, width), fixed(1, 1, width), pl.BlockSpec(memory_space=pl.ANY)]
+        out_specs.append(fixed(*carry))
+        out_shape.append(jax.ShapeDtypeStruct(carry, jnp.bfloat16))
     return pl.pallas_call(
-        own_kernel,
-        grid=(CORES,),
-        in_specs=[
-            pl.BlockSpec((1, rows, width), lambda b: (0, b, 0)),
-            pl.BlockSpec((rows, RANK), lambda b: (b, 0)),
-            pl.BlockSpec((MAPS, rows), lambda b: (map_row, b)),
-            fixed(*cols.shape),
-            fixed(*bias.shape),
-            fixed(*rates.shape),
-            fixed(*gain.shape),
-        ],
-        out_specs=[
-            block,
-            block,
-            pl.BlockSpec((1, 2 * NS, rows), lambda b: (b, 0, 0)),
-            fixed(NS, width),
-            fixed(1, width),
-        ],
-        out_shape=[
-            jax.ShapeDtypeStruct((CORES * rows, width), jnp.bfloat16),
-            jax.ShapeDtypeStruct((CORES * rows, width), jnp.bfloat16),
-            jax.ShapeDtypeStruct((CORES, 2 * NS, rows), jnp.float32),
-            jax.ShapeDtypeStruct((NS, width), jnp.float32),
-            jax.ShapeDtypeStruct((1, width), jnp.float32),
-        ],
-        scratch_shapes=[pltpu.VMEM((rows, width), jnp.bfloat16)] + work_shapes(rows, width),
+        functools.partial(tokens_kernel, carried=carried),
+        grid_spec=pltpu.PrefetchScalarGridSpec(
+            num_scalar_prefetch=1,
+            grid=(blocks,),
+            in_specs=in_specs,
+            out_specs=out_specs,
+            scratch_shapes=[
+                pltpu.VMEM((rows, width), jnp.bfloat16),
+                pltpu.VMEM((NS, width), jnp.float32),
+                pltpu.VMEM((1, width), jnp.float32),
+                pltpu.VMEM((SUBLANES, LANES), jnp.float32),
+            ]
+            + work_shapes(rows, width),
+        ),
+        out_shape=out_shape,
         compiler_params=params,
         cost_estimate=pl.CostEstimate(flops=4 * 10**9, bytes_accessed=1 << 21, transcendentals=0),
-        name="scan_own",
-    )(stream, lows, lows, cols, bias, rates, gain)
-
-
-def others_kernel(
-    place_ref, stream_ref, steps_ref, maps_ref, rates_ref, gain_ref, out_ref, last_ref, *work_refs
-):
-    @pl.when(lax.rem(pl.program_id(0), CORES) == 0)
-    def _():
-        last_ref[...] = jnp.zeros_like(last_ref)
-
-    scan_blocks(
-        stream_ref, steps_ref, maps_ref[0], rates_ref, gain_ref, out_ref, last_ref.at[0], work_refs
-    )
-
-
-def scan_others(place, stream, steps, maps, rates, gain):
-    others = stream.shape[0]
-    chips = others + 1
-    rows, width = stream.shape[1] // CORES, stream.shape[2]
-
-    def slot(b, s):
-        chip = b // CORES
-        return lax.rem(s[0] - jnp.where(chip < s[0], chip, chip + 1) + chips, chips) - 1
-
-    def fixed(*shape):
-        return pl.BlockSpec(shape, lambda b, s: (0,) * len(shape))
-
-    block = pl.BlockSpec((rows, width), lambda b, s: (b, 0))
+        name="scan_tokens",
+    )(place, stream, lows, lows, cols, bias, rates, gain, *more)
+
+
+def write_rates(wide_ref, rates_ref):
+    width = rates_ref.shape[1]
+    for n in range(NS):
+        wide_ref[n * NS : (n + 1) * NS, :] = jnp.broadcast_to(
+            rates_ref[n : n + 1, :], (NS, width)
+        ).astype(jnp.bfloat16)
+
+
+def write_spread(spread_ref, maps):
+    rows = maps.shape[1]
+    maps = jnp.concatenate([maps, jnp.zeros((LANES - 2 * NS, rows), jnp.float32)], axis=0).T
+    for n in range(NS):
+        spread_ref[:, n * LANES : (n + 1) * LANES] = jnp.broadcast_to(
+            maps[:, NS + n : NS + n + 1], (rows, LANES)
+        ).astype(jnp.bfloat16)
+
+
+def factor(sums, wide_ref, spread_ref, near, n, lanes):
+    out_of = spread_ref[near, n * LANES : (n + 1) * LANES]
+    copies = (lanes.stop - lanes.start) // LANES
+    decay = jnp.exp2(sums * wide_ref[n * NS : (n + 1) * NS, lanes])
+    return decay * jnp.concatenate([out_of] * copies, axis=1)
+
+
+def factors_kernel(sums_ref, maps_ref, rates_ref, out_ref, wide_ref, spread_ref):
+    rows, width = sums_ref.shape
+    step = pl.program_id(0)
+    parts = spread_ref.shape[0] // rows
+
+    @pl.when(step == 0)
+    def _():
+        write_rates(wide_ref, rates_ref)
+
+    @pl.when(lax.rem(step, parts) == 0)
+    def _():
+        write_spread(spread_ref, maps_ref[0])
+
+    chunk = CORES * LANES
+
+    def some(index, nothing):
+        start = pl.multiple_of(index * NS, NS)
+        near = pl.ds(pl.multiple_of(lax.rem(step, parts) * rows + start, NS), NS)
+        for item in range(width // chunk):
+            lanes = slice(item * chunk, (item + 1) * chunk)
+            sums = sums_ref[pl.ds(start, NS), lanes]
+            for n in range(NS):
+                to = pl.ds(pl.multiple_of(start * NS + n * NS, NS), NS)
+                out_ref[to, lanes] = factor(sums, wide_ref, spread_ref, near, n, lanes)
+        return nothing
+
+    lax.fori_loop(0, rows // NS, some, 0)
+
+
+def make_factors(sums, maps, rates):
+    rows, width = sums.shape[0] // maps.shape[0], sums.shape[1]
+    parts = 2
+    some = rows // parts
     return pl.pallas_call(
-        others_kernel,
-        grid_spec=pltpu.PrefetchScalarGridSpec(
-            num_scalar_prefetch=1,
-            grid=(others * CORES,),
-            in_specs=[
-                pl.BlockSpec((1, rows, width), lambda b, s: (slot(b, s), lax.rem(b, CORES), 0)),
-                block,
-                pl.BlockSpec((1, 2 * NS, rows), lambda b, s: (b, 0, 0)),
-                fixed(*rates.shape),
-                fixed(*gain.shape),
-            ],
-            out_specs=[block, pl.BlockSpec((1, NS, width), lambda b, s: (b // CORES, 0, 0))],
-            scratch_shapes=work_shapes(rows, width),
-        ),
-        out_shape=[
-            jax.ShapeDtypeStruct((others * CORES * rows, width), jnp.bfloat16),
-            jax.ShapeDtypeStruct((others, NS, width), jnp.float32),
+        factors_kernel,
+        grid=(maps.shape[0] * parts,),
+        in_specs=[
+            pl.BlockSpec((some, width), lambda b: (b, 0)),
+            pl.BlockSpec((1, 2 * NS, rows), lambda b: (b // parts, 0, 0)),
+            pl.BlockSpec((NS, width), lambda b: (0, 0)),
+        ],
+        out_specs=pl.BlockSpec((some * NS, width), lambda b: (b, 0)),
+        out_shape=jax.ShapeDtypeStruct((sums.shape[0] * NS, width), jnp.bfloat16),
+        scratch_shapes=[
+            pltpu.VMEM((NS * NS, width), jnp.bfloat16),
+            pltpu.VMEM((rows, NS * LANES), jnp.bfloat16),
         ],
         compiler_params=params,
-        cost_estimate=pl.CostEstimate(flops=4 * 10**9, bytes_accessed=1 << 21, transcendentals=0),
-        name="scan_others",
-    )(place, stream, steps, maps, rates, gain)
+        cost_estimate=pl.CostEstimate(flops=3 * 10**9, bytes_accessed=1 << 23, transcendentals=0),
+        name="make_factors",
+    )(sums, maps, rates)
 
 
 def carried_kernel(
-    places_ref, part_own_ref, part_come_ref, sums_own_ref, sums_come_ref,
-    maps_own_ref, maps_come_ref, last_own_ref, last_come_ref, rates_ref, carries_ref,
-    out_ref, state_ref, wide_ref, begin_ref, spread_ref, sums_ref,
+    places_ref, part_own_ref, part_come_ref, factors_ref, sums_own_ref, sums_come_ref, maps_ref,
+    last_own_ref, total_own_ref, last_come_ref, total_come_ref, rates_ref, carries_ref,
+    out_ref, state_ref, starts_ref, total_ref, wide_ref, begin_ref, spread_ref,
 ):
     block = pl.program_id(0)
     rows, width = out_ref.shape
-    chip = block // CORES
-    here = chip == places_ref[0]
+    others = last_come_ref.shape[0]
+    chip = places_ref[0]
+    first_core = lax.rem(block, CORES) == 0
+    own = block >= others * CORES
 
     @pl.when(block == 0)
     def _():
@@ -651,108 +609,143 @@
             return nothing
 
         lax.fori_loop(0, places_ref[1], compose, 0)
-        for n in range(NS):
-            wide_ref[n * NS : (n + 1) * NS, :] = jnp.broadcast_to(
-                rates_ref[n : n + 1, :], (NS, width)
-            ).astype(jnp.bfloat16)
-
-    @pl.when((block > 0) & (lax.rem(block, CORES) == 0))
-    def _():
-        before = jnp.where(chip - 1 == places_ref[0], last_own_ref[...], last_come_ref[0])
-        state_ref[...] = state_ref[...] + before
+        write_rates(wide_ref, rates_ref)
+
+        def place_own():
+            starts_ref[others] = state_ref[...]
+            add_states(rates_ref, state_ref, total_ref, last_own_ref[0], total_own_ref[0])
+
+        total_ref[...] = jnp.zeros_like(total_ref)
+        for other in range(others):
+            pl.when(chip == other)(place_own)
+            starts_ref[other] = state_ref[...]
+            add_states(
+                rates_ref, state_ref, total_ref, last_come_ref[other], total_come_ref[other]
+            )
+        pl.when(chip == others)(place_own)
+
+    @pl.when(first_core)
+    def _():
+        state_ref[...] = starts_ref[block // CORES]
 
     state = state_ref[...]
     for n in range(NS):
         begin_ref[n * NS : (n + 1) * NS, :] = jnp.broadcast_to(
             state[n : n + 1, :], (NS, width)
         ).astype(jnp.bfloat16)
-    maps = jnp.where(here, maps_own_ref[0], maps_come_ref[0])
-    maps = jnp.concatenate([maps, jnp.zeros((LANES - 2 * NS, rows), jnp.float32)], axis=0).T
-    for n in range(NS):
-        spread_ref[:, n * LANES : (n + 1) * LANES] = jnp.broadcast_to(
-            maps[:, NS + n : NS + n + 1], (rows, LANES)
-        ).astype(jnp.bfloat16)
-    sums = jnp.where(here, sums_own_ref[...], sums_come_ref[...])
-    sums_ref[...] = sums
-    last = sums[rows - NS :, :].astype(jnp.float32)[NS - 1 :, :]
+    sums = jnp.where(own, sums_own_ref[...], sums_come_ref[rows - NS :, :])
+    last = sums.astype(jnp.float32)[NS - 1 :, :]
     state_ref[...] = jnp.exp2(rates_ref[...] * last) * state
     chunk, several = CORES * LANES, 4
 
-    def some(index, nothing):
-        near = pl.ds(pl.multiple_of(index * NS, NS), NS)
-        for item in range(width // chunk):
-            lanes = slice(item * chunk, (item + 1) * chunk)
-            part = jnp.where(here, part_own_ref[near, lanes], part_come_ref[near, lanes])
-            total = part.astype(jnp.float32)
-            sums = sums_ref[near, lanes]
-            for first in range(0, NS, several):
-                terms = []
-                for n in range(first, first + several):
-                    decay = jnp.exp2(sums * wide_ref[n * NS : (n + 1) * NS, lanes])
-                    out_of = spread_ref[near, n * LANES : (n + 1) * LANES]
-                    out_of = jnp.concatenate([out_of] * (chunk // LANES), axis=1)
-                    terms.append(decay * begin_ref[n * NS : (n + 1) * NS, lanes] * out_of)
-                four = (terms[0] + terms[1]) + (terms[2] + terms[3])
-                total = total + four.astype(jnp.float32)
-            out_ref[near, lanes] = total.astype(jnp.bfloat16)
-        return nothing
-
-    lax.fori_loop(0, rows // NS, some, 0)
-
-
-def add_carried(places, parts, sums, maps, lasts, rates, carries):
-    blocks_come, _, rows = maps[1].shape
-    chips = blocks_come // CORES + 1
-    width = rates.shape[1]
+    def add_up(part_ref, near, lanes, factor_of):
+        total = part_ref[near, lanes].astype(jnp.float32)
+        for first in range(0, NS, several):
+            terms = [
+                factor_of(n) * begin_ref[n * NS : (n + 1) * NS, lanes]
+                for n in range(first, first + several)
+            ]
+            four = (terms[0] + terms[1]) + (terms[2] + terms[3])
+            total = total + four.astype(jnp.float32)
+        out_ref[near, lanes] = total.astype(jnp.bfloat16)
+
+    @pl.when(own)
+    def _():
+        def some(index, nothing):
+            start = pl.multiple_of(index * NS, NS)
+            for item in range(width // chunk):
+                lanes = slice(item * chunk, (item + 1) * chunk)
+                add_up(
+                    part_own_ref, pl.ds(start, NS), lanes,
+                    lambda n: factors_ref[
+                        pl.ds(pl.multiple_of(start * NS + n * NS, NS), NS), lanes
+                    ],
+                )
+            return nothing
+
+        lax.fori_loop(0, rows // NS, some, 0)
+
+    @pl.when(jnp.logical_not(own))
+    def _():
+        write_spread(spread_ref, maps_ref[0])
+
+        def some(index, nothing):
+            near = pl.ds(pl.multiple_of(index * NS, NS), NS)
+            for item in range(width // chunk):
+                lanes = slice(item * chunk, (item + 1) * chunk)
+                sums = sums_come_ref[near, lanes]
+                add_up(
+                    part_come_ref, near, lanes,
+                    lambda n: factor(sums, wide_ref, spread_ref, near, n, lanes),
+                )
+            return nothing
+
+        lax.fori_loop(0, rows // NS, some, 0)
+
+
+def add_carried(places, own, come, factors, rates, carries):
+    part_own, sums_own, _, last_own, total_own = own
+    part_come, sums_come, maps, last_come, total_come = come
+    others, _, width = last_come.shape
+    rows = part_own.shape[0] // CORES
+    chips = others + 1
 
     def core(b):
         return lax.rem(b, CORES)
 
-    def order(b, s):
-        chip = b // CORES
-        return jnp.minimum(
-            jnp.where(chip < s[0], b, jnp.maximum(b - CORES, 0)), blocks_come - 1
+    def other(b, s):
+        return jnp.minimum(b, others * CORES - 1)
+
+    def mine(b, s):
+        return jnp.maximum(b - others * CORES, 0)
+
+    def out(b, s):
+        place = b // CORES
+        chip = jnp.where(
+            place == others, s[0], jnp.where(place < s[0], place, place + 1)
         )
-
-    def before(b, s):
-        chip = jnp.maximum(b // CORES - 1, 0)
-        return jnp.minimum(jnp.where(chip < s[0], chip, jnp.maximum(chip - 1, 0)), chips - 2)
+        return (chip * CORES + core(b), 0)
 
     def fixed(*shape):
         return pl.BlockSpec(shape, lambda b, s: (0,) * len(shape))
 
-    own = pl.BlockSpec((rows, width), lambda b, s: (core(b), 0))
-    come = pl.BlockSpec((rows, width), lambda b, s: (order(b, s), 0))
+    last_rows = rows // NS
     return pl.pallas_call(
         carried_kernel,
         grid_spec=pltpu.PrefetchScalarGridSpec(
             num_scalar_prefetch=1,
             grid=(chips * CORES,),
             in_specs=[
-                own,
-                come,
-                own,
-                come,
-                pl.BlockSpec((1, 2 * NS, rows), lambda b, s: (core(b), 0, 0)),
-                pl.BlockSpec((1, 2 * NS, rows), lambda b, s: (order(b, s), 0, 0)),
-                fixed(NS, width),
-                pl.BlockSpec((1, NS, width), lambda b, s: (before(b, s), 0, 0)),
+                pl.BlockSpec((rows, width), lambda b, s: (mine(b, s), 0)),
+                pl.BlockSpec((rows, width), lambda b, s: (other(b, s), 0)),
+                pl.BlockSpec((rows * NS, width), lambda b, s: (mine(b, s), 0)),
+                pl.BlockSpec((NS, width), lambda b, s: ((mine(b, s) + 1) * last_rows - 1, 0)),
+                pl.BlockSpec((rows, width), lambda b, s: (other(b, s), 0)),
+                pl.BlockSpec((1, 2 * NS, rows), lambda b, s: (other(b, s), 0, 0)),
+                fixed(*last_own.shape),
+                fixed(*total_own.shape),
+                fixed(*last_come.shape),
+                fixed(*total_come.shape),
                 fixed(*rates.shape),
                 fixed(*carries.shape),
             ],
-            out_specs=pl.BlockSpec((rows, width), lambda b, s: (b, 0)),
+            out_specs=pl.BlockSpec((rows, width), out),
             scratch_shapes=[
                 pltpu.VMEM((NS, width), jnp.float32),
+                pltpu.VMEM((chips, NS, width), jnp.float32),
+                pltpu.VMEM((1, width), jnp.float32),
                 pltpu.VMEM((NS * NS, width), jnp.bfloat16),
                 pltpu.VMEM((NS * NS, width), jnp.bfloat16),
                 pltpu.VMEM((rows, NS * LANES), jnp.bfloat16),
-                pltpu.VMEM((rows, width), jnp.bfloat16),
             ],
         ),
         out_shape=jax.ShapeDtypeStruct((chips * CORES * rows, width), jnp.bfloat16),
         compiler_params=params,
         name="add_carried",
-    )(places, *parts, *sums, *maps, *lasts, rates, carries)
+    )(
+        places, part_own, part_come, factors, sums_own, sums_come, maps, last_own, total_own,
+        last_come, total_come, rates, carries,
+    )
 
 
 def local(
@@ -804,16 +797,15 @@
     got_stayed = lax.ppermute(stayed, "seq", swap)
     attn_rows = join_heads(sent, stayed, got_sent, got_stayed)
 
-    part_own, sums_own, maps_own, state, total = scan_own(stayed, low_own, cols, bias, rates, gain)
-    come, low_come = jnp.stack(come), jnp.stack(low_come)
-    steps, sums_come, maps_come, carry = step_sizes(
-        place, come, low_come, cols, bias, rates, state, total, targets, attn_rows
+    given = (cols, bias, rates, gain)
+    own = scan_tokens(place, stayed, low_own[None], *given, None, targets, None)
+    *come, carry = scan_tokens(
+        place, jnp.stack(come), jnp.stack(low_come), *given, own[3:], targets, attn_rows
     )
     carries = lax.all_to_all(carry, "chan", split_axis=0, concat_axis=0, tiled=True)
-    part_come, last_come = scan_others(place, come, steps, maps_come, rates, gain)
+    factors = make_factors(own[1], own[2], rates)
     ssm_rows = add_carried(
-        jnp.stack([chip, chan_place]), (part_own, part_come), (sums_own, sums_come),
-        (maps_own, maps_come), (state, last_come), rates, carries,
+        jnp.stack([chip, chan_place]), own, come, factors, rates, carries
     )
     return (attn_rows[None], ssm_rows[None])
 

time: 81.8 us -> 87 us (1.064)
  Pallas kernels: 46.8 us -> 50.5 us
    pallas_call x3, Pallas kernels: 23 us -> 25.1 us  [the longest x2 18.8 us: scan_tokens(): pl.pallas_call(functools.partial(tokens_kernel, carried=carried), grid_sp...]
    all_to_all x1, waiting for transfers between devices: 1.06 us -> 2.6 us  [local(): lax.all_to_all(carry, 'chan', split_axis=0, concat_axis=0, tiled=True)]
    pallas_call x1, Pallas kernels: 9.75 us -> 11.2 us  [add_carried(): pl.pallas_call(carried_kernel, grid_spec=pltpu.PrefetchScalarGridSpec(num...]
    unnamed x16 -> x18, local copies, waits for them, and re-layouts: 4.01 us -> 4.81 us
  transfers between devices with their start and end apart: 10 -> 10, of which waited for: 3 -> 2; matrix products, arithmetic and copies ran while one was open for 8% -> 7% of each run, Pallas kernels for 25% -> 23%
where the time goes in v1:
time: 87 us; the launch traced here: 86.4 us
  Pallas kernels  50.5 us (58%)
  starting transfers between devices  17.6 us (20%)
  local copies, waits for them, and re-layouts  8.21 us (9%)
  waiting for transfers between devices  6.56 us (8%)
  other arithmetic  2.8 us (3%)
    pallas_call x2, Pallas kernels, scan_tokens(): pl.pallas_call(functools.partial(tokens_kernel, carried=carried), grid_sp...  18.8 us
    pallas_call x1, Pallas kernels, add_carried(): pl.pallas_call(carried_kernel, grid_spec=pltpu.PrefetchScalarGridSpec(num...  11.2 us
    pallas_call x1, Pallas kernels, attend(): pl.pallas_call(functools.partial(attend_kernel, chips=chips), grid_spec=p...  8.07 us
    pallas_call x1, Pallas kernels, make_factors(): pl.pallas_call(factors_kernel, grid=(maps.shape[0] * parts,), in_specs=[p...  6.38 us
    all_to_all x1, starting transfers between devices, local(): lax.all_to_all(carry, 'chan', split_axis=0, concat_axis=0, tiled=True)  5.82 us
    unnamed x18, local copies, waits for them, and re-layouts  4.81 us
    ppermute x1, starting transfers between devices, local(): from_far = lax.ppermute(theirs, 'seq', far)  4.54 us
    ppermute x1, waiting for transfers between devices, local(): from_near = lax.ppermute(own, 'seq', near)  3.94 us
  transfers between devices with their start and end apart: 10, of which 2 were waited for; matrix products, arithmetic and copies ran while one was open for 7% of the time, Pallas kernels for 23%

profile of v1, /device:TPU:0, one launch (start us, length us, event | category | flops | bytes accessed | tf_op | source)
XLA Modules:
  0.0 86.4 jit_solution(7647831201017183075)
XLA Ops:
  0.6 0.0 copy-start
  0.6 2.1 %select_heads.1 = (bf16[2,2,128,256]{3,2,1,0:T(8,128)(2,1)}, bf16[2,2,128,256]{3,2,1,0:T(8,128)(2,1)}) custom-call(bf16[128,1024]{1,0:T(8,128)(2,1)} %bitcast.20, bf16[128,1024]{1,0:T(8,128)(2,1)} %bitcast.21), custom_call_target="tpu_custom_call" | custom-call | tf_op jit(solution)/shard_map/select_heads/pallas_call | solution.py:61
  2.7 0.5 collective-permute-start
  3.3 4.5 %collective-permute-start.3 = (bf16[2,2,128,256]{3,2,1,0:T(8,128)(2,1)}, bf16[2,2,128,256]{3,2,1,0:T(8,128)(2,1)S(1)}, u32[]{:S(2)}, u32[]{:S(2)}) collective-permute-start(bf16[2,2,128,256]{3,2,1,0:T(8,128)(2,1)} %get-tuple-element.21), channel_id=1, source_target_pairs={{0,24},{8,16},{1,25},{9,17},{2,26},{10,18},{3,27},{11,19},{4,28},{... | collective-permute-start | bytes 786440 | tf_op jit(solution)/shard_map/ppermute | solution.py:776
  7.8 0.1 collective-permute-start.1
  7.9 2.3 %collective-permute-start.2 = (bf16[2,2,128,256]{3,2,1,0:T(8,128)(2,1)}, bf16[2,2,128,256]{3,2,1,0:T(8,128)(2,1)}, u32[]{:S(2)}, u32[]{:S(2)}) collective-permute-start(bf16[2,2,128,256]{3,2,1,0:T(8,128)(2,1)} %get-tuple-element.19.own_ref), channel_id=1, source_target_pairs={{0,16},{8,24},{1,17},{9,25},{2,18},{10,26},{3,19},{11,27},{4,20},{... | collective-permute-start | bytes 786440 | tf_op jit(solution)/shard_map/ppermute | solution.py:775
  10.2 0.7 pad_add_fusion.place_ref
  10.9 1.3 %dynamic_slice.14 = f32[1024]{0:T(1024)} dynamic-slice(f32[4096]{0:T(1024)} %param.17, s32[]{:T(128)S(6)} %select_n.12), dynamic_slice_sizes={1024} | dynamic-slice | bytes 8196 | tf_op jit(solution)/shard_map/dynamic_slice | solution.py:786
  12.2 1.3 %dynamic_slice.15 = f32[1024]{0:T(1024)} dynamic-slice(f32[4096]{0:T(1024)} %param.19, s32[]{:T(128)S(6)} %select_n.12), dynamic_slice_sizes={1024} | dynamic-slice | bytes 8196 | tf_op jit(solution)/shard_map/dynamic_slice | solution.py:787
  13.5 1.5 %multiply_bitcast_fusion.rest_0_.rates_ref = f32[16,1024]{1,0:T(8,128)} fusion(f32[4096,16]{0,1:T(8,128)} %param.18, s32[]{:T(128)S(6)} %select_n.12), kind=kLoop, calls=%fused_computation | loop fusion | flops 16384 | bytes 131076 | tf_op jit(solution)/shard_map/transpose | solution.py:784
  14.9 0.0 copy-done
  14.9 0.8 constant_dynamic-slice_fusion.rest_1_.cols_ref
  15.8 0.0 collective-permute-done.3.far_ref
  15.8 0.0 collective-permute-done.1.swap_ref
  15.8 3.9 %collective-permute-done.2.near_ref = bf16[2,2,128,256]{3,2,1,0:T(8,128)(2,1)} collective-permute-done((bf16[2,2,128,256]{3,2,1,0:T(8,128)(2,1)}, bf16[2,2,128,256]{3,2,1,0:T(8,128)(2,1)}, u32[]{:S(2)}, u32[]{:S(2)}) %collective-permute-start.2) | collective-permute-done | bytes 262176 | tf_op jit(solution)/shard_map/ppermute | solution.py:775
  19.7 0.0 collective-permute-done.theirs_ref
  19.7 0.0 copy-start.5
  19.7 0.0 copy-done.7
  19.7 1.0 %copy-done.5 = bf16[128,4096]{1,0:T(8,128)(2,1)} copy-done((bf16[128,4096]{1,0:T(8,128)(2,1)}, bf16[128,4096]{1,0:T(8,128)(2,1)S(1)}, u32[]{:S(2)}) %copy-start.5) | copy-done | bytes 1048600
  20.7 8.1 %attend.1 = (bf16[1,256,1024]{2,1,0:T(8,128)(2,1)}, bf16[1,256,1024]{2,1,0:T(8,128)(2,1)}, f32[288,256]{1,0:T(8,128)}) custom-call(s32[2]{0:T(128)} %pad_add_fusion.place_ref, s32[1,16]{1,0:T(1,128)} %doc_ref.1, bf16[128,4096]{1,0:T(8,128)(2,1)} %bitcast.31, bf16[128,4096]{1,0:T(8,128)(2,1)} %copy-done.5, ...), custom_call_target="tpu_custom_call" | custom-call | flops 5000000000 | bytes 4194304 | tf_op jit(solution)/shard_map/attend/pallas_call | solution.py:235
  28.8 0.1 collective-permute-start.6
  28.9 0.5 collective-permute-start.4
  29.4 0.1 collective-permute-start.5
  29.4 2.5 %collective-permute-start.7 = (bf16[256,1024]{1,0:T(8,128)(2,1)}, bf16[256,1024]{1,0:T(8,128)(2,1)S(1)}, u32[]{:S(2)}, u32[]{:S(2)}) collective-permute-start(bf16[256,1024]{1,0:T(8,128)(2,1)} %bitcast.19), channel_id=1, source_target_pairs={{0,16},{8,24},{16,0},{24,8},{1,17},{9,25},{17,1},{25,9},{2,18},{10... | collective-permute-start | bytes 1572872 | tf_op jit(solution)/shard_map/ppermute | solution.py:793
  31.9 0.0 collective-permute-done.6.theirs_ref
  31.9 0.7 copy-done.4
  32.6 1.7 %low_and_maps.1 = bf16[288,256]{1,0:T(8,128)(2,1)} custom-call(f32[288,256]{1,0:T(8,128)} %get-tuple-element.24.mine_ref, f32[288,256]{1,0:T(8,128)} %copy-done.4), custom_call_target="tpu_custom_call" | custom-call | flops 1 | bytes 1 | tf_op jit(solution)/shard_map/low_and_maps/pallas_call | solution.py:273
  34.4 1.2 %collective-permute-start.8 = (bf16[288,256]{1,0:T(8,128)(2,1)}, bf16[288,256]{1,0:T(8,128)(2,1)S(1)}, u32[]{:S(2)}, u32[]{:S(2)}) collective-permute-start(bf16[288,256]{1,0:T(8,128)(2,1)} %low_and_maps.1), channel_id=1, source_target_pairs={{0,16},{8,24},{16,0},{24,8},{1,17},{9,25},{17,1},{25,9},{2,18},{10... | collective-permute-start | bytes 442376 | tf_op jit(solution)/shard_map/ppermute | solution.py:795
  35.6 9.1 %scan_tokens.2 = (bf16[256,1024]{1,0:T(8,128)(2,1)}, bf16[256,1024]{1,0:T(8,128)(2,1)}, f32[2,32,128]{2,1,0:T(8,128)}, f32[1,16,1024]{2,1,0:T(8,128)}, f32[1,1,1024]{2,1,0:T(1,128)}) custom-call(s32[2]{0:T(128)} %pad_add_fusion.place_ref, bf16[1,256,1024]{2,1,0:T(8,128)(2,1)} %get-tuple-element.23.stayed_ref.stream_ref, bf16[1,288,256]{2,1,0:T(8,128)(2,1)} %bitcast.22, ...), custom_call_target="tpu_custom_call" | custom-call | flops 4000000000 | bytes 2097152 | tf_op jit(solution)/shard_map/scan_tokens/pallas_call | solution.py:492
  44.7 0.0 collective-permute-done.4.got_sent_ref
  44.7 0.0 copy-start.2
  44.8 0.0 collective-permute-done.5.got_stayed_ref
  44.8 0.8 copy-done.2
  45.5 0.8 copy-done.3
  46.4 2.2 %join_heads.1.rest_2_ = bf16[128,4096]{1,0:T(8,128)(2,1)} custom-call(bf16[1,256,1024]{2,1,0:T(8,128)(2,1)} %get-tuple-element.22.sent_ref, bf16[1,256,1024]{2,1,0:T(8,128)(2,1)} %get-tuple-element.23.stayed_ref.stream_ref, bf16[1,256,1024]{2,1,0:T(8,128)(2,1)} %copy-done.2, bf16[1,256,1024]{2,1,0:T(8,128)(2,1)} %copy-done.3), custom_call_target="tpu_custom_call" | custom-call | tf_op jit(solution)/shard_map/join_heads/pallas_call | solution.py:90
  48.5 0.0 collective-permute-done.8
  48.6 0.0 copy-start.8
  48.6 0.0 collective-permute-done.7
  48.6 0.0 copy-start.6
  48.6 0.6 copy-done.8
  49.2 0.2 copy-done.6
  49.4 9.6 %scan_tokens.3 = (bf16[256,1024]{1,0:T(8,128)(2,1)}, bf16[256,1024]{1,0:T(8,128)(2,1)}, f32[2,32,128]{2,1,0:T(8,128)}, f32[1,16,1024]{2,1,0:T(8,128)}, f32[1,1,1...) custom-call(s32[2]{0:T(128)} %pad_add_fusion.place_ref, bf16[1,256,1024]{2,1,0:T(8,128)(2,1)} %bitcast.32, ...), custom_call_target="tpu_custom_call" | custom-call | flops 4000000000 | bytes 2097152 | tf_op jit(solution)/shard_map/scan_tokens/pallas_call | solution.py:492
  59.0 5.8 %all-to-all-start = ((bf16[8,144,128]{2,1,0:T(8,128)(2,1)}), bf16[8,144,128]{2,1,0:T(8,128)(2,1)S(1)}, u32[]{:S(2)}, u32[]{:S(2)}) async-start(bf16[8,144,128]{2,1,0:T(8,128)(2,1)} %get-tuple-element.35), calls=%async_computation | async-start | bytes 589824 | tf_op jit(solution)/shard_map/all_to_all | solution.py:805
  64.8 0.7 pad_add_fusion.1.places_ref
  65.5 6.4 %make_factors.1.factors_ref = bf16[4096,1024]{1,0:T(8,128)(2,1)} custom-call(bf16[256,1024]{1,0:T(8,128)(2,1)} %get-tuple-element.29.sums_ref.sums_own_ref, f32[2,32,128]{2,1,0:T(8,128)} %get-tuple-element.30.maps_ref, f32[16,1024]{1,0:T(8,128)} %multiply_bitcast_fusion.rest_0_.rates_ref), custom_call_target="tpu_custom_call" | custom-call | flops 3000000000 | bytes 8388608 | tf_op jit(solution)/shard_map/make_factors/pallas_call | solution.py:571
  71.9 2.6 %all-to-all-done.carries_ref = bf16[8,144,128]{2,1,0:T(8,128)(2,1)S(1)} async-done(((bf16[8,144,128]{2,1,0:T(8,128)(2,1)}), bf16[8,144,128]{2,1,0:T(8,128)(2,1)S(1)}, u32[]{:S(2)}, u32[]{:S(2)}) %all-to-all-start) | async-done | bytes 294944 | tf_op jit(solution)/shard_map/all_to_all | solution.py:805
  74.5 0.7 copy-done.1
  75.2 11.2 %add_carried.1 = bf16[512,1024]{1,0:T(8,128)(2,1)} custom-call(s32[2]{0:T(128)} %pad_add_fusion.1.places_ref, bf16[256,1024]{1,0:T(8,128)(2,1)} %get-tuple-element.25.part_own_ref, bf16[256,1024]{1,0:T(8,128)(2,1)} %get-tuple-element.28.part_come_ref, bf16[4096,1024]{1,0:T(8,128)(2,1)} %make_factors.1.factors_ref, ...), custom_call_target="tpu_custom_call" | custom-call | tf_op jit(solution)/shard_map/add_carried/pallas_call | solution.py:713
  (4 shorter events, 0.0 us)
Async XLA Ops:
  0.6 14.3 %copy-start = (bf16[256,4096]{1,0:T(8,128)(2,1)S(1)}, bf16[256,4096]{1,0:T(8,128)(2,1)}, u32[]{:S(2)}) copy-start(bf16[256,4096]{1,0:T(8,128)(2,1)} %param.16) | copy-start | bytes 6291460
  2.7 17.0 %collective-permute-start = (bf16[128,4096]{1,0:T(8,128)(2,1)}, bf16[128,4096]{1,0:T(8,128)(2,1)S(1)}, u32[]{:S(2)}, u32[]{:S(2)}) collective-permute-start(bf16[128,4096]{1,0:T(8,128)(2,1)} %bitcast.30), channel_id=1, source_target_pairs={{0,8},{8,0},{16,24},{24,16},{1,9},{9,1},{17,25},{25,17},{2,10},{10... | collective-permute-start | bytes 3145736 | tf_op jit(solution)/shard_map/ppermute | solution.py:779
  3.3 12.5 %collective-permute-start.3 = (bf16[2,2,128,256]{3,2,1,0:T(8,128)(2,1)}, bf16[2,2,128,256]{3,2,1,0:T(8,128)(2,1)S(1)}, u32[]{:S(2)}, u32[]{:S(2)}) collective-permute-start(bf16[2,2,128,256]{3,2,1,0:T(8,128)(2,1)} %get-tuple-element.21), channel_id=1, source_target_pairs={{0,24},{8,16},{1,25},{9,17},{2,26},{10,18},{3,27},{11,19},{4,28},{... | collective-permute-start | bytes 786440 | tf_op jit(solution)/shard_map/ppermute | solution.py:776
  7.8 8.0 %collective-permute-start.1 = (bf16[2,2,128,256]{3,2,1,0:T(8,128)(2,1)}, bf16[2,2,128,256]{3,2,1,0:T(8,128)(2,1)}, u32[]{:S(2)}, u32[]{:S(2)}) collective-permute-start(bf16[2,2,128,256]{3,2,1,0:T(8,128)(2,1)} %get-tuple-element.21), channel_id=1, source_target_pairs={{0,8},{8,0},{16,24},{24,16},{1,9},{9,1},{17,25},{25,17},{2,10},{10... | collective-permute-start | bytes 786440 | tf_op jit(solution)/shard_map/ppermute | solution.py:777
  7.9 11.8 %collective-permute-start.2 = (bf16[2,2,128,256]{3,2,1,0:T(8,128)(2,1)}, bf16[2,2,128,256]{3,2,1,0:T(8,128)(2,1)}, u32[]{:S(2)}, u32[]{:S(2)}) collective-permute-start(bf16[2,2,128,256]{3,2,1,0:T(8,128)(2,1)} %get-tuple-element.19.own_ref), channel_id=1, source_target_pairs={{0,16},{8,24},{1,17},{9,25},{2,18},{10,26},{3,19},{11,27},{4,20},{... | collective-permute-start | bytes 786440 | tf_op jit(solution)/shard_map/ppermute | solution.py:775
  15.8 4.0 %copy-start.7 = (bf16[2,2,128,256]{3,2,1,0:T(8,128)(2,1)}, bf16[2,2,128,256]{3,2,1,0:T(8,128)(2,1)S(1)}, u32[]{:S(2)}) copy-start(bf16[2,2,128,256]{3,2,1,0:T(8,128)(2,1)S(1)} %collective-permute-done.3.far_ref) | copy-start | bytes 786436
  19.7 1.0 %copy-start.5 = (bf16[128,4096]{1,0:T(8,128)(2,1)}, bf16[128,4096]{1,0:T(8,128)(2,1)S(1)}, u32[]{:S(2)}) copy-start(bf16[128,4096]{1,0:T(8,128)(2,1)S(1)} %collective-permute-done.theirs_ref) | copy-start | bytes 3145732
  28.8 3.1 %collective-permute-start.6 = (f32[288,256]{1,0:T(8,128)}, f32[288,256]{1,0:T(8,128)S(1)}, u32[]{:S(2)}, u32[]{:S(2)}) collective-permute-start(f32[288,256]{1,0:T(8,128)} %get-tuple-element.24.mine_ref), channel_id=1, source_target_pairs={{0,8},{8,0},{16,24},{24,16},{1,9},{9,1},{17,25},{25,17},{2,10},{10... | collective-permute-start | bytes 884744 | tf_op jit(solution)/shard_map/ppermute | solution.py:794
  28.9 15.9 %collective-permute-start.4 = (bf16[1,256,1024]{2,1,0:T(8,128)(2,1)}, bf16[1,256,1024]{2,1,0:T(8,128)(2,1)S(1)}, u32[]{:S(2)}, u32[]{:S(2)}) collective-permute-start(bf16[1,256,1024]{2,1,0:T(8,128)(2,1)} %get-tuple-element.22.sent_ref), channel_id=1, source_target_pairs={{0,8},{8,0},{16,24},{24,16},{1,9},{9,1},{17,25},{25,17},{2,10},{10... | collective-permute-start | bytes 1572872 | tf_op jit(solution)/shard_map/ppermute | solution.py:796
  29.4 15.4 %collective-permute-start.5 = (bf16[1,256,1024]{2,1,0:T(8,128)(2,1)}, bf16[1,256,1024]{2,1,0:T(8,128)(2,1)S(1)}, u32[]{:S(2)}, u32[]{:S(2)}) collective-permute-start(bf16[1,256,1024]{2,1,0:T(8,128)(2,1)} %get-tuple-element.23.stayed_ref.stream_ref), channel_id=1, source_target_pairs={{0,8},{8,0},{16,24},{24,16},{1,9},{9,1},{17,25},{25,17},{2,10},{10... | collective-permute-start | bytes 1572872 | tf_op jit(solution)/shard_map/ppermute | solution.py:797
  29.4 19.1 %collective-permute-start.7 = (bf16[256,1024]{1,0:T(8,128)(2,1)}, bf16[256,1024]{1,0:T(8,128)(2,1)S(1)}, u32[]{:S(2)}, u32[]{:S(2)}) collective-permute-start(bf16[256,1024]{1,0:T(8,128)(2,1)} %bitcast.19), channel_id=1, source_target_pairs={{0,16},{8,24},{16,0},{24,8},{1,17},{9,25},{17,1},{25,9},{2,18},{10... | collective-permute-start | bytes 1572872 | tf_op jit(solution)/shard_map/ppermute | solution.py:793
  31.9 0.7 copy-start.4
  34.4 14.2 %collective-permute-start.8 = (bf16[288,256]{1,0:T(8,128)(2,1)}, bf16[288,256]{1,0:T(8,128)(2,1)S(1)}, u32[]{:S(2)}, u32[]{:S(2)}) collective-permute-start(bf16[288,256]{1,0:T(8,128)(2,1)} %low_and_maps.1), channel_id=1, source_target_pairs={{0,16},{8,24},{16,0},{24,8},{1,17},{9,25},{17,1},{25,9},{2,18},{10... | collective-permute-start | bytes 442376 | tf_op jit(solution)/shard_map/ppermute | solution.py:795
  44.7 0.8 copy-start.2
  45.5 0.8 copy-start.3
  48.6 0.7 copy-start.8
  48.6 0.8 copy-start.6
  59.0 15.5 %all-to-all-start = ((bf16[8,144,128]{2,1,0:T(8,128)(2,1)}), bf16[8,144,128]{2,1,0:T(8,128)(2,1)S(1)}, u32[]{:S(2)}, u32[]{:S(2)}) async-start(bf16[8,144,128]{2,1,0:T(8,128)(2,1)} %get-tuple-element.35), calls=%async_computation | async-start | bytes 589824 | tf_op jit(solution)/shard_map/all_to_all | solution.py:805
  74.5 0.7 copy-start.1

commit v2 on v0

--- a/solution.py
+++ b/solution.py
@@ -22,6 +22,7 @@
 
 masked_fill = -1e30
 params = pltpu.CompilerParams(vmem_limit_bytes=60 << 20)
+less = pltpu.CompilerParams(vmem_limit_bytes=40 << 20)
 
 
 def split(value):
@@ -299,36 +300,43 @@
 
 
 def step_kernel(
-    place_ref, stream_ref, low_ref, map_ref, cols_ref, bias_ref, rates_ref, *rest
+    place_ref, stream_ref, low_ref, cols_ref, bias_ref, rates_ref, *rest
 ):
     own_state_ref, own_total_ref = rest[:2]
-    steps_ref, sums_ref, maps_ref, carry_ref, state_ref, total_ref, wide_ref, turn_ref = rest[3:]
+    steps_ref, sums_ref, maps_ref, carry_ref, state_ref, total_ref, wide_ref, turn_ref = rest[2:]
     block = pl.program_id(0)
-    rows, width = stream_ref.shape[1:]
+    others, both, width = stream_ref.shape
+    rows = both // CORES
+    chip = block // CORES
+    slot = lax.rem(
+        place_ref[0] - jnp.where(chip < place_ref[0], chip, chip + 1) + others + 1, others + 1
+    ) - 1
+    here = pl.ds(pl.multiple_of(lax.rem(block, CORES) * rows, rows), rows)
+    stream = stream_ref[slot, here, :]
 
     @pl.when(block == 0)
     def _():
         state_ref[...] = jnp.zeros_like(state_ref)
         total_ref[...] = jnp.zeros_like(total_ref)
         for n in range(NS):
-            wide_ref[n * SUBLANES : (n + 1) * SUBLANES, :] = jnp.broadcast_to(
-                rates_ref[n : n + 1, :], (SUBLANES, width)
-            )
+            wide_ref[n * NS : (n + 1) * NS, :] = jnp.broadcast_to(
+                rates_ref[n : n + 1, :], (NS, width)
+            ).astype(jnp.bfloat16)
 
     @pl.when(block == place_ref[0] * CORES)
     def _():
         add_states(rates_ref, state_ref, total_ref, own_state_ref[...], own_total_ref[...])
 
-    maps = map_ref[0].astype(jnp.float32)
+    maps = low_ref[slot, both:, here].astype(jnp.float32)
     maps_ref[0] = maps
-    logits = jnp.dot(low_ref[0], cols_ref[...], preferred_element_type=jnp.float32)
+    logits = jnp.dot(low_ref[slot, here, :], cols_ref[...], preferred_element_type=jnp.float32)
     steps = softplus(logits + bias_ref[...]).astype(jnp.bfloat16)
     steps_ref[...] = steps
-    push = steps * stream_ref[0]
+    push = steps * stream
     within = sums_within(steps)
     sums_ref[...] = within.astype(jnp.bfloat16)
     whole = within[rows - 1 :, :]
-    left = whole - within
+    left = (whole - within).astype(jnp.bfloat16)
     some, chunk, several = rows // 2, CORES * LANES, 4
     state_row = lax.broadcasted_iota(jnp.int32, (NS, some), 0)
     for first in range(0, rows, some):
@@ -345,17 +353,16 @@
         ]
         for item in range(width // chunk):
             lanes = slice(item * chunk, (item + 1) * chunk)
-            left_here = left[span, lanes].reshape(some // SUBLANES, SUBLANES, chunk)
-            push_here = push[span, lanes]
+            left_here = left[span, lanes].reshape(some // NS, NS, chunk)
+            push_here = push[span, lanes].reshape(some // NS, NS, chunk)
             added = state_ref[:, lanes]
             if first == 0:
                 added = jnp.exp2(rates_ref[:, lanes] * whole[:, lanes]) * added
             for n in range(0, NS, several):
                 pushed = []
                 for m in range(n, n + several):
-                    rate = wide_ref[m * SUBLANES : (m + 1) * SUBLANES, lanes]
-                    decay = jnp.exp2(left_here * rate[None]).reshape(some, chunk)
-                    pushed.append(decay.astype(jnp.bfloat16) * push_here)
+                    decay = jnp.exp2(left_here * wide_ref[m * NS : (m + 1) * NS, lanes][None])
+                    pushed.append((decay * push_here).reshape(some, chunk))
                 added = added + jnp.dot(
                     chosen[n // several],
                     jnp.concatenate(pushed, axis=0),
@@ -377,20 +384,11 @@
             carry_ref[target] = carry_ref[0]
 
 
-def step_sizes(place, stream, lows, cols, bias, rates, state, total, targets, after):
+def step_sizes(place, stream, lows, cols, bias, rates, state, total, targets):
     others = stream.shape[0]
-    chips = others + 1
     rows, width = stream.shape[1] // CORES, stream.shape[2]
-    map_row = CORES * rows // MAPS
     blocks = others * CORES
     carry = (targets, (width // LANES + 1) * NS, LANES)
-
-    def slot(b, s):
-        chip = b // CORES
-        return lax.rem(s[0] - jnp.where(chip < s[0], chip, chip + 1) + chips, chips) - 1
-
-    def core(b):
-        return lax.rem(b, CORES)
 
     def fixed(*shape):
         return pl.BlockSpec(shape, lambda b, s: (0,) * len(shape))
@@ -401,15 +399,13 @@
             num_scalar_prefetch=1,
             grid=(blocks,),
             in_specs=[
-                pl.BlockSpec((1, rows, width), lambda b, s: (slot(b, s), core(b), 0)),
-                pl.BlockSpec((1, rows, RANK), lambda b, s: (slot(b, s), core(b), 0)),
-                pl.BlockSpec((1, MAPS, rows), lambda b, s: (slot(b, s), map_row, core(b))),
+                pl.BlockSpec(memory_space=pltpu.VMEM),
+                pl.BlockSpec(memory_space=pltpu.VMEM),
                 fixed(*cols.shape),
                 fixed(*bias.shape),
                 fixed(*rates.shape),
                 fixed(*state.shape),
                 fixed(*total.shape),
-                pl.BlockSpec(memory_space=pl.ANY),
             ],
             out_specs=[
                 pl.BlockSpec((rows, width), lambda b, s: (b, 0)),
@@ -420,7 +416,7 @@
             scratch_shapes=[
                 pltpu.VMEM((NS, width), jnp.float32),
                 pltpu.VMEM((1, width), jnp.float32),
-                pltpu.VMEM((NS * SUBLANES, width), jnp.float32),
+                pltpu.VMEM((NS * NS, width), jnp.bfloat16),
                 pltpu.VMEM((SUBLANES, LANES), jnp.float32),
             ],
         ),
@@ -430,9 +426,9 @@
             jax.ShapeDtypeStruct((blocks, 2 * NS, rows), jnp.float32),
             jax.ShapeDtypeStruct(carry, jnp.bfloat16),
         ],
-        compiler_params=params,
+        compiler_params=less,
         name="step_sizes",
-    )(place, stream, lows, lows, cols, bias, rates, state, total, after)
+    )(place, stream, lows, cols, bias, rates, state, total)
 
 
 def write_carry(out_ref, state, total, turn_ref):
@@ -576,7 +572,7 @@
             jax.ShapeDtypeStruct((1, width), jnp.float32),
         ],
         scratch_shapes=[pltpu.VMEM((rows, width), jnp.bfloat16)] + work_shapes(rows, width),
-        compiler_params=params,
+        compiler_params=less,
         cost_estimate=pl.CostEstimate(flops=4 * 10**9, bytes_accessed=1 << 21, transcendentals=0),
         name="scan_own",
     )(stream, lows, lows, cols, bias, rates, gain)
@@ -626,7 +622,7 @@
             jax.ShapeDtypeStruct((others * CORES * rows, width), jnp.bfloat16),
             jax.ShapeDtypeStruct((others, NS, width), jnp.float32),
         ],
-        compiler_params=params,
+        compiler_params=less,
         cost_estimate=pl.CostEstimate(flops=4 * 10**9, bytes_accessed=1 << 21, transcendentals=0),
         name="scan_others",
     )(place, stream, steps, maps, rates, gain)
@@ -650,7 +646,7 @@
             follow(carries_ref.at[row], rates_ref, state_ref)
             return nothing
 
-        lax.fori_loop(0, places_ref[1], compose, 0)
+        lax.fori_loop(0, lax.axis_index("chan"), compose, 0)
         for n in range(NS):
             wide_ref[n * NS : (n + 1) * NS, :] = jnp.broadcast_to(
                 rates_ref[n : n + 1, :], (NS, width)
@@ -738,7 +734,7 @@
                 fixed(NS, width),
                 pl.BlockSpec((1, NS, width), lambda b, s: (before(b, s), 0, 0)),
                 fixed(*rates.shape),
-                fixed(*carries.shape),
+                pl.BlockSpec(memory_space=pltpu.VMEM),
             ],
             out_specs=pl.BlockSpec((rows, width), lambda b, s: (b, 0)),
             scratch_shapes=[
@@ -750,7 +746,7 @@
             ],
         ),
         out_shape=jax.ShapeDtypeStruct((chips * CORES * rows, width), jnp.bfloat16),
-        compiler_params=params,
+        compiler_params=less,
         name="add_carried",
     )(places, *parts, *sums, *maps, *lasts, rates, carries)
 
@@ -762,7 +758,6 @@
     chips = devices // CORES
     targets = lax.axis_size("chan")
     seq_place = lax.axis_index("seq").astype(jnp.int32)
-    chan_place = lax.axis_index("chan").astype(jnp.int32)
     chip, core = seq_place // CORES, lax.rem(seq_place, CORES)
     place = jnp.stack([chip, core])
     width = queries.shape[2] // devices
@@ -782,7 +777,7 @@
     from_near = lax.ppermute(own, "seq", near)
     from_far = lax.ppermute(theirs, "seq", far)
     swapped = lax.ppermute(theirs, "seq", swap)
-    queries_after, _ = lax.optimization_barrier((queries[0], own))
+    queries_after, swapped = lax.optimization_barrier((queries[0], swapped))
     their_queries = lax.ppermute(queries_after, "seq", swap)
     blocks = (own, swapped, from_near, from_far)
 
@@ -806,13 +801,14 @@
 
     part_own, sums_own, maps_own, state, total = scan_own(stayed, low_own, cols, bias, rates, gain)
     come, low_come = jnp.stack(come), jnp.stack(low_come)
+    state, attn_rows = lax.optimization_barrier((state, attn_rows))
     steps, sums_come, maps_come, carry = step_sizes(
-        place, come, low_come, cols, bias, rates, state, total, targets, attn_rows
+        place, come, low_come, cols, bias, rates, state, total, targets
     )
     carries = lax.all_to_all(carry, "chan", split_axis=0, concat_axis=0, tiled=True)
     part_come, last_come = scan_others(place, come, steps, maps_come, rates, gain)
     ssm_rows = add_carried(
-        jnp.stack([chip, chan_place]), (part_own, part_come), (sums_own, sums_come),
+        place, (part_own, part_come), (sums_own, sums_come),
         (maps_own, maps_come), (state, last_come), rates, carries,
     )
     return (attn_rows[None], ssm_rows[None])

time: 81.8 us -> 87.2 us (1.066)
  local copies, waits for them, and re-layouts: 7.41 us -> 19.5 us
  Pallas kernels: 46.8 us -> 39.1 us
    unnamed x16 -> x54, local copies, waits for them, and re-layouts: 4.01 us -> 16.1 us
    pallas_call x1, Pallas kernels: 6.6 us -> 4.31 us  [step_sizes(): pl.pallas_call(step_kernel, grid_spec=pltpu.PrefetchScalarGridSpec(num_sc...]
    pallas_call x1, Pallas kernels: 7.97 us -> 6.01 us  [scan_others(): pl.pallas_call(others_kernel, grid_spec=pltpu.PrefetchScalarGridSpec(num_...]
    pallas_call x1, Pallas kernels: 8.42 us -> 6.46 us  [scan_own(): pl.pallas_call(own_kernel, grid=(CORES,), in_specs=[pl.BlockSpec((1, rows...]
    pallas_call x1, Pallas kernels: 9.75 us -> 8.01 us  [add_carried(): pl.pallas_call(carried_kernel, grid_spec=pltpu.PrefetchScalarGridSpec(num...]
    ppermute x1, waiting for transfers between devices: 0.01 us -> 1.37 us  [local(): swapped = lax.ppermute(theirs, 'seq', swap)]
  transfers between devices with their start and end apart: 10 -> 10, of which waited for: 3 -> 4; matrix products, arithmetic and copies ran while one was open for 8% -> 6% of each run, Pallas kernels for 25% -> 19%
where the time goes in v2:
time: 87.2 us; the launch traced here: 86.2 us
  Pallas kernels  39.1 us (45%)
  local copies, waits for them, and re-layouts  19.5 us (22%)
  starting transfers between devices  18.3 us (21%)
  waiting for transfers between devices  6.5 us (7%)
  other arithmetic  2.02 us (2%)
    unnamed x54, local copies, waits for them, and re-layouts  16.1 us
    pallas_call x1, Pallas kernels, attend(): pl.pallas_call(functools.partial(attend_kernel, chips=chips), grid_spec=p...  8.3 us
    pallas_call x1, Pallas kernels, add_carried(): pl.pallas_call(carried_kernel, grid_spec=pltpu.PrefetchScalarGridSpec(num...  8.01 us
    pallas_call x1, Pallas kernels, scan_own(): pl.pallas_call(own_kernel, grid=(CORES,), in_specs=[pl.BlockSpec((1, rows...  6.46 us
    pallas_call x1, Pallas kernels, scan_others(): pl.pallas_call(others_kernel, grid_spec=pltpu.PrefetchScalarGridSpec(num_...  6.01 us
    all_to_all x1, starting transfers between devices, local(): lax.all_to_all(carry, 'chan', split_axis=0, concat_axis=0, tiled=True)  5.81 us
    ppermute x1, starting transfers between devices, local(): from_far = lax.ppermute(theirs, 'seq', far)  5.24 us
    pallas_call x1, Pallas kernels, step_sizes(): pl.pallas_call(step_kernel, grid_spec=pltpu.PrefetchScalarGridSpec(num_sc...  4.31 us
  transfers between devices with their start and end apart: 10, of which 4 were waited for; matrix products, arithmetic and copies ran while one was open for 6% of the time, Pallas kernels for 19%

profile of v2, /device:TPU:0, one launch (start us, length us, event | category | flops | bytes accessed | tf_op | source)
XLA Modules:
  0.0 86.2 jit_solution(3464647879682497266)
XLA Ops:
  0.6 0.0 copy-start
  0.6 2.1 %select_heads.1 = (bf16[2,2,128,256]{3,2,1,0:T(8,128)(2,1)}, bf16[2,2,128,256]{3,2,1,0:T(8,128)(2,1)}) custom-call(bf16[128,1024]{1,0:T(8,128)(2,1)} %bitcast.27, bf16[128,1024]{1,0:T(8,128)(2,1)} %bitcast.28), custom_call_target="tpu_custom_call" | custom-call | tf_op jit(solution)/shard_map/select_heads/pallas_call | solution.py:62
  2.7 0.5 collective-permute-start
  3.3 1.4 %collective-permute-done.swap_ref = bf16[2,2,128,256]{3,2,1,0:T(8,128)(2,1)S(1)} collective-permute-done((bf16[2,2,128,256]{3,2,1,0:T(8,128)(2,1)}, bf16[2,2,128,256]{3,2,1,0:T(8,128)(2,1)S(1)}, u32[]{:S(2)}, u32[]{:S(2)}) %collective-permute-start) | collective-permute-done | bytes 262176 | tf_op jit(solution)/shard_map/ppermute | solution.py:779
  4.6 0.4 collective-permute-start.1
  5.0 5.2 %collective-permute-start.3 = (bf16[2,2,128,256]{3,2,1,0:T(8,128)(2,1)}, bf16[2,2,128,256]{3,2,1,0:T(8,128)(2,1)}, u32[]{:S(2)}, u32[]{:S(2)}) collective-permute-start(bf16[2,2,128,256]{3,2,1,0:T(8,128)(2,1)} %get-tuple-element.22), channel_id=1, source_target_pairs={{0,24},{8,16},{1,25},{9,17},{2,26},{10,18},{3,27},{11,19},{4,28},{... | collective-permute-start | bytes 786440 | tf_op jit(solution)/shard_map/ppermute | solution.py:778
  10.2 2.0 %collective-permute-start.2 = (bf16[2,2,128,256]{3,2,1,0:T(8,128)(2,1)}, bf16[2,2,128,256]{3,2,1,0:T(8,128)(2,1)}, u32[]{:S(2)}, u32[]{:S(2)}) collective-permute-start(bf16[2,2,128,256]{3,2,1,0:T(8,128)(2,1)} %get-tuple-element.24.own_ref), channel_id=1, source_target_pairs={{0,16},{8,24},{1,17},{9,25},{2,18},{10,26},{3,19},{11,27},{4,20},{... | collective-permute-start | bytes 786440 | tf_op jit(solution)/shard_map/ppermute | solution.py:777
  12.2 0.6 pad_add_fusion.place_ref.places_ref
  12.8 1.3 %dynamic_slice.14 = f32[1024]{0:T(1024)} dynamic-slice(f32[4096]{0:T(1024)} %param.17, s32[]{:T(128)S(6)} %select_n.12), dynamic_slice_sizes={1024} | dynamic-slice | bytes 8196 | tf_op jit(solution)/shard_map/dynamic_slice | solution.py:788
  14.1 1.3 %dynamic_slice.15 = f32[1024]{0:T(1024)} dynamic-slice(f32[4096]{0:T(1024)} %param.19, s32[]{:T(128)S(6)} %select_n.12), dynamic_slice_sizes={1024} | dynamic-slice | bytes 8196 | tf_op jit(solution)/shard_map/dynamic_slice | solution.py:789
  15.3 1.5 %multiply_bitcast_fusion.rest_0_.rates_ref = f32[16,1024]{1,0:T(8,128)} fusion(f32[4096,16]{0,1:T(8,128)} %param.18, s32[]{:T(128)S(6)} %select_n.12), kind=kLoop, calls=%fused_computation | loop fusion | flops 16384 | bytes 131076 | tf_op jit(solution)/shard_map/transpose | solution.py:786
  16.8 0.8 constant_dynamic-slice_fusion.rest_1_.cols_ref
  17.7 0.0 collective-permute-done.3.far_ref
  17.7 3.9 %collective-permute-done.2.near_ref = bf16[2,2,128,256]{3,2,1,0:T(8,128)(2,1)} collective-permute-done((bf16[2,2,128,256]{3,2,1,0:T(8,128)(2,1)}, bf16[2,2,128,256]{3,2,1,0:T(8,128)(2,1)}, u32[]{:S(2)}, u32[]{:S(2)}) %collective-permute-start.2) | collective-permute-done | bytes 262176 | tf_op jit(solution)/shard_map/ppermute | solution.py:777
  21.6 1.0 %copy-done.25 = bf16[128,4096]{1,0:T(8,128)(2,1)} copy-done((bf16[128,4096]{1,0:T(8,128)(2,1)}, bf16[128,4096]{1,0:T(8,128)(2,1)S(1)}, u32[]{:S(2)}) %copy-start.25) | copy-done | bytes 1048600
  22.6 8.3 %attend.1 = (bf16[1,256,1024]{2,1,0:T(8,128)(2,1)}, bf16[1,256,1024]{2,1,0:T(8,128)(2,1)}, f32[288,256]{1,0:T(8,128)}) custom-call(s32[2]{0:T(128)} %pad_add_fusion.place_ref.places_ref, s32[1,16]{1,0:T(1,128)} %doc_ref.1, bf16[128,4096]{1,0:T(8,128)(2,1)} %bitcast.30, bf16[128,4096]{1,0:T(8,128)(2,1)} %copy-done.25, ...), custom_call_target="tpu_custom_call" | custom-call | flops 5000000000 | bytes 4194304 | tf_op jit(solution)/shard_map/attend/pallas_call | solution.py:236
  30.9 0.1 collective-permute-start.4
  31.0 0.5 collective-permute-start.6
  31.5 0.1 collective-permute-start.5
  31.6 2.5 %collective-permute-start.7 = (bf16[256,1024]{1,0:T(8,128)(2,1)}, bf16[256,1024]{1,0:T(8,128)(2,1)S(1)}, u32[]{:S(2)}, u32[]{:S(2)}) collective-permute-start(bf16[256,1024]{1,0:T(8,128)(2,1)} %bitcast.26), channel_id=1, source_target_pairs={{0,16},{8,24},{16,0},{24,8},{1,17},{9,25},{17,1},{25,9},{2,18},{10... | collective-permute-start | bytes 1572872 | tf_op jit(solution)/shard_map/ppermute | solution.py:795
  34.0 0.7 copy-done.24
  34.7 1.7 %low_and_maps.1.low_ref.map_ref = bf16[288,256]{1,0:T(8,128)(2,1)} custom-call(f32[288,256]{1,0:T(8,128)} %get-tuple-element.27.mine_ref, f32[288,256]{1,0:T(8,128)} %copy-done.24), custom_call_target="tpu_custom_call" | custom-call | flops 1 | bytes 1 | tf_op jit(solution)/shard_map/low_and_maps/pallas_call | solution.py:274
  36.5 1.2 %collective-permute-start.8 = (bf16[288,256]{1,0:T(8,128)(2,1)}, bf16[288,256]{1,0:T(8,128)(2,1)S(1)}, u32[]{:S(2)}, u32[]{:S(2)}) collective-permute-start(bf16[288,256]{1,0:T(8,128)(2,1)} %low_and_maps.1.low_ref.map_ref), channel_id=1, source_target_pairs={{0,16},{8,24},{16,0},{24,8},{1,17},{9,25},{17,1},{25,9},{2,18},{10... | collective-permute-start | bytes 442376 | tf_op jit(solution)/shard_map/ppermute | solution.py:797
  37.7 1.0 %copy-done.5 = bf16[1,256,1024]{2,1,0:T(8,128)(2,1)S(1)} copy-done((bf16[1,256,1024]{2,1,0:T(8,128)(2,1)S(1)}, bf16[1,256,1024]{2,1,0:T(8,128)(2,1)}, u32[]{:S(2)}) %copy-start.5) | copy-done | bytes 524312
  38.7 0.9 %copy-done.13 = bf16[288,256]{1,0:T(8,128)(2,1)S(1)} copy-done((bf16[288,256]{1,0:T(8,128)(2,1)S(1)}, bf16[288,256]{1,0:T(8,128)(2,1)}, u32[]{:S(2)}) %copy-start.13) | copy-done | bytes 147480
  39.6 6.5 %scan_own.1 = (bf16[256,1024]{1,0:T(8,128)(2,1)S(1)}, bf16[256,1024]{1,0:T(8,128)(2,1)S(1)}, f32[2,32,128]{2,1,0:T(8,128)S(1)}, f32[16,1024]{1,0:T(8,128)S(1)}, f32[1,1024]{1,0:T(1,128)S(1)}) custom-call(bf16[1,256,1024]{2,1,0:T(8,128)(2,1)S(1)} %copy-done.5, bf16[288,256]{1,0:T(8,128)(2,1)S(1)} %copy-done.13, bf16[288,256]{1,0:T(8,128)(2,1)S(1)} %copy-done.13, ...), custom_call_target="tpu_custom_call" | custom-call | flops 4000000000 | bytes 2097152 | tf_op jit(solution)/shard_map/scan_own/pallas_call | solution.py:548
  46.1 0.8 copy-done.3
  46.9 2.2 %join_heads.1 = bf16[128,4096]{1,0:T(8,128)(2,1)} custom-call(bf16[1,256,1024]{2,1,0:T(8,128)(2,1)} %get-tuple-element.29.sent_ref, bf16[1,256,1024]{2,1,0:T(8,128)(2,1)} %get-tuple-element.26.stream_ref.stayed_ref, bf16[1,256,1024]{2,1,0:T(8,128)(2,1)} %collective-permute-done.5.got_sent_ref, bf16[1,256,1024]{2,1,0:T(8,128)(2,1)} %collective-permute-done.6.got_stayed_ref), custom_call_target="tpu_custom_call" | custom-call | tf_op jit(solution)/shard_map/join_heads/pallas_call | solution.py:91
  49.2 0.8 collective-permute-done.8
  49.9 4.3 %step_sizes.1 = (bf16[256,1024]{1,0:T(8,128)(2,1)S(1)}, bf16[256,1024]{1,0:T(8,128)(2,1)S(1)}, f32[2,32,128]{2,1,0:T(8,128)S(1)}, bf16[8,144,128]{2,1,0:T(8,128)(2,1)S(1)}) custom-call(s32[2]{0:T(128)S(1)} %copy-done.21, bf16[1,256,1024]{2,1,0:T(8,128)(2,1)S(1)} %bitcast.15, bf16[1,288,256]{2,1,0:T(8,128)(2,1)S(1)} %bitcast.17, ...), custom_call_target="tpu_custom_call" | custom-call | tf_op jit(solution)/shard_map/step_sizes/pallas_call | solution.py:396
  54.3 0.8 copy-done.6
  55.0 0.7 copy-done.10
  55.8 0.6 copy-done.16
  56.4 0.8 copy-done.22
  57.2 5.8 %all-to-all-start = ((bf16[8,144,128]{2,1,0:T(8,128)(2,1)}), bf16[8,144,128]{2,1,0:T(8,128)(2,1)S(1)}, u32[]{:S(2)}, u32[]{:S(2)}) async-start(bf16[8,144,128]{2,1,0:T(8,128)(2,1)} %copy-done.10), calls=%async_computation | async-start | bytes 589824 | tf_op jit(solution)/shard_map/all_to_all | solution.py:808
  63.0 0.8 copy-done.17
  63.7 1.0 %copy-done.23 = bf16[256,1024]{1,0:T(8,128)(2,1)S(1)} copy-done((bf16[256,1024]{1,0:T(8,128)(2,1)S(1)}, bf16[256,1024]{1,0:T(8,128)(2,1)}, u32[]{:S(2)}) %copy-start.23) | copy-done | bytes 524312
  64.8 6.0 %scan_others.1 = (bf16[256,1024]{1,0:T(8,128)(2,1)S(1)}, f32[1,16,1024]{2,1,0:T(8,128)S(1)}) custom-call(s32[2]{0:T(128)S(1)} %copy-done.21, bf16[1,256,1024]{2,1,0:T(8,128)(2,1)S(1)} %bitcast.16, bf16[256,1024]{1,0:T(8,128)(2,1)S(1)} %copy-done.23, f32[2,32,128]{2,1,0:T(8,128)S(1)} %copy-done.17, f32[16,1024]{1,0:T(8,128)S(1)} %copy-done.2, ...), custom_call_target="tpu_custom_call" | custom-call | flops 4000000000 | bytes 2097152 | tf_op jit(solution)/shard_map/scan_others/pallas_call | solution.py:606
  70.8 0.8 copy-done.8
  71.6 0.6 copy-done.14
  72.2 0.4 all-to-all-done.carries_ref
  72.6 1.0 %copy-done.4 = bf16[256,1024]{1,0:T(8,128)(2,1)S(1)} copy-done((bf16[256,1024]{1,0:T(8,128)(2,1)S(1)}, bf16[256,1024]{1,0:T(8,128)(2,1)}, u32[]{:S(2)}) %copy-start.4) | copy-done | bytes 524312
  73.7 1.0 %copy-done.7 = bf16[256,1024]{1,0:T(8,128)(2,1)S(1)} copy-done((bf16[256,1024]{1,0:T(8,128)(2,1)S(1)}, bf16[256,1024]{1,0:T(8,128)(2,1)}, u32[]{:S(2)}) %copy-start.7) | copy-done | bytes 524312
  74.7 1.0 %copy-done.9 = bf16[256,1024]{1,0:T(8,128)(2,1)S(1)} copy-done((bf16[256,1024]{1,0:T(8,128)(2,1)S(1)}, bf16[256,1024]{1,0:T(8,128)(2,1)}, u32[]{:S(2)}) %copy-start.9) | copy-done | bytes 524312
  75.7 0.8 copy-done.12
  76.6 0.8 copy-done.15
  77.4 0.8 copy-done.18
  78.2 8.0 %add_carried.1 = bf16[512,1024]{1,0:T(8,128)(2,1)} custom-call(s32[2]{0:T(128)S(1)} %copy-done.21, bf16[256,1024]{1,0:T(8,128)(2,1)S(1)} %get-tuple-element.31.part_own_ref, bf16[256,1024]{1,0:T(8,128)(2,1)S(1)} %copy-done.9, bf16[256,1024]{1,0:T(8,128)(2,1)S(1)} %copy-done.4, bf16[256,1024]{1,0:T(8,128)(2,1)S(1)} %copy-done.7, ...), custom_call_target="tpu_custom_call" | custom-call | tf_op jit(solution)/shard_map/add_carried/pallas_call | solution.py:722
  (39 shorter events, 0.1 us)
Async XLA Ops:
  0.6 16.2 %copy-start = (bf16[256,4096]{1,0:T(8,128)(2,1)S(1)}, bf16[256,4096]{1,0:T(8,128)(2,1)}, u32[]{:S(2)}) copy-start(bf16[256,4096]{1,0:T(8,128)(2,1)} %param.16) | copy-start | bytes 6291460
  2.7 1.9 %collective-permute-start = (bf16[2,2,128,256]{3,2,1,0:T(8,128)(2,1)}, bf16[2,2,128,256]{3,2,1,0:T(8,128)(2,1)S(1)}, u32[]{:S(2)}, u32[]{:S(2)}) collective-permute-start(bf16[2,2,128,256]{3,2,1,0:T(8,128)(2,1)} %get-tuple-element.22), channel_id=1, source_target_pairs={{0,8},{8,0},{16,24},{24,16},{1,9},{9,1},{17,25},{25,17},{2,10},{10... | collective-permute-start | bytes 786440 | tf_op jit(solution)/shard_map/ppermute | solution.py:779
  4.6 17.0 %copy-start.26 = (bf16[2,2,128,256]{3,2,1,0:T(8,128)(2,1)}, bf16[2,2,128,256]{3,2,1,0:T(8,128)(2,1)S(1)}, u32[]{:S(2)}) copy-start(bf16[2,2,128,256]{3,2,1,0:T(8,128)(2,1)S(1)} %collective-permute-done.swap_ref) | copy-start | bytes 786436
  4.6 17.0 %collective-permute-start.1 = (bf16[128,4096]{1,0:T(8,128)(2,1)}, bf16[128,4096]{1,0:T(8,128)(2,1)S(1)}, u32[]{:S(2)}, u32[]{:S(2)}) collective-permute-start(bf16[128,4096]{1,0:T(8,128)(2,1)} %bitcast.29), channel_id=1, source_target_pairs={{0,8},{8,0},{16,24},{24,16},{1,9},{9,1},{17,25},{25,17},{2,10},{10... | collective-permute-start | bytes 3145736 | tf_op jit(solution)/shard_map/ppermute | solution.py:781
  5.0 12.7 %collective-permute-start.3 = (bf16[2,2,128,256]{3,2,1,0:T(8,128)(2,1)}, bf16[2,2,128,256]{3,2,1,0:T(8,128)(2,1)}, u32[]{:S(2)}, u32[]{:S(2)}) collective-permute-start(bf16[2,2,128,256]{3,2,1,0:T(8,128)(2,1)} %get-tuple-element.22), channel_id=1, source_target_pairs={{0,24},{8,16},{1,25},{9,17},{2,26},{10,18},{3,27},{11,19},{4,28},{... | collective-permute-start | bytes 786440 | tf_op jit(solution)/shard_map/ppermute | solution.py:778
  10.2 11.4 %collective-permute-start.2 = (bf16[2,2,128,256]{3,2,1,0:T(8,128)(2,1)}, bf16[2,2,128,256]{3,2,1,0:T(8,128)(2,1)}, u32[]{:S(2)}, u32[]{:S(2)}) collective-permute-start(bf16[2,2,128,256]{3,2,1,0:T(8,128)(2,1)} %get-tuple-element.24.own_ref), channel_id=1, source_target_pairs={{0,16},{8,24},{1,17},{9,25},{2,18},{10,26},{3,19},{11,27},{4,20},{... | collective-permute-start | bytes 786440 | tf_op jit(solution)/shard_map/ppermute | solution.py:777
  21.6 1.0 %copy-start.25 = (bf16[128,4096]{1,0:T(8,128)(2,1)}, bf16[128,4096]{1,0:T(8,128)(2,1)S(1)}, u32[]{:S(2)}) copy-start(bf16[128,4096]{1,0:T(8,128)(2,1)S(1)} %collective-permute-done.1.theirs_ref) | copy-start | bytes 3145732
  22.6 15.1 %copy-start.1 = (bf16[256,1024]{1,0:T(8,128)(2,1)S(1)}, bf16[256,1024]{1,0:T(8,128)(2,1)}, u32[]{:S(2)}) copy-start(bf16[256,1024]{1,0:T(8,128)(2,1)} %constant_dynamic-slice_fusion.rest_1_.cols_ref) | copy-start | bytes 1572868
  22.6 15.1 %copy-start.2 = (f32[16,1024]{1,0:T(8,128)S(1)}, f32[16,1024]{1,0:T(8,128)}, u32[]{:S(2)}) copy-start(f32[16,1024]{1,0:T(8,128)} %multiply_bitcast_fusion.rest_0_.rates_ref) | copy-start | bytes 196612
  22.6 15.1 %copy-start.19 = (f32[1024]{0:T(1024)S(1)}, f32[1024]{0:T(1024)}, u32[]{:S(2)}) copy-start(f32[1024]{0:T(1024)} %dynamic_slice.14) | copy-start | bytes 12292
  22.6 15.1 %copy-start.20 = (f32[1024]{0:T(1024)S(1)}, f32[1024]{0:T(1024)}, u32[]{:S(2)}) copy-start(f32[1024]{0:T(1024)} %dynamic_slice.15) | copy-start | bytes 12292
  30.9 3.1 %collective-permute-start.4 = (f32[288,256]{1,0:T(8,128)}, f32[288,256]{1,0:T(8,128)S(1)}, u32[]{:S(2)}, u32[]{:S(2)}) collective-permute-start(f32[288,256]{1,0:T(8,128)} %get-tuple-element.27.mine_ref), channel_id=1, source_target_pairs={{0,8},{8,0},{16,24},{24,16},{1,9},{9,1},{17,25},{25,17},{2,10},{10... | collective-permute-start | bytes 884744 | tf_op jit(solution)/shard_map/ppermute | solution.py:796
  31.0 15.9 %collective-permute-start.6 = (bf16[1,256,1024]{2,1,0:T(8,128)(2,1)}, bf16[1,256,1024]{2,1,0:T(8,128)(2,1)}, u32[]{:S(2)}, u32[]{:S(2)}) collective-permute-start(bf16[1,256,1024]{2,1,0:T(8,128)(2,1)} %get-tuple-element.26.stream_ref.stayed_ref), channel_id=1, source_target_pairs={{0,8},{8,0},{16,24},{24,16},{1,9},{9,1},{17,25},{25,17},{2,10},{10... | collective-permute-start | bytes 1572872 | tf_op jit(solution)/shard_map/ppermute | solution.py:799
  31.5 15.5 %collective-permute-start.5 = (bf16[1,256,1024]{2,1,0:T(8,128)(2,1)}, bf16[1,256,1024]{2,1,0:T(8,128)(2,1)}, u32[]{:S(2)}, u32[]{:S(2)}) collective-permute-start(bf16[1,256,1024]{2,1,0:T(8,128)(2,1)} %get-tuple-element.29.sent_ref), channel_id=1, source_target_pairs={{0,8},{8,0},{16,24},{24,16},{1,9},{9,1},{17,25},{25,17},{2,10},{10... | collective-permute-start | bytes 1572872 | tf_op jit(solution)/shard_map/ppermute | solution.py:798
  31.6 18.4 %collective-permute-start.7 = (bf16[256,1024]{1,0:T(8,128)(2,1)}, bf16[256,1024]{1,0:T(8,128)(2,1)S(1)}, u32[]{:S(2)}, u32[]{:S(2)}) collective-permute-start(bf16[256,1024]{1,0:T(8,128)(2,1)} %bitcast.26), channel_id=1, source_target_pairs={{0,16},{8,24},{16,0},{24,8},{1,17},{9,25},{17,1},{25,9},{2,18},{10... | collective-permute-start | bytes 1572872 | tf_op jit(solution)/shard_map/ppermute | solution.py:795
  34.0 0.7 copy-start.24
  36.5 13.4 %collective-permute-start.8 = (bf16[288,256]{1,0:T(8,128)(2,1)}, bf16[288,256]{1,0:T(8,128)(2,1)S(1)}, u32[]{:S(2)}, u32[]{:S(2)}) collective-permute-start(bf16[288,256]{1,0:T(8,128)(2,1)} %low_and_maps.1.low_ref.map_ref), channel_id=1, source_target_pairs={{0,16},{8,24},{16,0},{24,8},{1,17},{9,25},{17,1},{25,9},{2,18},{10... | collective-permute-start | bytes 442376 | tf_op jit(solution)/shard_map/ppermute | solution.py:797
  37.7 1.0 %copy-start.5 = (bf16[1,256,1024]{2,1,0:T(8,128)(2,1)S(1)}, bf16[1,256,1024]{2,1,0:T(8,128)(2,1)}, u32[]{:S(2)}) copy-start(bf16[1,256,1024]{2,1,0:T(8,128)(2,1)} %get-tuple-element.26.stream_ref.stayed_ref) | copy-start | bytes 1572868
  38.7 0.9 %copy-start.13 = (bf16[288,256]{1,0:T(8,128)(2,1)S(1)}, bf16[288,256]{1,0:T(8,128)(2,1)}, u32[]{:S(2)}) copy-start(bf16[288,256]{1,0:T(8,128)(2,1)} %low_and_maps.1.low_ref.map_ref) | copy-start | bytes 442372
  46.1 0.8 copy-start.3
  46.9 7.3 %copy-start.11 = (f32[16,1024]{1,0:T(8,128)}, f32[16,1024]{1,0:T(8,128)S(1)}, u32[]{:S(2)}) copy-start(f32[16,1024]{1,0:T(8,128)S(1)} %get-tuple-element.32.rest_0_.last_own_ref) | copy-start | bytes 196612
  46.9 3.0 %copy-start.21 = (s32[2]{0:T(128)S(1)}, s32[2]{0:T(128)}, u32[]{:S(2)}) copy-start(s32[2]{0:T(128)} %pad_add_fusion.place_ref.places_ref) | copy-start | bytes 28
  54.2 0.8 copy-start.6
  55.0 0.7 copy-start.10
  55.8 0.6 copy-start.16
  56.4 0.8 copy-start.22
  57.2 15.4 %all-to-all-start = ((bf16[8,144,128]{2,1,0:T(8,128)(2,1)}), bf16[8,144,128]{2,1,0:T(8,128)(2,1)S(1)}, u32[]{:S(2)}, u32[]{:S(2)}) async-start(bf16[8,144,128]{2,1,0:T(8,128)(2,1)} %copy-done.10), calls=%async_computation | async-start | bytes 589824 | tf_op jit(solution)/shard_map/all_to_all | solution.py:808
  63.0 0.8 copy-start.17
  63.7 1.0 %copy-start.23 = (bf16[256,1024]{1,0:T(8,128)(2,1)S(1)}, bf16[256,1024]{1,0:T(8,128)(2,1)}, u32[]{:S(2)}) copy-start(bf16[256,1024]{1,0:T(8,128)(2,1)} %copy-done.22) | copy-start | bytes 1572868
  70.8 0.8 copy-start.8
  71.6 0.6 copy-start.14
  72.6 1.0 %copy-start.4 = (bf16[256,1024]{1,0:T(8,128)(2,1)S(1)}, bf16[256,1024]{1,0:T(8,128)(2,1)}, u32[]{:S(2)}) copy-start(bf16[256,1024]{1,0:T(8,128)(2,1)} %copy-done.3) | copy-start | bytes 1572868
  73.7 1.0 %copy-start.7 = (bf16[256,1024]{1,0:T(8,128)(2,1)S(1)}, bf16[256,1024]{1,0:T(8,128)(2,1)}, u32[]{:S(2)}) copy-start(bf16[256,1024]{1,0:T(8,128)(2,1)} %copy-done.6) | copy-start | bytes 1572868
  74.7 1.0 %copy-start.9 = (bf16[256,1024]{1,0:T(8,128)(2,1)S(1)}, bf16[256,1024]{1,0:T(8,128)(2,1)}, u32[]{:S(2)}) copy-start(bf16[256,1024]{1,0:T(8,128)(2,1)} %copy-done.8) | copy-start | bytes 1572868
  75.7 0.8 copy-start.12
  76.6 0.8 copy-start.15
  77.4 0.8 copy-start.18

commit v3 on v0

--- a/solution.py
+++ b/solution.py
@@ -302,7 +302,7 @@
     place_ref, stream_ref, low_ref, map_ref, cols_ref, bias_ref, rates_ref, *rest
 ):
     own_state_ref, own_total_ref = rest[:2]
-    steps_ref, sums_ref, maps_ref, carry_ref, state_ref, total_ref, wide_ref, turn_ref = rest[3:]
+    steps_ref, sums_ref, maps_ref, carry_ref, state_ref, total_ref, wide_ref, turn_ref = rest[5:]
     block = pl.program_id(0)
     rows, width = stream_ref.shape[1:]
 
@@ -311,9 +311,9 @@
         state_ref[...] = jnp.zeros_like(state_ref)
         total_ref[...] = jnp.zeros_like(total_ref)
         for n in range(NS):
-            wide_ref[n * SUBLANES : (n + 1) * SUBLANES, :] = jnp.broadcast_to(
-                rates_ref[n : n + 1, :], (SUBLANES, width)
-            )
+            wide_ref[n * NS : (n + 1) * NS, :] = jnp.broadcast_to(
+                rates_ref[n : n + 1, :], (NS, width)
+            ).astype(jnp.bfloat16)
 
     @pl.when(block == place_ref[0] * CORES)
     def _():
@@ -328,7 +328,7 @@
     within = sums_within(steps)
     sums_ref[...] = within.astype(jnp.bfloat16)
     whole = within[rows - 1 :, :]
-    left = whole - within
+    left = (whole - within).astype(jnp.bfloat16)
     some, chunk, several = rows // 2, CORES * LANES, 4
     state_row = lax.broadcasted_iota(jnp.int32, (NS, some), 0)
     for first in range(0, rows, some):
@@ -345,17 +345,16 @@
         ]
         for item in range(width // chunk):
             lanes = slice(item * chunk, (item + 1) * chunk)
-            left_here = left[span, lanes].reshape(some // SUBLANES, SUBLANES, chunk)
-            push_here = push[span, lanes]
+            left_here = left[span, lanes].reshape(some // NS, NS, chunk)
+            push_here = push[span, lanes].reshape(some // NS, NS, chunk)
             added = state_ref[:, lanes]
             if first == 0:
                 added = jnp.exp2(rates_ref[:, lanes] * whole[:, lanes]) * added
             for n in range(0, NS, several):
                 pushed = []
                 for m in range(n, n + several):
-                    rate = wide_ref[m * SUBLANES : (m + 1) * SUBLANES, lanes]
-                    decay = jnp.exp2(left_here * rate[None]).reshape(some, chunk)
-                    pushed.append(decay.astype(jnp.bfloat16) * push_here)
+                    decay = jnp.exp2(left_here * wide_ref[m * NS : (m + 1) * NS, lanes][None])
+                    pushed.append((decay * push_here).reshape(some, chunk))
                 added = added + jnp.dot(
                     chosen[n // several],
                     jnp.concatenate(pushed, axis=0),
@@ -377,7 +376,7 @@
             carry_ref[target] = carry_ref[0]
 
 
-def step_sizes(place, stream, lows, cols, bias, rates, state, total, targets, after):
+def step_sizes(place, stream, lows, cols, bias, rates, state, total, targets, after, sums, maps):
     others = stream.shape[0]
     chips = others + 1
     rows, width = stream.shape[1] // CORES, stream.shape[2]
@@ -391,6 +390,9 @@
 
     def core(b):
         return lax.rem(b, CORES)
+
+    def in_row(b, s):
+        return jnp.where(b // CORES < s[0], b, b + CORES)
 
     def fixed(*shape):
         return pl.BlockSpec(shape, lambda b, s: (0,) * len(shape))
@@ -409,30 +411,31 @@
                 fixed(*rates.shape),
                 fixed(*state.shape),
                 fixed(*total.shape),
-                pl.BlockSpec(memory_space=pl.ANY),
-            ],
+            ]
+            + [pl.BlockSpec(memory_space=pl.ANY)] * 3,
             out_specs=[
                 pl.BlockSpec((rows, width), lambda b, s: (b, 0)),
-                pl.BlockSpec((rows, width), lambda b, s: (b, 0)),
-                pl.BlockSpec((1, 2 * NS, rows), lambda b, s: (b, 0, 0)),
+                pl.BlockSpec((rows, width), lambda b, s: (in_row(b, s), 0)),
+                pl.BlockSpec((1, 2 * NS, rows), lambda b, s: (in_row(b, s), 0, 0)),
                 fixed(*carry),
             ],
             scratch_shapes=[
                 pltpu.VMEM((NS, width), jnp.float32),
                 pltpu.VMEM((1, width), jnp.float32),
-                pltpu.VMEM((NS * SUBLANES, width), jnp.float32),
+                pltpu.VMEM((NS * NS, width), jnp.bfloat16),
                 pltpu.VMEM((SUBLANES, LANES), jnp.float32),
             ],
         ),
         out_shape=[
             jax.ShapeDtypeStruct((blocks * rows, width), jnp.bfloat16),
-            jax.ShapeDtypeStruct((blocks * rows, width), jnp.bfloat16),
-            jax.ShapeDtypeStruct((blocks, 2 * NS, rows), jnp.float32),
+            jax.ShapeDtypeStruct(sums.shape, sums.dtype),
+            jax.ShapeDtypeStruct(maps.shape, maps.dtype),
             jax.ShapeDtypeStruct(carry, jnp.bfloat16),
         ],
+        input_output_aliases={10: 1, 11: 2},
         compiler_params=params,
         name="step_sizes",
-    )(place, stream, lows, lows, cols, bias, rates, state, total, after)
+    )(place, stream, lows, lows, cols, bias, rates, state, total, after, sums, maps)
 
 
 def write_carry(out_ref, state, total, turn_ref):
@@ -520,7 +523,7 @@
 
 
 def own_kernel(
-    stream_ref, low_ref, map_ref, cols_ref, bias_ref, rates_ref, gain_ref,
+    place_ref, stream_ref, low_ref, map_ref, cols_ref, bias_ref, rates_ref, gain_ref,
     out_ref, sums_ref, maps_ref, state_ref, total_ref, steps_ref, *work_refs
 ):
     rows = steps_ref.shape[0]
@@ -541,50 +544,61 @@
     scan_blocks(stream_ref, steps_ref, maps, rates_ref, gain_ref, out_ref, state_ref, work_refs)
 
 
-def scan_own(stream, lows, cols, bias, rates, gain):
+def scan_own(place, stream, lows, cols, bias, rates, gain):
     rows, width = stream.shape[1] // CORES, stream.shape[2]
     map_row = CORES * rows // MAPS
 
+    blocks = lax.axis_size("seq")
+
+    def in_row(b, s):
+        return s[0] * CORES + b
+
     def fixed(*shape):
-        return pl.BlockSpec(shape, lambda b: (0,) * len(shape))
-
-    block = pl.BlockSpec((rows, width), lambda b: (b, 0))
+        return pl.BlockSpec(shape, lambda b, s: (0,) * len(shape))
+
+    block = pl.BlockSpec((rows, width), lambda b, s: (in_row(b, s), 0))
     return pl.pallas_call(
         own_kernel,
-        grid=(CORES,),
-        in_specs=[
-            pl.BlockSpec((1, rows, width), lambda b: (0, b, 0)),
-            pl.BlockSpec((rows, RANK), lambda b: (b, 0)),
-            pl.BlockSpec((MAPS, rows), lambda b: (map_row, b)),
-            fixed(*cols.shape),
-            fixed(*bias.shape),
-            fixed(*rates.shape),
-            fixed(*gain.shape),
-        ],
-        out_specs=[
-            block,
-            block,
-            pl.BlockSpec((1, 2 * NS, rows), lambda b: (b, 0, 0)),
-            fixed(NS, width),
-            fixed(1, width),
-        ],
+        grid_spec=pltpu.PrefetchScalarGridSpec(
+            num_scalar_prefetch=1,
+            grid=(CORES,),
+            in_specs=[
+                pl.BlockSpec((1, rows, width), lambda b, s: (0, b, 0)),
+                pl.BlockSpec((rows, RANK), lambda b, s: (b, 0)),
+                pl.BlockSpec((MAPS, rows), lambda b, s: (map_row, b)),
+                fixed(*cols.shape),
+                fixed(*bias.shape),
+                fixed(*rates.shape),
+                fixed(*gain.shape),
+            ],
+            out_specs=[
+                block,
+                block,
+                pl.BlockSpec((1, 2 * NS, rows), lambda b, s: (in_row(b, s), 0, 0)),
+                fixed(NS, width),
+                fixed(1, width),
+            ],
+            scratch_shapes=[pltpu.VMEM((rows, width), jnp.bfloat16)] + work_shapes(rows, width),
+        ),
         out_shape=[
-            jax.ShapeDtypeStruct((CORES * rows, width), jnp.bfloat16),
-            jax.ShapeDtypeStruct((CORES * rows, width), jnp.bfloat16),
-            jax.ShapeDtypeStruct((CORES, 2 * NS, rows), jnp.float32),
+            jax.ShapeDtypeStruct((blocks * rows, width), jnp.bfloat16),
+            jax.ShapeDtypeStruct((blocks * rows, width), jnp.bfloat16),
+            jax.ShapeDtypeStruct((blocks, 2 * NS, rows), jnp.float32),
             jax.ShapeDtypeStruct((NS, width), jnp.float32),
             jax.ShapeDtypeStruct((1, width), jnp.float32),
         ],
-        scratch_shapes=[pltpu.VMEM((rows, width), jnp.bfloat16)] + work_shapes(rows, width),
         compiler_params=params,
         cost_estimate=pl.CostEstimate(flops=4 * 10**9, bytes_accessed=1 << 21, transcendentals=0),
         name="scan_own",
-    )(stream, lows, lows, cols, bias, rates, gain)
+    )(place, stream, lows, lows, cols, bias, rates, gain)
 
 
 def others_kernel(
-    place_ref, stream_ref, steps_ref, maps_ref, rates_ref, gain_ref, out_ref, last_ref, *work_refs
+    place_ref, stream_ref, steps_ref, maps_ref, rates_ref, gain_ref, part_ref, out_ref, last_ref,
+    *work_refs
 ):
+    del part_ref
+
     @pl.when(lax.rem(pl.program_id(0), CORES) == 0)
     def _():
         last_ref[...] = jnp.zeros_like(last_ref)
@@ -594,7 +608,7 @@
     )
 
 
-def scan_others(place, stream, steps, maps, rates, gain):
+def scan_others(place, stream, steps, maps, rates, gain, part):
     others = stream.shape[0]
     chips = others + 1
     rows, width = stream.shape[1] // CORES, stream.shape[2]
@@ -603,10 +617,12 @@
         chip = b // CORES
         return lax.rem(s[0] - jnp.where(chip < s[0], chip, chip + 1) + chips, chips) - 1
 
+    def in_row(b, s):
+        return jnp.where(b // CORES < s[0], b, b + CORES)
+
     def fixed(*shape):
         return pl.BlockSpec(shape, lambda b, s: (0,) * len(shape))
 
-    block = pl.BlockSpec((rows, width), lambda b, s: (b, 0))
     return pl.pallas_call(
         others_kernel,
         grid_spec=pltpu.PrefetchScalarGridSpec(
@@ -614,33 +630,36 @@
             grid=(others * CORES,),
             in_specs=[
                 pl.BlockSpec((1, rows, width), lambda b, s: (slot(b, s), lax.rem(b, CORES), 0)),
-                block,
-                pl.BlockSpec((1, 2 * NS, rows), lambda b, s: (b, 0, 0)),
+                pl.BlockSpec((rows, width), lambda b, s: (b, 0)),
+                pl.BlockSpec((1, 2 * NS, rows), lambda b, s: (in_row(b, s), 0, 0)),
                 fixed(*rates.shape),
                 fixed(*gain.shape),
+                pl.BlockSpec(memory_space=pl.ANY),
             ],
-            out_specs=[block, pl.BlockSpec((1, NS, width), lambda b, s: (b // CORES, 0, 0))],
+            out_specs=[
+                pl.BlockSpec((rows, width), lambda b, s: (in_row(b, s), 0)),
+                pl.BlockSpec((1, NS, width), lambda b, s: (b // CORES, 0, 0)),
+            ],
             scratch_shapes=work_shapes(rows, width),
         ),
         out_shape=[
-            jax.ShapeDtypeStruct((others * CORES * rows, width), jnp.bfloat16),
+            jax.ShapeDtypeStruct(part.shape, part.dtype),
             jax.ShapeDtypeStruct((others, NS, width), jnp.float32),
         ],
+        input_output_aliases={6: 0},
         compiler_params=params,
         cost_estimate=pl.CostEstimate(flops=4 * 10**9, bytes_accessed=1 << 21, transcendentals=0),
         name="scan_others",
-    )(place, stream, steps, maps, rates, gain)
+    )(place, stream, steps, maps, rates, gain, part)
 
 
 def carried_kernel(
-    places_ref, part_own_ref, part_come_ref, sums_own_ref, sums_come_ref,
-    maps_own_ref, maps_come_ref, last_own_ref, last_come_ref, rates_ref, carries_ref,
-    out_ref, state_ref, wide_ref, begin_ref, spread_ref, sums_ref,
+    place_ref, part_ref, sums_ref, maps_ref, last_own_ref, last_come_ref, rates_ref, carries_ref,
+    out_ref, state_ref, wide_ref, begin_ref, spread_ref,
 ):
     block = pl.program_id(0)
     rows, width = out_ref.shape
     chip = block // CORES
-    here = chip == places_ref[0]
 
     @pl.when(block == 0)
     def _():
@@ -650,7 +669,7 @@
             follow(carries_ref.at[row], rates_ref, state_ref)
             return nothing
 
-        lax.fori_loop(0, places_ref[1], compose, 0)
+        lax.fori_loop(0, lax.axis_index("chan"), compose, 0)
         for n in range(NS):
             wide_ref[n * NS : (n + 1) * NS, :] = jnp.broadcast_to(
                 rates_ref[n : n + 1, :], (NS, width)
@@ -658,7 +677,7 @@
 
     @pl.when((block > 0) & (lax.rem(block, CORES) == 0))
     def _():
-        before = jnp.where(chip - 1 == places_ref[0], last_own_ref[...], last_come_ref[0])
+        before = jnp.where(chip - 1 == place_ref[0], last_own_ref[...], last_come_ref[0])
         state_ref[...] = state_ref[...] + before
 
     state = state_ref[...]
@@ -666,15 +685,12 @@
         begin_ref[n * NS : (n + 1) * NS, :] = jnp.broadcast_to(
             state[n : n + 1, :], (NS, width)
         ).astype(jnp.bfloat16)
-    maps = jnp.where(here, maps_own_ref[0], maps_come_ref[0])
-    maps = jnp.concatenate([maps, jnp.zeros((LANES - 2 * NS, rows), jnp.float32)], axis=0).T
+    maps = jnp.concatenate([maps_ref[0], jnp.zeros((LANES - 2 * NS, rows), jnp.float32)], axis=0).T
     for n in range(NS):
         spread_ref[:, n * LANES : (n + 1) * LANES] = jnp.broadcast_to(
             maps[:, NS + n : NS + n + 1], (rows, LANES)
         ).astype(jnp.bfloat16)
-    sums = jnp.where(here, sums_own_ref[...], sums_come_ref[...])
-    sums_ref[...] = sums
-    last = sums[rows - NS :, :].astype(jnp.float32)[NS - 1 :, :]
+    last = sums_ref[rows - NS :, :].astype(jnp.float32)[NS - 1 :, :]
     state_ref[...] = jnp.exp2(rates_ref[...] * last) * state
     chunk, several = CORES * LANES, 4
 
@@ -682,8 +698,7 @@
         near = pl.ds(pl.multiple_of(index * NS, NS), NS)
         for item in range(width // chunk):
             lanes = slice(item * chunk, (item + 1) * chunk)
-            part = jnp.where(here, part_own_ref[near, lanes], part_come_ref[near, lanes])
-            total = part.astype(jnp.float32)
+            total = part_ref[near, lanes].astype(jnp.float32)
             sums = sums_ref[near, lanes]
             for first in range(0, NS, several):
                 terms = []
@@ -700,59 +715,45 @@
     lax.fori_loop(0, rows // NS, some, 0)
 
 
-def add_carried(places, parts, sums, maps, lasts, rates, carries):
-    blocks_come, _, rows = maps[1].shape
-    chips = blocks_come // CORES + 1
+def add_carried(place, part, sums, maps, lasts, rates, carries):
+    blocks, _, rows = maps.shape
+    others = lasts[1].shape[0]
     width = rates.shape[1]
-
-    def core(b):
-        return lax.rem(b, CORES)
-
-    def order(b, s):
-        chip = b // CORES
-        return jnp.minimum(
-            jnp.where(chip < s[0], b, jnp.maximum(b - CORES, 0)), blocks_come - 1
-        )
 
     def before(b, s):
         chip = jnp.maximum(b // CORES - 1, 0)
-        return jnp.minimum(jnp.where(chip < s[0], chip, jnp.maximum(chip - 1, 0)), chips - 2)
+        return jnp.minimum(jnp.where(chip < s[0], chip, jnp.maximum(chip - 1, 0)), others - 1)
 
     def fixed(*shape):
         return pl.BlockSpec(shape, lambda b, s: (0,) * len(shape))
 
-    own = pl.BlockSpec((rows, width), lambda b, s: (core(b), 0))
-    come = pl.BlockSpec((rows, width), lambda b, s: (order(b, s), 0))
+    block = pl.BlockSpec((rows, width), lambda b, s: (b, 0))
     return pl.pallas_call(
         carried_kernel,
         grid_spec=pltpu.PrefetchScalarGridSpec(
             num_scalar_prefetch=1,
-            grid=(chips * CORES,),
+            grid=(blocks,),
             in_specs=[
-                own,
-                come,
-                own,
-                come,
-                pl.BlockSpec((1, 2 * NS, rows), lambda b, s: (core(b), 0, 0)),
-                pl.BlockSpec((1, 2 * NS, rows), lambda b, s: (order(b, s), 0, 0)),
+                block,
+                block,
+                pl.BlockSpec((1, 2 * NS, rows), lambda b, s: (b, 0, 0)),
                 fixed(NS, width),
                 pl.BlockSpec((1, NS, width), lambda b, s: (before(b, s), 0, 0)),
                 fixed(*rates.shape),
                 fixed(*carries.shape),
             ],
-            out_specs=pl.BlockSpec((rows, width), lambda b, s: (b, 0)),
+            out_specs=block,
             scratch_shapes=[
                 pltpu.VMEM((NS, width), jnp.float32),
                 pltpu.VMEM((NS * NS, width), jnp.bfloat16),
                 pltpu.VMEM((NS * NS, width), jnp.bfloat16),
                 pltpu.VMEM((rows, NS * LANES), jnp.bfloat16),
-                pltpu.VMEM((rows, width), jnp.bfloat16),
             ],
         ),
-        out_shape=jax.ShapeDtypeStruct((chips * CORES * rows, width), jnp.bfloat16),
+        out_shape=jax.ShapeDtypeStruct(part.shape, jnp.bfloat16),
         compiler_params=params,
         name="add_carried",
-    )(places, *parts, *sums, *maps, *lasts, rates, carries)
+    )(place, part, sums, maps, *lasts, rates, carries)
 
 
 def local(
@@ -762,7 +763,6 @@
     chips = devices // CORES
     targets = lax.axis_size("chan")
     seq_place = lax.axis_index("seq").astype(jnp.int32)
-    chan_place = lax.axis_index("chan").astype(jnp.int32)
     chip, core = seq_place // CORES, lax.rem(seq_place, CORES)
     place = jnp.stack([chip, core])
     width = queries.shape[2] // devices
@@ -804,17 +804,14 @@
     got_stayed = lax.ppermute(stayed, "seq", swap)
     attn_rows = join_heads(sent, stayed, got_sent, got_stayed)
 
-    part_own, sums_own, maps_own, state, total = scan_own(stayed, low_own, cols, bias, rates, gain)
+    part, sums, maps, state, total = scan_own(place, stayed, low_own, cols, bias, rates, gain)
     come, low_come = jnp.stack(come), jnp.stack(low_come)
-    steps, sums_come, maps_come, carry = step_sizes(
-        place, come, low_come, cols, bias, rates, state, total, targets, attn_rows
+    steps, sums, maps, carry = step_sizes(
+        place, come, low_come, cols, bias, rates, state, total, targets, attn_rows, sums, maps
     )
     carries = lax.all_to_all(carry, "chan", split_axis=0, concat_axis=0, tiled=True)
-    part_come, last_come = scan_others(place, come, steps, maps_come, rates, gain)
-    ssm_rows = add_carried(
-        jnp.stack([chip, chan_place]), (part_own, part_come), (sums_own, sums_come),
-        (maps_own, maps_come), (state, last_come), rates, carries,
-    )
+    part, last_come = scan_others(place, come, steps, maps, rates, gain, part)
+    ssm_rows = add_carried(place, part, sums, maps, (state, last_come), rates, carries)
     return (attn_rows[None], ssm_rows[None])
 
 

time: 81.8 us -> 81.2 us (level)
  transfers between devices with their start and end apart: 10 -> 10, of which waited for: 3 -> 3; matrix products, arithmetic and copies ran while one was open for 8% -> 7% of each run, Pallas kernels for 25% -> 26%
where the time goes in v3:
time: 81.2 us; the launch traced here: 80.6 us
  Pallas kernels  47 us (58%)
  starting transfers between devices  17.6 us (22%)
  local copies, waits for them, and re-layouts  7.39 us (9%)
  waiting for transfers between devices  5.78 us (7%)
  other arithmetic  2.08 us (3%)
    pallas_call x1, Pallas kernels, add_carried(): pl.pallas_call(carried_kernel, grid_spec=pltpu.PrefetchScalarGridSpec(num...  9.17 us
    pallas_call x1, Pallas kernels, scan_own(): pl.pallas_call(own_kernel, grid_spec=pltpu.PrefetchScalarGridSpec(num_sca...  9.14 us
    pallas_call x1, Pallas kernels, attend(): pl.pallas_call(functools.partial(attend_kernel, chips=chips), grid_spec=p...  8.07 us
    pallas_call x1, Pallas kernels, scan_others(): pl.pallas_call(others_kernel, grid_spec=pltpu.PrefetchScalarGridSpec(num_...  8.01 us
    pallas_call x1, Pallas kernels, step_sizes(): pl.pallas_call(step_kernel, grid_spec=pltpu.PrefetchScalarGridSpec(num_sc...  6.6 us
    all_to_all x1, starting transfers between devices, local(): lax.all_to_all(carry, 'chan', split_axis=0, concat_axis=0, tiled=True)  5.82 us
    ppermute x1, starting transfers between devices, local(): from_far = lax.ppermute(theirs, 'seq', far)  4.54 us
    ppermute x1, waiting for transfers between devices, local(): from_near = lax.ppermute(own, 'seq', near)  4.04 us
  transfers between devices with their start and end apart: 10, of which 3 were waited for; matrix products, arithmetic and copies ran while one was open for 7% of the time, Pallas kernels for 26%

profile of v3, /device:TPU:0, one launch (start us, length us, event | category | flops | bytes accessed | tf_op | source)
XLA Modules:
  0.0 80.6 jit_solution(16566394382608309581)
XLA Ops:
  0.6 0.0 copy-start
  0.6 2.1 %select_heads.1 = (bf16[2,2,128,256]{3,2,1,0:T(8,128)(2,1)}, bf16[2,2,128,256]{3,2,1,0:T(8,128)(2,1)}) custom-call(bf16[128,1024]{1,0:T(8,128)(2,1)} %bitcast.22, bf16[128,1024]{1,0:T(8,128)(2,1)} %bitcast.23), custom_call_target="tpu_custom_call" | custom-call | tf_op jit(solution)/shard_map/select_heads/pallas_call | solution.py:61
  2.7 0.5 collective-permute-start
  3.3 4.5 %collective-permute-start.3 = (bf16[2,2,128,256]{3,2,1,0:T(8,128)(2,1)}, bf16[2,2,128,256]{3,2,1,0:T(8,128)(2,1)S(1)}, u32[]{:S(2)}, u32[]{:S(2)}) collective-permute-start(bf16[2,2,128,256]{3,2,1,0:T(8,128)(2,1)} %get-tuple-element.21), channel_id=1, source_target_pairs={{0,24},{8,16},{1,25},{9,17},{2,26},{10,18},{3,27},{11,19},{4,28},{... | collective-permute-start | bytes 786440 | tf_op jit(solution)/shard_map/ppermute | solution.py:783
  7.8 0.1 collective-permute-start.1
  7.9 2.3 %collective-permute-start.2 = (bf16[2,2,128,256]{3,2,1,0:T(8,128)(2,1)}, bf16[2,2,128,256]{3,2,1,0:T(8,128)(2,1)}, u32[]{:S(2)}, u32[]{:S(2)}) collective-permute-start(bf16[2,2,128,256]{3,2,1,0:T(8,128)(2,1)} %get-tuple-element.19.own_ref), channel_id=1, source_target_pairs={{0,16},{8,24},{1,17},{9,25},{2,18},{10,26},{3,19},{11,27},{4,20},{... | collective-permute-start | bytes 786440 | tf_op jit(solution)/shard_map/ppermute | solution.py:782
  10.2 0.6 pad_add_fusion.place_ref
  10.8 1.3 %dynamic_slice.14 = f32[1024]{0:T(1024)} dynamic-slice(f32[4096]{0:T(1024)} %param.17, s32[]{:T(128)S(6)} %select_n.12), dynamic_slice_sizes={1024} | dynamic-slice | bytes 8196 | tf_op jit(solution)/shard_map/dynamic_slice | solution.py:793
  12.1 1.3 %dynamic_slice.15 = f32[1024]{0:T(1024)} dynamic-slice(f32[4096]{0:T(1024)} %param.19, s32[]{:T(128)S(6)} %select_n.12), dynamic_slice_sizes={1024} | dynamic-slice | bytes 8196 | tf_op jit(solution)/shard_map/dynamic_slice | solution.py:794
  13.4 1.5 %multiply_bitcast_fusion.rest_0_.rates_ref = f32[16,1024]{1,0:T(8,128)} fusion(f32[4096,16]{0,1:T(8,128)} %param.18, s32[]{:T(128)S(6)} %select_n.12), kind=kLoop, calls=%fused_computation | loop fusion | flops 16384 | bytes 131076 | tf_op jit(solution)/shard_map/transpose | solution.py:791
  14.8 0.0 copy-done
  14.9 0.8 %constant_dynamic-slice_fusion.rest_1_.cols_ref = bf16[256,1024]{1,0:T(8,128)(2,1)} fusion(bf16[256,4096]{1,0:T(8,128)(2,1)S(1)} %copy-done, s32[]{:T(128)S(6)} %select_n.12), kind=kLoop, calls=%fused_computation.2 | loop fusion | bytes 1048580 | tf_op jit(solution)/shard_map/dynamic_slice | solution.py:792
  15.7 0.0 collective-permute-done.3.far_ref
  15.7 0.0 copy-start.7
  15.7 0.0 collective-permute-done.1.swap_ref
  15.7 4.0 %collective-permute-done.2.near_ref = bf16[2,2,128,256]{3,2,1,0:T(8,128)(2,1)} collective-permute-done((bf16[2,2,128,256]{3,2,1,0:T(8,128)(2,1)}, bf16[2,2,128,256]{3,2,1,0:T(8,128)(2,1)}, u32[]{:S(2)}, u32[]{:S(2)}) %collective-permute-start.2) | collective-permute-done | bytes 262176 | tf_op jit(solution)/shard_map/ppermute | solution.py:782
  19.7 0.0 collective-permute-done.theirs_ref
  19.7 0.0 copy-start.6
  19.7 0.0 copy-done.7
  19.7 1.0 %copy-done.6 = bf16[128,4096]{1,0:T(8,128)(2,1)} copy-done((bf16[128,4096]{1,0:T(8,128)(2,1)}, bf16[128,4096]{1,0:T(8,128)(2,1)S(1)}, u32[]{:S(2)}) %copy-start.6) | copy-done | bytes 1048600
  20.7 8.1 %attend.1 = (bf16[1,256,1024]{2,1,0:T(8,128)(2,1)}, bf16[1,256,1024]{2,1,0:T(8,128)(2,1)}, f32[288,256]{1,0:T(8,128)}) custom-call(s32[2]{0:T(128)} %pad_add_fusion.place_ref, s32[1,16]{1,0:T(1,128)} %doc_ref.1, bf16[128,4096]{1,0:T(8,128)(2,1)} %bitcast.31, bf16[128,4096]{1,0:T(8,128)(2,1)} %copy-done.6, ...), custom_call_target="tpu_custom_call" | custom-call | flops 5000000000 | bytes 4194304 | tf_op jit(solution)/shard_map/attend/pallas_call | solution.py:235
  28.8 0.1 collective-permute-start.7
  28.9 0.5 collective-permute-start.4
  29.4 0.1 collective-permute-start.5
  29.4 2.5 %collective-permute-start.6 = (bf16[256,1024]{1,0:T(8,128)(2,1)}, bf16[256,1024]{1,0:T(8,128)(2,1)S(1)}, u32[]{:S(2)}, u32[]{:S(2)}) collective-permute-start(bf16[256,1024]{1,0:T(8,128)(2,1)} %bitcast.21), channel_id=1, source_target_pairs={{0,16},{8,24},{16,0},{24,8},{1,17},{9,25},{17,1},{25,9},{2,18},{10... | collective-permute-start | bytes 1572872 | tf_op jit(solution)/shard_map/ppermute | solution.py:800
  31.9 0.0 collective-permute-done.7.theirs_ref
  31.9 0.0 copy-start.5
  31.9 0.7 copy-done.5
  32.6 1.7 %low_and_maps.1.low_ref.map_ref = bf16[288,256]{1,0:T(8,128)(2,1)} custom-call(f32[288,256]{1,0:T(8,128)} %get-tuple-element.24.mine_ref, f32[288,256]{1,0:T(8,128)} %copy-done.5), custom_call_target="tpu_custom_call" | custom-call | flops 1 | bytes 1 | tf_op jit(solution)/shard_map/low_and_maps/pallas_call | solution.py:273
  34.4 1.2 %collective-permute-start.8 = (bf16[288,256]{1,0:T(8,128)(2,1)}, bf16[288,256]{1,0:T(8,128)(2,1)S(1)}, u32[]{:S(2)}, u32[]{:S(2)}) collective-permute-start(bf16[288,256]{1,0:T(8,128)(2,1)} %low_and_maps.1.low_ref.map_ref), channel_id=1, source_target_pairs={{0,16},{8,24},{16,0},{24,8},{1,17},{9,25},{17,1},{25,9},{2,18},{10... | collective-permute-start | bytes 442376 | tf_op jit(solution)/shard_map/ppermute | solution.py:802
  35.6 9.1 %scan_own.1 = (bf16[512,1024]{1,0:T(8,128)(2,1)}, bf16[512,1024]{1,0:T(8,128)(2,1)}, f32[4,32,128]{2,1,0:T(8,128)}, f32[16,1024]{1,0:T(8,128)}, f32[1,1024]{1,0:T(1,128)}) custom-call(s32[2]{0:T(128)} %pad_add_fusion.place_ref, bf16[1,256,1024]{2,1,0:T(8,128)(2,1)} %get-tuple-element.23.stayed_ref.stream_ref, bf16[288,256]{1,0:T(8,128)(2,1)} %low_and_maps.1.low_ref.map_ref, ...), custom_call_target="tpu_custom_call" | custom-call | flops 4000000000 | bytes 2097152 | tf_op jit(solution)/shard_map/scan_own/pallas_call | solution.py:560
  44.7 0.0 collective-permute-done.4.got_sent_ref
  44.7 0.0 copy-start.4
  44.7 0.0 collective-permute-done.5.got_stayed_ref
  44.7 0.8 copy-done.4
  45.5 2.2 %join_heads.1.rest_2_ = bf16[128,4096]{1,0:T(8,128)(2,1)} custom-call(bf16[1,256,1024]{2,1,0:T(8,128)(2,1)} %get-tuple-element.22.sent_ref, bf16[1,256,1024]{2,1,0:T(8,128)(2,1)} %get-tuple-element.23.stayed_ref.stream_ref, bf16[1,256,1024]{2,1,0:T(8,128)(2,1)} %copy-done.4, bf16[1,256,1024]{2,1,0:T(8,128)(2,1)} %collective-permute-done.5.got_stayed_ref), custom_call_target="tpu_custom_call" | custom-call | tf_op jit(solution)/shard_map/join_heads/pallas_call | solution.py:90
  47.7 0.1 collective-permute-done.8
  47.8 0.0 copy-start.2
  47.8 0.0 collective-permute-done.6
  47.8 0.0 copy-start.3
  47.8 0.7 copy-done.2
  48.5 0.2 copy-done.3
  48.7 6.6 %step_sizes.1 = (bf16[256,1024]{1,0:T(8,128)(2,1)}, bf16[512,1024]{1,0:T(8,128)(2,1)}, f32[4,32,128]{2,1,0:T(8,128)}, bf16[8,144,128]{2,1,0:T(8,128)(2,1)}) custom-call(s32[2]{0:T(128)} %pad_add_fusion.place_ref, bf16[1,256,1024]{2,1,0:T(8,128)(2,1)} %bitcast.19, bf16[1,288,256]{2,1,0:T(8,128)(2,1)} %bitcast.17, ...), custom_call_target="tpu_custom_call", output_to_operand_aliasing={{1}: (10, {}), {2}: (11, {})} | custom-call | tf_op jit(solution)/shard_map/step_sizes/pallas_call | solution.py:400
  55.3 5.8 %all-to-all-start = ((bf16[8,144,128]{2,1,0:T(8,128)(2,1)}), bf16[8,144,128]{2,1,0:T(8,128)(2,1)S(1)}, u32[]{:S(2)}, u32[]{:S(2)}) async-start(bf16[8,144,128]{2,1,0:T(8,128)(2,1)} %get-tuple-element.35), calls=%async_computation | async-start | bytes 589824 | tf_op jit(solution)/shard_map/all_to_all | solution.py:812
  61.1 8.0 %scan_others.1 = (bf16[512,1024]{1,0:T(8,128)(2,1)}, f32[1,16,1024]{2,1,0:T(8,128)}) custom-call(s32[2]{0:T(128)} %pad_add_fusion.place_ref, bf16[1,256,1024]{2,1,0:T(8,128)(2,1)} %bitcast.20, bf16[256,1024]{1,0:T(8,128)(2,1)} %get-tuple-element.29.steps_ref, f32[4,32,128]{2,1,0:T(8,128)} %get-tuple-element.30.maps_ref, ...), custom_call_target="tpu_custom_call", output_to_operand_aliasing={{0}: (6, {})} | custom-call | flops 4000000000 | bytes 2097152 | tf_op jit(solution)/shard_map/scan_others/pallas_call | solution.py:626
  69.1 1.6 %all-to-all-done.carries_ref = bf16[8,144,128]{2,1,0:T(8,128)(2,1)S(1)} async-done(((bf16[8,144,128]{2,1,0:T(8,128)(2,1)}), bf16[8,144,128]{2,1,0:T(8,128)(2,1)S(1)}, u32[]{:S(2)}, u32[]{:S(2)}) %all-to-all-start) | async-done | bytes 294944 | tf_op jit(solution)/shard_map/all_to_all | solution.py:812
  70.7 0.7 copy-done.1
  71.4 9.2 %add_carried.1 = bf16[512,1024]{1,0:T(8,128)(2,1)} custom-call(s32[2]{0:T(128)} %pad_add_fusion.place_ref, bf16[512,1024]{1,0:T(8,128)(2,1)} %get-tuple-element.32.part_ref, bf16[512,1024]{1,0:T(8,128)(2,1)} %get-tuple-element.33.sums_ref, f32[4,32,128]{2,1,0:T(8,128)} %get-tuple-element.30.maps_ref, f32[16,1024]{1,0:T(8,128)} %get-tuple-element.25.rest_0_.last_own_ref, ...), custom_call_target="tpu_custom_call" | custom-call | tf_op jit(solution)/shard_map/add_carried/pallas_call | solution.py:731
  (1 shorter events, 0.0 us)
Async XLA Ops:
  0.6 14.2 %copy-start = (bf16[256,4096]{1,0:T(8,128)(2,1)S(1)}, bf16[256,4096]{1,0:T(8,128)(2,1)}, u32[]{:S(2)}) copy-start(bf16[256,4096]{1,0:T(8,128)(2,1)} %param.16) | copy-start | bytes 6291460
  2.7 17.0 %collective-permute-start = (bf16[128,4096]{1,0:T(8,128)(2,1)}, bf16[128,4096]{1,0:T(8,128)(2,1)S(1)}, u32[]{:S(2)}, u32[]{:S(2)}) collective-permute-start(bf16[128,4096]{1,0:T(8,128)(2,1)} %bitcast.30), channel_id=1, source_target_pairs={{0,8},{8,0},{16,24},{24,16},{1,9},{9,1},{17,25},{25,17},{2,10},{10... | collective-permute-start | bytes 3145736 | tf_op jit(solution)/shard_map/ppermute | solution.py:786
  3.3 12.4 %collective-permute-start.3 = (bf16[2,2,128,256]{3,2,1,0:T(8,128)(2,1)}, bf16[2,2,128,256]{3,2,1,0:T(8,128)(2,1)S(1)}, u32[]{:S(2)}, u32[]{:S(2)}) collective-permute-start(bf16[2,2,128,256]{3,2,1,0:T(8,128)(2,1)} %get-tuple-element.21), channel_id=1, source_target_pairs={{0,24},{8,16},{1,25},{9,17},{2,26},{10,18},{3,27},{11,19},{4,28},{... | collective-permute-start | bytes 786440 | tf_op jit(solution)/shard_map/ppermute | solution.py:783
  7.8 7.9 %collective-permute-start.1 = (bf16[2,2,128,256]{3,2,1,0:T(8,128)(2,1)}, bf16[2,2,128,256]{3,2,1,0:T(8,128)(2,1)}, u32[]{:S(2)}, u32[]{:S(2)}) collective-permute-start(bf16[2,2,128,256]{3,2,1,0:T(8,128)(2,1)} %get-tuple-element.21), channel_id=1, source_target_pairs={{0,8},{8,0},{16,24},{24,16},{1,9},{9,1},{17,25},{25,17},{2,10},{10... | collective-permute-start | bytes 786440 | tf_op jit(solution)/shard_map/ppermute | solution.py:784
  7.9 11.8 %collective-permute-start.2 = (bf16[2,2,128,256]{3,2,1,0:T(8,128)(2,1)}, bf16[2,2,128,256]{3,2,1,0:T(8,128)(2,1)}, u32[]{:S(2)}, u32[]{:S(2)}) collective-permute-start(bf16[2,2,128,256]{3,2,1,0:T(8,128)(2,1)} %get-tuple-element.19.own_ref), channel_id=1, source_target_pairs={{0,16},{8,24},{1,17},{9,25},{2,18},{10,26},{3,19},{11,27},{4,20},{... | collective-permute-start | bytes 786440 | tf_op jit(solution)/shard_map/ppermute | solution.py:782
  15.7 4.1 %copy-start.7 = (bf16[2,2,128,256]{3,2,1,0:T(8,128)(2,1)}, bf16[2,2,128,256]{3,2,1,0:T(8,128)(2,1)S(1)}, u32[]{:S(2)}) copy-start(bf16[2,2,128,256]{3,2,1,0:T(8,128)(2,1)S(1)} %collective-permute-done.3.far_ref) | copy-start | bytes 786436
  19.7 1.0 %copy-start.6 = (bf16[128,4096]{1,0:T(8,128)(2,1)}, bf16[128,4096]{1,0:T(8,128)(2,1)S(1)}, u32[]{:S(2)}) copy-start(bf16[128,4096]{1,0:T(8,128)(2,1)S(1)} %collective-permute-done.theirs_ref) | copy-start | bytes 3145732
  28.8 3.1 %collective-permute-start.7 = (f32[288,256]{1,0:T(8,128)}, f32[288,256]{1,0:T(8,128)S(1)}, u32[]{:S(2)}, u32[]{:S(2)}) collective-permute-start(f32[288,256]{1,0:T(8,128)} %get-tuple-element.24.mine_ref), channel_id=1, source_target_pairs={{0,8},{8,0},{16,24},{24,16},{1,9},{9,1},{17,25},{25,17},{2,10},{10... | collective-permute-start | bytes 884744 | tf_op jit(solution)/shard_map/ppermute | solution.py:801
  28.9 15.9 %collective-permute-start.4 = (bf16[1,256,1024]{2,1,0:T(8,128)(2,1)}, bf16[1,256,1024]{2,1,0:T(8,128)(2,1)S(1)}, u32[]{:S(2)}, u32[]{:S(2)}) collective-permute-start(bf16[1,256,1024]{2,1,0:T(8,128)(2,1)} %get-tuple-element.22.sent_ref), channel_id=1, source_target_pairs={{0,8},{8,0},{16,24},{24,16},{1,9},{9,1},{17,25},{25,17},{2,10},{10... | collective-permute-start | bytes 1572872 | tf_op jit(solution)/shard_map/ppermute | solution.py:803
  29.4 15.4 %collective-permute-start.5 = (bf16[1,256,1024]{2,1,0:T(8,128)(2,1)}, bf16[1,256,1024]{2,1,0:T(8,128)(2,1)}, u32[]{:S(2)}, u32[]{:S(2)}) collective-permute-start(bf16[1,256,1024]{2,1,0:T(8,128)(2,1)} %get-tuple-element.23.stayed_ref.stream_ref), channel_id=1, source_target_pairs={{0,8},{8,0},{16,24},{24,16},{1,9},{9,1},{17,25},{25,17},{2,10},{10... | collective-permute-start | bytes 1572872 | tf_op jit(solution)/shard_map/ppermute | solution.py:804
  29.4 18.4 %collective-permute-start.6 = (bf16[256,1024]{1,0:T(8,128)(2,1)}, bf16[256,1024]{1,0:T(8,128)(2,1)S(1)}, u32[]{:S(2)}, u32[]{:S(2)}) collective-permute-start(bf16[256,1024]{1,0:T(8,128)(2,1)} %bitcast.21), channel_id=1, source_target_pairs={{0,16},{8,24},{16,0},{24,8},{1,17},{9,25},{17,1},{25,9},{2,18},{10... | collective-permute-start | bytes 1572872 | tf_op jit(solution)/shard_map/ppermute | solution.py:800
  31.9 0.7 copy-start.5
  34.4 13.4 %collective-permute-start.8 = (bf16[288,256]{1,0:T(8,128)(2,1)}, bf16[288,256]{1,0:T(8,128)(2,1)S(1)}, u32[]{:S(2)}, u32[]{:S(2)}) collective-permute-start(bf16[288,256]{1,0:T(8,128)(2,1)} %low_and_maps.1.low_ref.map_ref), channel_id=1, source_target_pairs={{0,16},{8,24},{16,0},{24,8},{1,17},{9,25},{17,1},{25,9},{2,18},{10... | collective-permute-start | bytes 442376 | tf_op jit(solution)/shard_map/ppermute | solution.py:802
  44.7 0.8 copy-start.4
  47.8 0.7 copy-start.2
  47.8 0.8 %copy-start.3 = (bf16[256,1024]{1,0:T(8,128)(2,1)}, bf16[256,1024]{1,0:T(8,128)(2,1)S(1)}, u32[]{:S(2)}) copy-start(bf16[256,1024]{1,0:T(8,128)(2,1)S(1)} %collective-permute-done.6) | copy-start | bytes 1572868
  55.3 15.5 %all-to-all-start = ((bf16[8,144,128]{2,1,0:T(8,128)(2,1)}), bf16[8,144,128]{2,1,0:T(8,128)(2,1)S(1)}, u32[]{:S(2)}, u32[]{:S(2)}) async-start(bf16[8,144,128]{2,1,0:T(8,128)(2,1)} %get-tuple-element.35), calls=%async_computation | async-start | bytes 589824 | tf_op jit(solution)/shard_map/all_to_all | solution.py:812
  70.7 0.7 copy-start.1

commit v4 on v3

--- a/solution.py
+++ b/solution.py
@@ -43,26 +43,40 @@
     return ref.at[:, pl.ds(pl.multiple_of(index * size, LANES), size)]
 
 
-def heads_kernel(key_ref, value_ref, own_ref, their_ref, sems):
+def heads_kernel(key_ref, value_ref, own_ref, their_ref, own_held, their_held, in_sems, out_sems):
     core = lax.rem(lax.axis_index("seq"), CORES)
     wide = own_ref.shape[3]
     halves = key_ref.shape[1] // wide // own_ref.shape[0]
-    pairs = []
-    for target, which in ((own_ref, core), (their_ref, 1 - core)):
+    arriving, leaving = [], []
+    for target, held, which in ((own_ref, own_held, core), (their_ref, their_held, 1 - core)):
         for chip in range(own_ref.shape[0]):
             index = chip * halves + (which if halves == CORES else 0)
             for kind, source in enumerate((key_ref, value_ref)):
-                pairs.append((columns_of(source, index, wide), target.at[chip, kind]))
-    run_copies(pairs, sems)
+                at, place = len(arriving), held.at[chip, kind]
+                arriving.append(
+                    pltpu.make_async_copy(columns_of(source, index, wide), place, in_sems.at[at])
+                )
+                leaving.append(
+                    pltpu.make_async_copy(place, target.at[chip, kind], out_sems.at[at])
+                )
+    for copy in arriving:
+        copy.start()
+    for copy, onward in zip(arriving, leaving):
+        copy.wait()
+        onward.start()
+    for onward in leaving:
+        onward.wait()
 
 
 def select_heads(keys, values, chips, wide):
-    shape = jax.ShapeDtypeStruct((chips, 2, keys.shape[0], wide), keys.dtype)
+    shape = (chips, 2, keys.shape[0], wide)
     return pl.pallas_call(
         heads_kernel,
         in_specs=[pl.BlockSpec(memory_space=pl.ANY)] * 2,
-        out_shape=[shape, shape],
-        scratch_shapes=[pltpu.SemaphoreType.DMA((4 * chips,))],
+        out_specs=[pl.BlockSpec(memory_space=pl.ANY)] * 2,
+        out_shape=[jax.ShapeDtypeStruct(shape, keys.dtype)] * 2,
+        scratch_shapes=[pltpu.VMEM(shape, keys.dtype)] * 2
+        + [pltpu.SemaphoreType.DMA((4 * chips,))] * 2,
         compiler_params=params,
         name="select_heads",
     )(keys, values)
@@ -143,50 +157,64 @@
             )
 
     scale = LOG2E / math.sqrt(HEAD_SIZE)
-    ones = jnp.ones((3 * rows, HEAD_SIZE), jnp.bfloat16)
-
-    def windows(kind):
-        own, swapped = own_ref[0, kind], swap_ref[0, kind]
-        near, far = near_ref[0, kind], far_ref[0, kind]
-        return (
-            jnp.concatenate([near, own, jnp.where(first_core, far, swapped)], axis=0),
-            jnp.concatenate([far, swapped, jnp.where(first_core, own, near)], axis=0),
-        )
-
-    scores = []
-    for keys, query in zip(windows(0), (mine_ref[...], theirs_ref[...])):
-        stacked = jnp.concatenate(
-            [query[:, i * HEAD_SIZE : (i + 1) * HEAD_SIZE] for i in range(group)], axis=0
-        )
-        scores.append(
-            lax.dot_general(
-                stacked, keys, (((1,), (1,)), ((), ())), preferred_element_type=jnp.float32
-            )
-        )
-    outputs = []
-    before = above((group * rows, rows))
-    for item, (values, score) in enumerate(zip(windows(1), scores)):
+    ones = jnp.ones((4 * rows, HEAD_SIZE), jnp.bfloat16)
+
+    def all_blocks(kind):
+        refs = (near_ref, far_ref, own_ref, swap_ref)
+        return jnp.concatenate([ref[0, kind] for ref in refs], axis=0)
+
+    stacked = jnp.concatenate(
+        [
+            query_ref[:, i * HEAD_SIZE : (i + 1) * HEAD_SIZE]
+            for query_ref in (mine_ref, theirs_ref)
+            for i in range(group)
+        ],
+        axis=0,
+    )
+    scores = lax.dot_general(
+        stacked, all_blocks(0), (((1,), (1,)), ((), ())), preferred_element_type=jnp.float32
+    )
+    shape = (group * rows, rows)
+    before = above(shape)
+    none = jnp.zeros(shape, jnp.bfloat16)
+    spreads = []
+    for item in range(CORES):
+        score = scores[item * group * rows : (item + 1) * group * rows, :]
+        near, far, own, swapped = (score[:, i * rows : (i + 1) * rows] for i in range(4))
+        if item == 0:
+            ends, middle = jnp.where(before, near, own), jnp.where(first_core, far, swapped)
+        else:
+            ends, middle = jnp.where(before, far, swapped), jnp.where(first_core, own, near)
         fill = mask_ref[item]
-        ends = jnp.where(before, score[:, :rows], score[:, rows : 2 * rows])
-        kept = jnp.concatenate([ends, score[:, 2 * rows :]], axis=1)
+        kept = jnp.concatenate([ends, middle], axis=1)
         kept = jnp.concatenate(
             [kept[i * rows : (i + 1) * rows, :] + fill for i in range(group)], axis=0
         )
         peak = jnp.max(kept, axis=1, keepdims=True)
         raw = jnp.exp2((kept - peak) * scale).astype(jnp.bfloat16)
-        ends = raw[:, :rows]
-        none = jnp.zeros_like(ends)
-        spread = jnp.concatenate(
-            [jnp.where(before, ends, none), jnp.where(before, none, ends), raw[:, rows:]], axis=1
+        ends, middle = raw[:, :rows], raw[:, rows:]
+        old, new = jnp.where(before, ends, none), jnp.where(before, none, ends)
+        if_first = jnp.where(first_core, middle, none)
+        if_second = jnp.where(first_core, none, middle)
+        spreads.append(
+            jnp.concatenate(
+                [old, if_first, new, if_second] if item == 0 else [if_second, old, if_first, new],
+                axis=1,
+            )
         )
-        both = jnp.dot(
-            spread, jnp.concatenate([values, ones], axis=1), preferred_element_type=jnp.float32
+    both = jnp.dot(
+        jnp.concatenate(spreads, axis=0),
+        jnp.concatenate([all_blocks(1), ones], axis=1),
+        preferred_element_type=jnp.float32,
+    )
+    mixed = (both[:, :HEAD_SIZE] * pl.reciprocal(both[:, HEAD_SIZE:])).astype(jnp.bfloat16)
+    outputs = [
+        jnp.concatenate(
+            [mixed[(item * group + i) * rows : (item * group + i + 1) * rows, :] for i in range(group)],
+            axis=1,
         )
-        mixed = both[:, :HEAD_SIZE] * pl.reciprocal(both[:, HEAD_SIZE:])
-        mixed = mixed.astype(jnp.bfloat16)
-        outputs.append(
-            jnp.concatenate([mixed[i * rows : (i + 1) * rows, :] for i in range(group)], axis=1)
-        )
+        for item in range(CORES)
+    ]
     stream = jnp.concatenate(
         [
             jnp.where(first_core, outputs[0], outputs[1]),

time: 81.2 us -> 82.2 us (1.012)
  Pallas kernels: 47 us -> 48 us
    pallas_call x1, Pallas kernels: 8.07 us -> 9.18 us  [attend(): pl.pallas_call(functools.partial(attend_kernel, chips=chips), grid_spec=p...]
where the time goes in v4:
time: 82.2 us; the launch traced here: 81.6 us
  Pallas kernels  48 us (58%)
  starting transfers between devices  17.6 us (21%)
  local copies, waits for them, and re-layouts  7.39 us (9%)
  waiting for transfers between devices  5.78 us (7%)
  other arithmetic  2.08 us (3%)
    pallas_call x1, Pallas kernels, attend(): pl.pallas_call(functools.partial(attend_kernel, chips=chips), grid_spec=p...  9.18 us
    pallas_call x1, Pallas kernels, add_carried(): pl.pallas_call(carried_kernel, grid_spec=pltpu.PrefetchScalarGridSpec(num...  9.17 us
    pallas_call x1, Pallas kernels, scan_own(): pl.pallas_call(own_kernel, grid_spec=pltpu.PrefetchScalarGridSpec(num_sca...  9.14 us
    pallas_call x1, Pallas kernels, scan_others(): pl.pallas_call(others_kernel, grid_spec=pltpu.PrefetchScalarGridSpec(num_...  8.01 us
    pallas_call x1, Pallas kernels, step_sizes(): pl.pallas_call(step_kernel, grid_spec=pltpu.PrefetchScalarGridSpec(num_sc...  6.6 us
    all_to_all x1, starting transfers between devices, local(): lax.all_to_all(carry, 'chan', split_axis=0, concat_axis=0, tiled=True)  5.82 us
    ppermute x1, starting transfers between devices, local(): from_far = lax.ppermute(theirs, 'seq', far)  4.54 us
    ppermute x1, waiting for transfers between devices, local(): from_near = lax.ppermute(own, 'seq', near)  4.04 us
  transfers between devices with their start and end apart: 10, of which 3 were waited for; matrix products, arithmetic and copies ran while one was open for 7% of the time, Pallas kernels for 26%

profile of v4, /device:TPU:0, one launch (start us, length us, event | category | flops | bytes accessed | tf_op | source)
XLA Modules:
  0.0 81.6 jit_solution(6599583716712134105)
XLA Ops:
  0.6 0.0 copy-start
  0.6 2.0 %select_heads.1 = (bf16[2,2,128,256]{3,2,1,0:T(8,128)(2,1)}, bf16[2,2,128,256]{3,2,1,0:T(8,128)(2,1)}) custom-call(bf16[128,1024]{1,0:T(8,128)(2,1)} %bitcast.22, bf16[128,1024]{1,0:T(8,128)(2,1)} %bitcast.23), custom_call_target="tpu_custom_call" | custom-call | tf_op jit(solution)/shard_map/select_heads/pallas_call | solution.py:73
  2.6 0.5 collective-permute-start
  3.2 4.5 %collective-permute-start.3 = (bf16[2,2,128,256]{3,2,1,0:T(8,128)(2,1)}, bf16[2,2,128,256]{3,2,1,0:T(8,128)(2,1)S(1)}, u32[]{:S(2)}, u32[]{:S(2)}) collective-permute-start(bf16[2,2,128,256]{3,2,1,0:T(8,128)(2,1)} %get-tuple-element.21), channel_id=1, source_target_pairs={{0,24},{8,16},{1,25},{9,17},{2,26},{10,18},{3,27},{11,19},{4,28},{... | collective-permute-start | bytes 786440 | tf_op jit(solution)/shard_map/ppermute | solution.py:811
  7.7 0.1 collective-permute-start.1
  7.8 2.3 %collective-permute-start.2 = (bf16[2,2,128,256]{3,2,1,0:T(8,128)(2,1)}, bf16[2,2,128,256]{3,2,1,0:T(8,128)(2,1)}, u32[]{:S(2)}, u32[]{:S(2)}) collective-permute-start(bf16[2,2,128,256]{3,2,1,0:T(8,128)(2,1)} %get-tuple-element.19.own_ref), channel_id=1, source_target_pairs={{0,16},{8,24},{1,17},{9,25},{2,18},{10,26},{3,19},{11,27},{4,20},{... | collective-permute-start | bytes 786440 | tf_op jit(solution)/shard_map/ppermute | solution.py:810
  10.1 0.6 pad_add_fusion.place_ref
  10.7 1.3 %dynamic_slice.14 = f32[1024]{0:T(1024)} dynamic-slice(f32[4096]{0:T(1024)} %param.17, s32[]{:T(128)S(6)} %select_n.12), dynamic_slice_sizes={1024} | dynamic-slice | bytes 8196 | tf_op jit(solution)/shard_map/dynamic_slice | solution.py:821
  12.0 1.3 %dynamic_slice.15 = f32[1024]{0:T(1024)} dynamic-slice(f32[4096]{0:T(1024)} %param.19, s32[]{:T(128)S(6)} %select_n.12), dynamic_slice_sizes={1024} | dynamic-slice | bytes 8196 | tf_op jit(solution)/shard_map/dynamic_slice | solution.py:822
  13.3 1.5 %multiply_bitcast_fusion.rest_0_.rates_ref = f32[16,1024]{1,0:T(8,128)} fusion(f32[4096,16]{0,1:T(8,128)} %param.18, s32[]{:T(128)S(6)} %select_n.12), kind=kLoop, calls=%fused_computation | loop fusion | flops 16384 | bytes 131076 | tf_op jit(solution)/shard_map/transpose | solution.py:819
  14.8 0.0 copy-done
  14.8 0.8 %constant_dynamic-slice_fusion.rest_1_.cols_ref = bf16[256,1024]{1,0:T(8,128)(2,1)} fusion(bf16[256,4096]{1,0:T(8,128)(2,1)S(1)} %copy-done, s32[]{:T(128)S(6)} %select_n.12), kind=kLoop, calls=%fused_computation.2 | loop fusion | bytes 1048580 | tf_op jit(solution)/shard_map/dynamic_slice | solution.py:820
  15.6 0.0 collective-permute-done.3.far_ref
  15.6 0.0 copy-start.7
  15.6 0.0 collective-permute-done.1.swap_ref
  15.6 4.0 %collective-permute-done.2.near_ref = bf16[2,2,128,256]{3,2,1,0:T(8,128)(2,1)} collective-permute-done((bf16[2,2,128,256]{3,2,1,0:T(8,128)(2,1)}, bf16[2,2,128,256]{3,2,1,0:T(8,128)(2,1)}, u32[]{:S(2)}, u32[]{:S(2)}) %collective-permute-start.2) | collective-permute-done | bytes 262176 | tf_op jit(solution)/shard_map/ppermute | solution.py:810
  19.6 0.0 collective-permute-done.theirs_ref
  19.7 0.0 copy-start.6
  19.7 0.0 copy-done.7
  19.7 1.0 %copy-done.6 = bf16[128,4096]{1,0:T(8,128)(2,1)} copy-done((bf16[128,4096]{1,0:T(8,128)(2,1)}, bf16[128,4096]{1,0:T(8,128)(2,1)S(1)}, u32[]{:S(2)}) %copy-start.6) | copy-done | bytes 1048600
  20.6 9.2 %attend.1 = (bf16[1,256,1024]{2,1,0:T(8,128)(2,1)}, bf16[1,256,1024]{2,1,0:T(8,128)(2,1)}, f32[288,256]{1,0:T(8,128)}) custom-call(s32[2]{0:T(128)} %pad_add_fusion.place_ref, s32[1,16]{1,0:T(1,128)} %doc_ref.1, bf16[128,4096]{1,0:T(8,128)(2,1)} %bitcast.31, bf16[128,4096]{1,0:T(8,128)(2,1)} %copy-done.6, ...), custom_call_target="tpu_custom_call" | custom-call | flops 5000000000 | bytes 4194304 | tf_op jit(solution)/shard_map/attend/pallas_call | solution.py:263
  29.8 0.1 collective-permute-start.7
  29.9 0.5 collective-permute-start.4
  30.4 0.1 collective-permute-start.5
  30.5 2.5 %collective-permute-start.6 = (bf16[256,1024]{1,0:T(8,128)(2,1)}, bf16[256,1024]{1,0:T(8,128)(2,1)S(1)}, u32[]{:S(2)}, u32[]{:S(2)}) collective-permute-start(bf16[256,1024]{1,0:T(8,128)(2,1)} %bitcast.21), channel_id=1, source_target_pairs={{0,16},{8,24},{16,0},{24,8},{1,17},{9,25},{17,1},{25,9},{2,18},{10... | collective-permute-start | bytes 1572872 | tf_op jit(solution)/shard_map/ppermute | solution.py:828
  33.0 0.0 collective-permute-done.7.theirs_ref
  33.0 0.0 copy-start.5
  33.0 0.7 copy-done.5
  33.7 1.7 %low_and_maps.1.low_ref.map_ref = bf16[288,256]{1,0:T(8,128)(2,1)} custom-call(f32[288,256]{1,0:T(8,128)} %get-tuple-element.24.mine_ref, f32[288,256]{1,0:T(8,128)} %copy-done.5), custom_call_target="tpu_custom_call" | custom-call | flops 1 | bytes 1 | tf_op jit(solution)/shard_map/low_and_maps/pallas_call | solution.py:301
  35.4 1.2 %collective-permute-start.8 = (bf16[288,256]{1,0:T(8,128)(2,1)}, bf16[288,256]{1,0:T(8,128)(2,1)S(1)}, u32[]{:S(2)}, u32[]{:S(2)}) collective-permute-start(bf16[288,256]{1,0:T(8,128)(2,1)} %low_and_maps.1.low_ref.map_ref), channel_id=1, source_target_pairs={{0,16},{8,24},{16,0},{24,8},{1,17},{9,25},{17,1},{25,9},{2,18},{10... | collective-permute-start | bytes 442376 | tf_op jit(solution)/shard_map/ppermute | solution.py:830
  36.6 9.1 %scan_own.1 = (bf16[512,1024]{1,0:T(8,128)(2,1)}, bf16[512,1024]{1,0:T(8,128)(2,1)}, f32[4,32,128]{2,1,0:T(8,128)}, f32[16,1024]{1,0:T(8,128)}, f32[1,1024]{1,0:T(1,128)}) custom-call(s32[2]{0:T(128)} %pad_add_fusion.place_ref, bf16[1,256,1024]{2,1,0:T(8,128)(2,1)} %get-tuple-element.23.stayed_ref.stream_ref, bf16[288,256]{1,0:T(8,128)(2,1)} %low_and_maps.1.low_ref.map_ref, ...), custom_call_target="tpu_custom_call" | custom-call | flops 4000000000 | bytes 2097152 | tf_op jit(solution)/shard_map/scan_own/pallas_call | solution.py:588
  45.8 0.0 collective-permute-done.4.got_sent_ref
  45.8 0.0 copy-start.4
  45.8 0.0 collective-permute-done.5.got_stayed_ref
  45.8 0.8 copy-done.4
  46.6 2.2 %join_heads.1.rest_2_ = bf16[128,4096]{1,0:T(8,128)(2,1)} custom-call(bf16[1,256,1024]{2,1,0:T(8,128)(2,1)} %get-tuple-element.22.sent_ref, bf16[1,256,1024]{2,1,0:T(8,128)(2,1)} %get-tuple-element.23.stayed_ref.stream_ref, bf16[1,256,1024]{2,1,0:T(8,128)(2,1)} %copy-done.4, bf16[1,256,1024]{2,1,0:T(8,128)(2,1)} %collective-permute-done.5.got_stayed_ref), custom_call_target="tpu_custom_call" | custom-call | tf_op jit(solution)/shard_map/join_heads/pallas_call | solution.py:104
  48.8 0.1 collective-permute-done.8
  48.8 0.0 copy-start.2
  48.8 0.0 collective-permute-done.6
  48.9 0.0 copy-start.3
  48.9 0.7 copy-done.2
  49.5 0.2 copy-done.3
  49.7 6.6 %step_sizes.1 = (bf16[256,1024]{1,0:T(8,128)(2,1)}, bf16[512,1024]{1,0:T(8,128)(2,1)}, f32[4,32,128]{2,1,0:T(8,128)}, bf16[8,144,128]{2,1,0:T(8,128)(2,1)}) custom-call(s32[2]{0:T(128)} %pad_add_fusion.place_ref, bf16[1,256,1024]{2,1,0:T(8,128)(2,1)} %bitcast.19, bf16[1,288,256]{2,1,0:T(8,128)(2,1)} %bitcast.17, ...), custom_call_target="tpu_custom_call", output_to_operand_aliasing={{1}: (10, {}), {2}: (11, {})} | custom-call | tf_op jit(solution)/shard_map/step_sizes/pallas_call | solution.py:428
  56.3 5.8 %all-to-all-start = ((bf16[8,144,128]{2,1,0:T(8,128)(2,1)}), bf16[8,144,128]{2,1,0:T(8,128)(2,1)S(1)}, u32[]{:S(2)}, u32[]{:S(2)}) async-start(bf16[8,144,128]{2,1,0:T(8,128)(2,1)} %get-tuple-element.35), calls=%async_computation | async-start | bytes 589824 | tf_op jit(solution)/shard_map/all_to_all | solution.py:840
  62.1 8.0 %scan_others.1 = (bf16[512,1024]{1,0:T(8,128)(2,1)}, f32[1,16,1024]{2,1,0:T(8,128)}) custom-call(s32[2]{0:T(128)} %pad_add_fusion.place_ref, bf16[1,256,1024]{2,1,0:T(8,128)(2,1)} %bitcast.20, bf16[256,1024]{1,0:T(8,128)(2,1)} %get-tuple-element.29.steps_ref, f32[4,32,128]{2,1,0:T(8,128)} %get-tuple-element.30.maps_ref, ...), custom_call_target="tpu_custom_call", output_to_operand_aliasing={{0}: (6, {})} | custom-call | flops 4000000000 | bytes 2097152 | tf_op jit(solution)/shard_map/scan_others/pallas_call | solution.py:654
  70.1 1.6 %all-to-all-done.carries_ref = bf16[8,144,128]{2,1,0:T(8,128)(2,1)S(1)} async-done(((bf16[8,144,128]{2,1,0:T(8,128)(2,1)}), bf16[8,144,128]{2,1,0:T(8,128)(2,1)S(1)}, u32[]{:S(2)}, u32[]{:S(2)}) %all-to-all-start) | async-done | bytes 294944 | tf_op jit(solution)/shard_map/all_to_all | solution.py:840
  71.7 0.7 copy-done.1
  72.5 9.2 %add_carried.1 = bf16[512,1024]{1,0:T(8,128)(2,1)} custom-call(s32[2]{0:T(128)} %pad_add_fusion.place_ref, bf16[512,1024]{1,0:T(8,128)(2,1)} %get-tuple-element.32.part_ref, bf16[512,1024]{1,0:T(8,128)(2,1)} %get-tuple-element.33.sums_ref, f32[4,32,128]{2,1,0:T(8,128)} %get-tuple-element.30.maps_ref, f32[16,1024]{1,0:T(8,128)} %get-tuple-element.25.rest_0_.last_own_ref, ...), custom_call_target="tpu_custom_call" | custom-call | tf_op jit(solution)/shard_map/add_carried/pallas_call | solution.py:759
  (1 shorter events, 0.0 us)
Async XLA Ops:
  0.6 14.1 %copy-start = (bf16[256,4096]{1,0:T(8,128)(2,1)S(1)}, bf16[256,4096]{1,0:T(8,128)(2,1)}, u32[]{:S(2)}) copy-start(bf16[256,4096]{1,0:T(8,128)(2,1)} %param.16) | copy-start | bytes 6291460
  2.6 17.0 %collective-permute-start = (bf16[128,4096]{1,0:T(8,128)(2,1)}, bf16[128,4096]{1,0:T(8,128)(2,1)S(1)}, u32[]{:S(2)}, u32[]{:S(2)}) collective-permute-start(bf16[128,4096]{1,0:T(8,128)(2,1)} %bitcast.30), channel_id=1, source_target_pairs={{0,8},{8,0},{16,24},{24,16},{1,9},{9,1},{17,25},{25,17},{2,10},{10... | collective-permute-start | bytes 3145736 | tf_op jit(solution)/shard_map/ppermute | solution.py:814
  3.2 12.4 %collective-permute-start.3 = (bf16[2,2,128,256]{3,2,1,0:T(8,128)(2,1)}, bf16[2,2,128,256]{3,2,1,0:T(8,128)(2,1)S(1)}, u32[]{:S(2)}, u32[]{:S(2)}) collective-permute-start(bf16[2,2,128,256]{3,2,1,0:T(8,128)(2,1)} %get-tuple-element.21), channel_id=1, source_target_pairs={{0,24},{8,16},{1,25},{9,17},{2,26},{10,18},{3,27},{11,19},{4,28},{... | collective-permute-start | bytes 786440 | tf_op jit(solution)/shard_map/ppermute | solution.py:811
  7.7 7.9 %collective-permute-start.1 = (bf16[2,2,128,256]{3,2,1,0:T(8,128)(2,1)}, bf16[2,2,128,256]{3,2,1,0:T(8,128)(2,1)}, u32[]{:S(2)}, u32[]{:S(2)}) collective-permute-start(bf16[2,2,128,256]{3,2,1,0:T(8,128)(2,1)} %get-tuple-element.21), channel_id=1, source_target_pairs={{0,8},{8,0},{16,24},{24,16},{1,9},{9,1},{17,25},{25,17},{2,10},{10... | collective-permute-start | bytes 786440 | tf_op jit(solution)/shard_map/ppermute | solution.py:812
  7.8 11.8 %collective-permute-start.2 = (bf16[2,2,128,256]{3,2,1,0:T(8,128)(2,1)}, bf16[2,2,128,256]{3,2,1,0:T(8,128)(2,1)}, u32[]{:S(2)}, u32[]{:S(2)}) collective-permute-start(bf16[2,2,128,256]{3,2,1,0:T(8,128)(2,1)} %get-tuple-element.19.own_ref), channel_id=1, source_target_pairs={{0,16},{8,24},{1,17},{9,25},{2,18},{10,26},{3,19},{11,27},{4,20},{... | collective-permute-start | bytes 786440 | tf_op jit(solution)/shard_map/ppermute | solution.py:810
  15.6 4.1 %copy-start.7 = (bf16[2,2,128,256]{3,2,1,0:T(8,128)(2,1)}, bf16[2,2,128,256]{3,2,1,0:T(8,128)(2,1)S(1)}, u32[]{:S(2)}) copy-start(bf16[2,2,128,256]{3,2,1,0:T(8,128)(2,1)S(1)} %collective-permute-done.3.far_ref) | copy-start | bytes 786436
  19.7 1.0 %copy-start.6 = (bf16[128,4096]{1,0:T(8,128)(2,1)}, bf16[128,4096]{1,0:T(8,128)(2,1)S(1)}, u32[]{:S(2)}) copy-start(bf16[128,4096]{1,0:T(8,128)(2,1)S(1)} %collective-permute-done.theirs_ref) | copy-start | bytes 3145732
  29.8 3.2 %collective-permute-start.7 = (f32[288,256]{1,0:T(8,128)}, f32[288,256]{1,0:T(8,128)S(1)}, u32[]{:S(2)}, u32[]{:S(2)}) collective-permute-start(f32[288,256]{1,0:T(8,128)} %get-tuple-element.24.mine_ref), channel_id=1, source_target_pairs={{0,8},{8,0},{16,24},{24,16},{1,9},{9,1},{17,25},{25,17},{2,10},{10... | collective-permute-start | bytes 884744 | tf_op jit(solution)/shard_map/ppermute | solution.py:829
  29.9 15.9 %collective-permute-start.4 = (bf16[1,256,1024]{2,1,0:T(8,128)(2,1)}, bf16[1,256,1024]{2,1,0:T(8,128)(2,1)S(1)}, u32[]{:S(2)}, u32[]{:S(2)}) collective-permute-start(bf16[1,256,1024]{2,1,0:T(8,128)(2,1)} %get-tuple-element.22.sent_ref), channel_id=1, source_target_pairs={{0,8},{8,0},{16,24},{24,16},{1,9},{9,1},{17,25},{25,17},{2,10},{10... | collective-permute-start | bytes 1572872 | tf_op jit(solution)/shard_map/ppermute | solution.py:831
  30.4 15.4 %collective-permute-start.5 = (bf16[1,256,1024]{2,1,0:T(8,128)(2,1)}, bf16[1,256,1024]{2,1,0:T(8,128)(2,1)}, u32[]{:S(2)}, u32[]{:S(2)}) collective-permute-start(bf16[1,256,1024]{2,1,0:T(8,128)(2,1)} %get-tuple-element.23.stayed_ref.stream_ref), channel_id=1, source_target_pairs={{0,8},{8,0},{16,24},{24,16},{1,9},{9,1},{17,25},{25,17},{2,10},{10... | collective-permute-start | bytes 1572872 | tf_op jit(solution)/shard_map/ppermute | solution.py:832
  30.5 18.4 %collective-permute-start.6 = (bf16[256,1024]{1,0:T(8,128)(2,1)}, bf16[256,1024]{1,0:T(8,128)(2,1)S(1)}, u32[]{:S(2)}, u32[]{:S(2)}) collective-permute-start(bf16[256,1024]{1,0:T(8,128)(2,1)} %bitcast.21), channel_id=1, source_target_pairs={{0,16},{8,24},{16,0},{24,8},{1,17},{9,25},{17,1},{25,9},{2,18},{10... | collective-permute-start | bytes 1572872 | tf_op jit(solution)/shard_map/ppermute | solution.py:828
  33.0 0.7 copy-start.5
  35.4 13.4 %collective-permute-start.8 = (bf16[288,256]{1,0:T(8,128)(2,1)}, bf16[288,256]{1,0:T(8,128)(2,1)S(1)}, u32[]{:S(2)}, u32[]{:S(2)}) collective-permute-start(bf16[288,256]{1,0:T(8,128)(2,1)} %low_and_maps.1.low_ref.map_ref), channel_id=1, source_target_pairs={{0,16},{8,24},{16,0},{24,8},{1,17},{9,25},{17,1},{25,9},{2,18},{10... | collective-permute-start | bytes 442376 | tf_op jit(solution)/shard_map/ppermute | solution.py:830
  45.8 0.8 copy-start.4
  48.8 0.7 copy-start.2
  48.9 0.8 %copy-start.3 = (bf16[256,1024]{1,0:T(8,128)(2,1)}, bf16[256,1024]{1,0:T(8,128)(2,1)S(1)}, u32[]{:S(2)}) copy-start(bf16[256,1024]{1,0:T(8,128)(2,1)S(1)} %collective-permute-done.6) | copy-start | bytes 1572868
  56.3 15.5 %all-to-all-start = ((bf16[8,144,128]{2,1,0:T(8,128)(2,1)}), bf16[8,144,128]{2,1,0:T(8,128)(2,1)S(1)}, u32[]{:S(2)}, u32[]{:S(2)}) async-start(bf16[8,144,128]{2,1,0:T(8,128)(2,1)} %get-tuple-element.35), calls=%async_computation | async-start | bytes 589824 | tf_op jit(solution)/shard_map/all_to_all | solution.py:840
  71.7 0.7 copy-start.1

commit v5 on v3

--- a/solution.py
+++ b/solution.py
@@ -110,9 +110,9 @@
     chip, core = place_ref[0], place_ref[1]
     first_core = core == 0
 
-    def above(shape):
-        row = lax.rem(lax.broadcasted_iota(jnp.int32, shape, 0), rows)
-        return lax.broadcasted_iota(jnp.int32, shape, 1) > row
+    def below(shape):
+        column = lax.rem(lax.broadcasted_iota(jnp.int32, shape, 1), rows)
+        return lax.broadcasted_iota(jnp.int32, shape, 0) > column
 
     @pl.when(step == 0)
     def _():
@@ -120,30 +120,29 @@
         own = chip * CORES + core
         swapped = chip * CORES + 1 - core
         near, far = own - CORES, swapped - CORES
-        lane = lax.broadcasted_iota(jnp.int32, (rows, rows), 1)
-        row = lax.broadcasted_iota(jnp.int32, (rows, rows), 0)
+        query = lax.broadcasted_iota(jnp.int32, (rows, rows), 1)
+        key = lax.broadcasted_iota(jnp.int32, (rows, rows), 0)
         for item, (place, before, middle) in enumerate(
             (
                 (own, near, jnp.where(first_core, far, swapped)),
                 (swapped, far, jnp.where(first_core, own, near)),
             )
         ):
-            query_pos = place * rows + row
+            query_pos = place * rows + query
             start = jnp.zeros((rows, rows), jnp.int32)
             bound = jnp.int32(0)
             for doc in range(doc_ref.shape[1]):
                 bound = bound + doc_ref[0, doc]
                 start = jnp.where(query_pos >= bound, bound, start)
-            ends = jnp.where(lane > row, before, place) * rows + lane
-            mask_ref[item, :, :rows] = jnp.where(
+            ends = jnp.where(key > query, before, place) * rows + key
+            mask_ref[item, :rows, :] = jnp.where(
                 (ends >= start) & (ends <= query_pos), 0.0, masked_fill
             )
-            mask_ref[item, :, rows:] = jnp.where(
-                middle * rows + lane >= start, 0.0, masked_fill
+            mask_ref[item, rows:, :] = jnp.where(
+                middle * rows + key >= start, 0.0, masked_fill
             )
 
     scale = LOG2E / math.sqrt(HEAD_SIZE)
-    ones = jnp.ones((3 * rows, HEAD_SIZE), jnp.bfloat16)
 
     def windows(kind):
         own, swapped = own_ref[0, kind], swap_ref[0, kind]
@@ -160,32 +159,34 @@
         )
         scores.append(
             lax.dot_general(
-                stacked, keys, (((1,), (1,)), ((), ())), preferred_element_type=jnp.float32
+                keys, stacked, (((1,), (1,)), ((), ())), preferred_element_type=jnp.float32
             )
         )
     outputs = []
-    before = above((group * rows, rows))
+    before = below((rows, group * rows))
+    none = jnp.zeros((rows, group * rows), jnp.bfloat16)
     for item, (values, score) in enumerate(zip(windows(1), scores)):
         fill = mask_ref[item]
-        ends = jnp.where(before, score[:, :rows], score[:, rows : 2 * rows])
-        kept = jnp.concatenate([ends, score[:, 2 * rows :]], axis=1)
-        kept = jnp.concatenate(
-            [kept[i * rows : (i + 1) * rows, :] + fill for i in range(group)], axis=0
+        ends = jnp.where(before, score[:rows, :], score[rows : 2 * rows, :])
+        kept = jnp.concatenate([ends, score[2 * rows :, :]], axis=0)
+        kept = kept + jnp.concatenate([fill] * group, axis=1)
+        peak = jnp.max(kept, axis=0, keepdims=True)
+        raw = jnp.exp2((kept - peak) * scale)
+        share = pl.reciprocal(jnp.sum(raw, axis=0, keepdims=True))
+        raw = raw.astype(jnp.bfloat16)
+        ends = raw[:rows, :]
+        spread = jnp.concatenate(
+            [jnp.where(before, ends, none), jnp.where(before, none, ends), raw[rows:, :]], axis=0
         )
-        peak = jnp.max(kept, axis=1, keepdims=True)
-        raw = jnp.exp2((kept - peak) * scale).astype(jnp.bfloat16)
-        ends = raw[:, :rows]
-        none = jnp.zeros_like(ends)
-        spread = jnp.concatenate(
-            [jnp.where(before, ends, none), jnp.where(before, none, ends), raw[:, rows:]], axis=1
+        mixed = lax.dot_general(
+            values, spread, (((0,), (0,)), ((), ())), preferred_element_type=jnp.float32
         )
-        both = jnp.dot(
-            spread, jnp.concatenate([values, ones], axis=1), preferred_element_type=jnp.float32
-        )
-        mixed = both[:, :HEAD_SIZE] * pl.reciprocal(both[:, HEAD_SIZE:])
-        mixed = mixed.astype(jnp.bfloat16)
+        mixed = mixed * share
         outputs.append(
-            jnp.concatenate([mixed[i * rows : (i + 1) * rows, :] for i in range(group)], axis=1)
+            jnp.concatenate(
+                [mixed[:, i * rows : (i + 1) * rows].T.astype(jnp.bfloat16) for i in range(group)],
+                axis=1,
+            )
         )
     stream = jnp.concatenate(
         [
@@ -252,7 +253,7 @@
                 ),
                 pl.BlockSpec((CORES * rows + 2 * NS, RANK), lambda j, s: (0, 0)),
             ],
-            scratch_shapes=[pltpu.VMEM((2, rows, 2 * rows), jnp.float32)],
+            scratch_shapes=[pltpu.VMEM((2, 2 * rows, rows), jnp.float32)],
         ),
         out_shape=[
             jax.ShapeDtypeStruct((chips - 1, CORES * rows, width), jnp.bfloat16),

time: 81.2 us -> 81.1 us (level)
  no operation moved by 1% of the time
where the time goes in v5:
time: 81.1 us; the launch traced here: 80.5 us
  Pallas kernels  46.9 us (58%)
  starting transfers between devices  17.6 us (22%)
  local copies, waits for them, and re-layouts  7.39 us (9%)
  waiting for transfers between devices  5.77 us (7%)
  other arithmetic  2.08 us (3%)
    pallas_call x1, Pallas kernels, add_carried(): pl.pallas_call(carried_kernel, grid_spec=pltpu.PrefetchScalarGridSpec(num...  9.17 us
    pallas_call x1, Pallas kernels, scan_own(): pl.pallas_call(own_kernel, grid_spec=pltpu.PrefetchScalarGridSpec(num_sca...  9.14 us
    pallas_call x1, Pallas kernels, attend(): pl.pallas_call(functools.partial(attend_kernel, chips=chips), grid_spec=p...  8.03 us
    pallas_call x1, Pallas kernels, scan_others(): pl.pallas_call(others_kernel, grid_spec=pltpu.PrefetchScalarGridSpec(num_...  8.01 us
    pallas_call x1, Pallas kernels, step_sizes(): pl.pallas_call(step_kernel, grid_spec=pltpu.PrefetchScalarGridSpec(num_sc...  6.6 us
    all_to_all x1, starting transfers between devices, local(): lax.all_to_all(carry, 'chan', split_axis=0, concat_axis=0, tiled=True)  5.82 us
    ppermute x1, starting transfers between devices, local(): from_far = lax.ppermute(theirs, 'seq', far)  4.54 us
    ppermute x1, waiting for transfers between devices, local(): from_near = lax.ppermute(own, 'seq', near)  4.04 us
  transfers between devices with their start and end apart: 10, of which 3 were waited for; matrix products, arithmetic and copies ran while one was open for 7% of the time, Pallas kernels for 26%

profile of v5, /device:TPU:0, one launch (start us, length us, event | category | flops | bytes accessed | tf_op | source)
XLA Modules:
  0.0 80.5 jit_solution(11059469640686180064)
XLA Ops:
  0.6 0.0 copy-start
  0.6 2.1 %select_heads.1 = (bf16[2,2,128,256]{3,2,1,0:T(8,128)(2,1)}, bf16[2,2,128,256]{3,2,1,0:T(8,128)(2,1)}) custom-call(bf16[128,1024]{1,0:T(8,128)(2,1)} %bitcast.22, bf16[128,1024]{1,0:T(8,128)(2,1)} %bitcast.23), custom_call_target="tpu_custom_call" | custom-call | tf_op jit(solution)/shard_map/select_heads/pallas_call | solution.py:61
  2.7 0.5 collective-permute-start
  3.3 4.5 %collective-permute-start.3 = (bf16[2,2,128,256]{3,2,1,0:T(8,128)(2,1)}, bf16[2,2,128,256]{3,2,1,0:T(8,128)(2,1)S(1)}, u32[]{:S(2)}, u32[]{:S(2)}) collective-permute-start(bf16[2,2,128,256]{3,2,1,0:T(8,128)(2,1)} %get-tuple-element.21), channel_id=1, source_target_pairs={{0,24},{8,16},{1,25},{9,17},{2,26},{10,18},{3,27},{11,19},{4,28},{... | collective-permute-start | bytes 786440 | tf_op jit(solution)/shard_map/ppermute | solution.py:784
  7.8 0.1 collective-permute-start.1
  7.9 2.3 %collective-permute-start.2 = (bf16[2,2,128,256]{3,2,1,0:T(8,128)(2,1)}, bf16[2,2,128,256]{3,2,1,0:T(8,128)(2,1)}, u32[]{:S(2)}, u32[]{:S(2)}) collective-permute-start(bf16[2,2,128,256]{3,2,1,0:T(8,128)(2,1)} %get-tuple-element.19.own_ref), channel_id=1, source_target_pairs={{0,16},{8,24},{1,17},{9,25},{2,18},{10,26},{3,19},{11,27},{4,20},{... | collective-permute-start | bytes 786440 | tf_op jit(solution)/shard_map/ppermute | solution.py:783
  10.2 0.6 pad_add_fusion.place_ref
  10.8 1.3 %dynamic_slice.14 = f32[1024]{0:T(1024)} dynamic-slice(f32[4096]{0:T(1024)} %param.17, s32[]{:T(128)S(6)} %select_n.12), dynamic_slice_sizes={1024} | dynamic-slice | bytes 8196 | tf_op jit(solution)/shard_map/dynamic_slice | solution.py:794
  12.1 1.3 %dynamic_slice.15 = f32[1024]{0:T(1024)} dynamic-slice(f32[4096]{0:T(1024)} %param.19, s32[]{:T(128)S(6)} %select_n.12), dynamic_slice_sizes={1024} | dynamic-slice | bytes 8196 | tf_op jit(solution)/shard_map/dynamic_slice | solution.py:795
  13.4 1.5 %multiply_bitcast_fusion.rest_0_.rates_ref = f32[16,1024]{1,0:T(8,128)} fusion(f32[4096,16]{0,1:T(8,128)} %param.18, s32[]{:T(128)S(6)} %select_n.12), kind=kLoop, calls=%fused_computation | loop fusion | flops 16384 | bytes 131076 | tf_op jit(solution)/shard_map/transpose | solution.py:792
  14.8 0.0 copy-done
  14.9 0.8 %constant_dynamic-slice_fusion.rest_1_.cols_ref = bf16[256,1024]{1,0:T(8,128)(2,1)} fusion(bf16[256,4096]{1,0:T(8,128)(2,1)S(1)} %copy-done, s32[]{:T(128)S(6)} %select_n.12), kind=kLoop, calls=%fused_computation.2 | loop fusion | bytes 1048580 | tf_op jit(solution)/shard_map/dynamic_slice | solution.py:793
  15.7 0.0 collective-permute-done.3.far_ref
  15.7 0.0 copy-start.7
  15.7 0.0 collective-permute-done.1.swap_ref
  15.7 4.0 %collective-permute-done.2.near_ref = bf16[2,2,128,256]{3,2,1,0:T(8,128)(2,1)} collective-permute-done((bf16[2,2,128,256]{3,2,1,0:T(8,128)(2,1)}, bf16[2,2,128,256]{3,2,1,0:T(8,128)(2,1)}, u32[]{:S(2)}, u32[]{:S(2)}) %collective-permute-start.2) | collective-permute-done | bytes 262176 | tf_op jit(solution)/shard_map/ppermute | solution.py:783
  19.7 0.0 collective-permute-done.theirs_ref
  19.7 0.0 copy-start.6
  19.7 0.0 copy-done.7
  19.7 1.0 %copy-done.6 = bf16[128,4096]{1,0:T(8,128)(2,1)} copy-done((bf16[128,4096]{1,0:T(8,128)(2,1)}, bf16[128,4096]{1,0:T(8,128)(2,1)S(1)}, u32[]{:S(2)}) %copy-start.6) | copy-done | bytes 1048600
  20.7 8.0 %attend.1 = (bf16[1,256,1024]{2,1,0:T(8,128)(2,1)}, bf16[1,256,1024]{2,1,0:T(8,128)(2,1)}, f32[288,256]{1,0:T(8,128)}) custom-call(s32[2]{0:T(128)} %pad_add_fusion.place_ref, s32[1,16]{1,0:T(1,128)} %doc_ref.1, bf16[128,4096]{1,0:T(8,128)(2,1)} %bitcast.31, bf16[128,4096]{1,0:T(8,128)(2,1)} %copy-done.6, ...), custom_call_target="tpu_custom_call" | custom-call | flops 5000000000 | bytes 4194304 | tf_op jit(solution)/shard_map/attend/pallas_call | solution.py:236
  28.7 0.1 collective-permute-start.7
  28.8 0.5 collective-permute-start.4
  29.3 0.1 collective-permute-start.5
  29.4 2.5 %collective-permute-start.6 = (bf16[256,1024]{1,0:T(8,128)(2,1)}, bf16[256,1024]{1,0:T(8,128)(2,1)S(1)}, u32[]{:S(2)}, u32[]{:S(2)}) collective-permute-start(bf16[256,1024]{1,0:T(8,128)(2,1)} %bitcast.21), channel_id=1, source_target_pairs={{0,16},{8,24},{16,0},{24,8},{1,17},{9,25},{17,1},{25,9},{2,18},{10... | collective-permute-start | bytes 1572872 | tf_op jit(solution)/shard_map/ppermute | solution.py:801
  31.9 0.0 collective-permute-done.7.theirs_ref
  31.9 0.0 copy-start.5
  31.9 0.7 copy-done.5
  32.6 1.7 %low_and_maps.1.low_ref.map_ref = bf16[288,256]{1,0:T(8,128)(2,1)} custom-call(f32[288,256]{1,0:T(8,128)} %get-tuple-element.24.mine_ref, f32[288,256]{1,0:T(8,128)} %copy-done.5), custom_call_target="tpu_custom_call" | custom-call | flops 1 | bytes 1 | tf_op jit(solution)/shard_map/low_and_maps/pallas_call | solution.py:274
  34.3 1.2 %collective-permute-start.8 = (bf16[288,256]{1,0:T(8,128)(2,1)}, bf16[288,256]{1,0:T(8,128)(2,1)S(1)}, u32[]{:S(2)}, u32[]{:S(2)}) collective-permute-start(bf16[288,256]{1,0:T(8,128)(2,1)} %low_and_maps.1.low_ref.map_ref), channel_id=1, source_target_pairs={{0,16},{8,24},{16,0},{24,8},{1,17},{9,25},{17,1},{25,9},{2,18},{10... | collective-permute-start | bytes 442376 | tf_op jit(solution)/shard_map/ppermute | solution.py:803
  35.5 9.1 %scan_own.1 = (bf16[512,1024]{1,0:T(8,128)(2,1)}, bf16[512,1024]{1,0:T(8,128)(2,1)}, f32[4,32,128]{2,1,0:T(8,128)}, f32[16,1024]{1,0:T(8,128)}, f32[1,1024]{1,0:T(1,128)}) custom-call(s32[2]{0:T(128)} %pad_add_fusion.place_ref, bf16[1,256,1024]{2,1,0:T(8,128)(2,1)} %get-tuple-element.23.stayed_ref.stream_ref, bf16[288,256]{1,0:T(8,128)(2,1)} %low_and_maps.1.low_ref.map_ref, ...), custom_call_target="tpu_custom_call" | custom-call | flops 4000000000 | bytes 2097152 | tf_op jit(solution)/shard_map/scan_own/pallas_call | solution.py:561
  44.7 0.0 collective-permute-done.4.got_sent_ref
  44.7 0.0 copy-start.4
  44.7 0.0 collective-permute-done.5.got_stayed_ref
  44.7 0.8 copy-done.4
  45.5 2.2 %join_heads.1.rest_2_ = bf16[128,4096]{1,0:T(8,128)(2,1)} custom-call(bf16[1,256,1024]{2,1,0:T(8,128)(2,1)} %get-tuple-element.22.sent_ref, bf16[1,256,1024]{2,1,0:T(8,128)(2,1)} %get-tuple-element.23.stayed_ref.stream_ref, bf16[1,256,1024]{2,1,0:T(8,128)(2,1)} %copy-done.4, bf16[1,256,1024]{2,1,0:T(8,128)(2,1)} %collective-permute-done.5.got_stayed_ref), custom_call_target="tpu_custom_call" | custom-call | tf_op jit(solution)/shard_map/join_heads/pallas_call | solution.py:90
  47.7 0.1 collective-permute-done.8
  47.8 0.0 copy-start.2
  47.8 0.0 collective-permute-done.6
  47.8 0.0 copy-start.3
  47.8 0.7 copy-done.2
  48.4 0.2 copy-done.3
  48.6 6.6 %step_sizes.1 = (bf16[256,1024]{1,0:T(8,128)(2,1)}, bf16[512,1024]{1,0:T(8,128)(2,1)}, f32[4,32,128]{2,1,0:T(8,128)}, bf16[8,144,128]{2,1,0:T(8,128)(2,1)}) custom-call(s32[2]{0:T(128)} %pad_add_fusion.place_ref, bf16[1,256,1024]{2,1,0:T(8,128)(2,1)} %bitcast.19, bf16[1,288,256]{2,1,0:T(8,128)(2,1)} %bitcast.17, ...), custom_call_target="tpu_custom_call", output_to_operand_aliasing={{1}: (10, {}), {2}: (11, {})} | custom-call | tf_op jit(solution)/shard_map/step_sizes/pallas_call | solution.py:401
  55.2 5.8 %all-to-all-start = ((bf16[8,144,128]{2,1,0:T(8,128)(2,1)}), bf16[8,144,128]{2,1,0:T(8,128)(2,1)S(1)}, u32[]{:S(2)}, u32[]{:S(2)}) async-start(bf16[8,144,128]{2,1,0:T(8,128)(2,1)} %get-tuple-element.35), calls=%async_computation | async-start | bytes 589824 | tf_op jit(solution)/shard_map/all_to_all | solution.py:813
  61.0 8.0 %scan_others.1 = (bf16[512,1024]{1,0:T(8,128)(2,1)}, f32[1,16,1024]{2,1,0:T(8,128)}) custom-call(s32[2]{0:T(128)} %pad_add_fusion.place_ref, bf16[1,256,1024]{2,1,0:T(8,128)(2,1)} %bitcast.20, bf16[256,1024]{1,0:T(8,128)(2,1)} %get-tuple-element.29.steps_ref, f32[4,32,128]{2,1,0:T(8,128)} %get-tuple-element.30.maps_ref, ...), custom_call_target="tpu_custom_call", output_to_operand_aliasing={{0}: (6, {})} | custom-call | flops 4000000000 | bytes 2097152 | tf_op jit(solution)/shard_map/scan_others/pallas_call | solution.py:627
  69.0 1.6 %all-to-all-done.carries_ref = bf16[8,144,128]{2,1,0:T(8,128)(2,1)S(1)} async-done(((bf16[8,144,128]{2,1,0:T(8,128)(2,1)}), bf16[8,144,128]{2,1,0:T(8,128)(2,1)S(1)}, u32[]{:S(2)}, u32[]{:S(2)}) %all-to-all-start) | async-done | bytes 294944 | tf_op jit(solution)/shard_map/all_to_all | solution.py:813
  70.7 0.7 copy-done.1
  71.4 9.2 %add_carried.1 = bf16[512,1024]{1,0:T(8,128)(2,1)} custom-call(s32[2]{0:T(128)} %pad_add_fusion.place_ref, bf16[512,1024]{1,0:T(8,128)(2,1)} %get-tuple-element.32.part_ref, bf16[512,1024]{1,0:T(8,128)(2,1)} %get-tuple-element.33.sums_ref, f32[4,32,128]{2,1,0:T(8,128)} %get-tuple-element.30.maps_ref, f32[16,1024]{1,0:T(8,128)} %get-tuple-element.25.rest_0_.last_own_ref, ...), custom_call_target="tpu_custom_call" | custom-call | tf_op jit(solution)/shard_map/add_carried/pallas_call | solution.py:732
  (1 shorter events, 0.0 us)
Async XLA Ops:
  0.6 14.2 %copy-start = (bf16[256,4096]{1,0:T(8,128)(2,1)S(1)}, bf16[256,4096]{1,0:T(8,128)(2,1)}, u32[]{:S(2)}) copy-start(bf16[256,4096]{1,0:T(8,128)(2,1)} %param.16) | copy-start | bytes 6291460
  2.7 17.0 %collective-permute-start = (bf16[128,4096]{1,0:T(8,128)(2,1)}, bf16[128,4096]{1,0:T(8,128)(2,1)S(1)}, u32[]{:S(2)}, u32[]{:S(2)}) collective-permute-start(bf16[128,4096]{1,0:T(8,128)(2,1)} %bitcast.30), channel_id=1, source_target_pairs={{0,8},{8,0},{16,24},{24,16},{1,9},{9,1},{17,25},{25,17},{2,10},{10... | collective-permute-start | bytes 3145736 | tf_op jit(solution)/shard_map/ppermute | solution.py:787
  3.3 12.4 %collective-permute-start.3 = (bf16[2,2,128,256]{3,2,1,0:T(8,128)(2,1)}, bf16[2,2,128,256]{3,2,1,0:T(8,128)(2,1)S(1)}, u32[]{:S(2)}, u32[]{:S(2)}) collective-permute-start(bf16[2,2,128,256]{3,2,1,0:T(8,128)(2,1)} %get-tuple-element.21), channel_id=1, source_target_pairs={{0,24},{8,16},{1,25},{9,17},{2,26},{10,18},{3,27},{11,19},{4,28},{... | collective-permute-start | bytes 786440 | tf_op jit(solution)/shard_map/ppermute | solution.py:784
  7.8 7.9 %collective-permute-start.1 = (bf16[2,2,128,256]{3,2,1,0:T(8,128)(2,1)}, bf16[2,2,128,256]{3,2,1,0:T(8,128)(2,1)}, u32[]{:S(2)}, u32[]{:S(2)}) collective-permute-start(bf16[2,2,128,256]{3,2,1,0:T(8,128)(2,1)} %get-tuple-element.21), channel_id=1, source_target_pairs={{0,8},{8,0},{16,24},{24,16},{1,9},{9,1},{17,25},{25,17},{2,10},{10... | collective-permute-start | bytes 786440 | tf_op jit(solution)/shard_map/ppermute | solution.py:785
  7.9 11.8 %collective-permute-start.2 = (bf16[2,2,128,256]{3,2,1,0:T(8,128)(2,1)}, bf16[2,2,128,256]{3,2,1,0:T(8,128)(2,1)}, u32[]{:S(2)}, u32[]{:S(2)}) collective-permute-start(bf16[2,2,128,256]{3,2,1,0:T(8,128)(2,1)} %get-tuple-element.19.own_ref), channel_id=1, source_target_pairs={{0,16},{8,24},{1,17},{9,25},{2,18},{10,26},{3,19},{11,27},{4,20},{... | collective-permute-start | bytes 786440 | tf_op jit(solution)/shard_map/ppermute | solution.py:783
  15.7 4.1 %copy-start.7 = (bf16[2,2,128,256]{3,2,1,0:T(8,128)(2,1)}, bf16[2,2,128,256]{3,2,1,0:T(8,128)(2,1)S(1)}, u32[]{:S(2)}) copy-start(bf16[2,2,128,256]{3,2,1,0:T(8,128)(2,1)S(1)} %collective-permute-done.3.far_ref) | copy-start | bytes 786436
  19.7 1.0 %copy-start.6 = (bf16[128,4096]{1,0:T(8,128)(2,1)}, bf16[128,4096]{1,0:T(8,128)(2,1)S(1)}, u32[]{:S(2)}) copy-start(bf16[128,4096]{1,0:T(8,128)(2,1)S(1)} %collective-permute-done.theirs_ref) | copy-start | bytes 3145732
  28.7 3.1 %collective-permute-start.7 = (f32[288,256]{1,0:T(8,128)}, f32[288,256]{1,0:T(8,128)S(1)}, u32[]{:S(2)}, u32[]{:S(2)}) collective-permute-start(f32[288,256]{1,0:T(8,128)} %get-tuple-element.24.mine_ref), channel_id=1, source_target_pairs={{0,8},{8,0},{16,24},{24,16},{1,9},{9,1},{17,25},{25,17},{2,10},{10... | collective-permute-start | bytes 884744 | tf_op jit(solution)/shard_map/ppermute | solution.py:802
  28.8 15.8 %collective-permute-start.4 = (bf16[1,256,1024]{2,1,0:T(8,128)(2,1)}, bf16[1,256,1024]{2,1,0:T(8,128)(2,1)S(1)}, u32[]{:S(2)}, u32[]{:S(2)}) collective-permute-start(bf16[1,256,1024]{2,1,0:T(8,128)(2,1)} %get-tuple-element.22.sent_ref), channel_id=1, source_target_pairs={{0,8},{8,0},{16,24},{24,16},{1,9},{9,1},{17,25},{25,17},{2,10},{10... | collective-permute-start | bytes 1572872 | tf_op jit(solution)/shard_map/ppermute | solution.py:804
  29.3 15.4 %collective-permute-start.5 = (bf16[1,256,1024]{2,1,0:T(8,128)(2,1)}, bf16[1,256,1024]{2,1,0:T(8,128)(2,1)}, u32[]{:S(2)}, u32[]{:S(2)}) collective-permute-start(bf16[1,256,1024]{2,1,0:T(8,128)(2,1)} %get-tuple-element.23.stayed_ref.stream_ref), channel_id=1, source_target_pairs={{0,8},{8,0},{16,24},{24,16},{1,9},{9,1},{17,25},{25,17},{2,10},{10... | collective-permute-start | bytes 1572872 | tf_op jit(solution)/shard_map/ppermute | solution.py:805
  29.4 18.4 %collective-permute-start.6 = (bf16[256,1024]{1,0:T(8,128)(2,1)}, bf16[256,1024]{1,0:T(8,128)(2,1)S(1)}, u32[]{:S(2)}, u32[]{:S(2)}) collective-permute-start(bf16[256,1024]{1,0:T(8,128)(2,1)} %bitcast.21), channel_id=1, source_target_pairs={{0,16},{8,24},{16,0},{24,8},{1,17},{9,25},{17,1},{25,9},{2,18},{10... | collective-permute-start | bytes 1572872 | tf_op jit(solution)/shard_map/ppermute | solution.py:801
  31.9 0.7 copy-start.5
  34.3 13.4 %collective-permute-start.8 = (bf16[288,256]{1,0:T(8,128)(2,1)}, bf16[288,256]{1,0:T(8,128)(2,1)S(1)}, u32[]{:S(2)}, u32[]{:S(2)}) collective-permute-start(bf16[288,256]{1,0:T(8,128)(2,1)} %low_and_maps.1.low_ref.map_ref), channel_id=1, source_target_pairs={{0,16},{8,24},{16,0},{24,8},{1,17},{9,25},{17,1},{25,9},{2,18},{10... | collective-permute-start | bytes 442376 | tf_op jit(solution)/shard_map/ppermute | solution.py:803
  44.7 0.8 copy-start.4
  47.8 0.7 copy-start.2
  47.8 0.8 %copy-start.3 = (bf16[256,1024]{1,0:T(8,128)(2,1)}, bf16[256,1024]{1,0:T(8,128)(2,1)S(1)}, u32[]{:S(2)}) copy-start(bf16[256,1024]{1,0:T(8,128)(2,1)S(1)} %collective-permute-done.6) | copy-start | bytes 1572868
  55.2 15.5 %all-to-all-start = ((bf16[8,144,128]{2,1,0:T(8,128)(2,1)}), bf16[8,144,128]{2,1,0:T(8,128)(2,1)S(1)}, u32[]{:S(2)}, u32[]{:S(2)}) async-start(bf16[8,144,128]{2,1,0:T(8,128)(2,1)} %get-tuple-element.35), calls=%async_computation | async-start | bytes 589824 | tf_op jit(solution)/shard_map/all_to_all | solution.py:813
  70.7 0.7 copy-start.1

commit v6 on v5

--- a/solution.py
+++ b/solution.py
@@ -803,6 +803,7 @@
     low_come = [lax.ppermute(low_own, "seq", onward(step + 1)) for step in range(chips - 1)]
     got_sent = lax.ppermute(sent, "seq", swap)
     got_stayed = lax.ppermute(stayed, "seq", swap)
+    *come, got_stayed = lax.optimization_barrier((*come, got_stayed))
     attn_rows = join_heads(sent, stayed, got_sent, got_stayed)
 
     part, sums, maps, state, total = scan_own(place, stayed, low_own, cols, bias, rates, gain)

time: 81.1 us -> 80.9 us (level)
  transfers between devices with their start and end apart: 10 -> 10, of which waited for: 3 -> 2; matrix products, arithmetic and copies ran while one was open for 7% -> 7% of each run, Pallas kernels for 26% -> 26%
where the time goes in v6:
time: 80.9 us; the launch traced here: 80.3 us
  Pallas kernels  46.9 us (58%)
  starting transfers between devices  17.6 us (22%)
  local copies, waits for them, and re-layouts  7.24 us (9%)
  waiting for transfers between devices  5.72 us (7%)
  other arithmetic  2.03 us (3%)
    pallas_call x1, Pallas kernels, add_carried(): pl.pallas_call(carried_kernel, grid_spec=pltpu.PrefetchScalarGridSpec(num...  9.17 us
    pallas_call x1, Pallas kernels, scan_own(): pl.pallas_call(own_kernel, grid_spec=pltpu.PrefetchScalarGridSpec(num_sca...  9.14 us
    pallas_call x1, Pallas kernels, attend(): pl.pallas_call(functools.partial(attend_kernel, chips=chips), grid_spec=p...  8.03 us
    pallas_call x1, Pallas kernels, scan_others(): pl.pallas_call(others_kernel, grid_spec=pltpu.PrefetchScalarGridSpec(num_...  8.01 us
    pallas_call x1, Pallas kernels, step_sizes(): pl.pallas_call(step_kernel, grid_spec=pltpu.PrefetchScalarGridSpec(num_sc...  6.58 us
    all_to_all x1, starting transfers between devices, local(): lax.all_to_all(carry, 'chan', split_axis=0, concat_axis=0, tiled=True)  5.82 us
    ppermute x1, starting transfers between devices, local(): from_far = lax.ppermute(theirs, 'seq', far)  4.54 us
    ppermute x1, waiting for transfers between devices, local(): from_near = lax.ppermute(own, 'seq', near)  4.07 us
  transfers between devices with their start and end apart: 10, of which 2 were waited for; matrix products, arithmetic and copies ran while one was open for 7% of the time, Pallas kernels for 26%

profile of v6, /device:TPU:0, one launch (start us, length us, event | category | flops | bytes accessed | tf_op | source)
XLA Modules:
  0.0 80.3 jit_solution(7851622771028624503)
XLA Ops:
  0.6 0.0 copy-start
  0.6 2.1 %select_heads.1 = (bf16[2,2,128,256]{3,2,1,0:T(8,128)(2,1)}, bf16[2,2,128,256]{3,2,1,0:T(8,128)(2,1)}) custom-call(bf16[128,1024]{1,0:T(8,128)(2,1)} %bitcast.22, bf16[128,1024]{1,0:T(8,128)(2,1)} %bitcast.23), custom_call_target="tpu_custom_call" | custom-call | tf_op jit(solution)/shard_map/select_heads/pallas_call | solution.py:61
  2.7 0.5 collective-permute-start
  3.3 4.5 %collective-permute-start.3 = (bf16[2,2,128,256]{3,2,1,0:T(8,128)(2,1)}, bf16[2,2,128,256]{3,2,1,0:T(8,128)(2,1)S(1)}, u32[]{:S(2)}, u32[]{:S(2)}) collective-permute-start(bf16[2,2,128,256]{3,2,1,0:T(8,128)(2,1)} %get-tuple-element.23), channel_id=1, source_target_pairs={{0,24},{8,16},{1,25},{9,17},{2,26},{10,18},{3,27},{11,19},{4,28},{... | collective-permute-start | bytes 786440 | tf_op jit(solution)/shard_map/ppermute | solution.py:784
  7.8 0.1 collective-permute-start.1
  7.9 2.3 %collective-permute-start.2 = (bf16[2,2,128,256]{3,2,1,0:T(8,128)(2,1)}, bf16[2,2,128,256]{3,2,1,0:T(8,128)(2,1)}, u32[]{:S(2)}, u32[]{:S(2)}) collective-permute-start(bf16[2,2,128,256]{3,2,1,0:T(8,128)(2,1)} %get-tuple-element.21.own_ref), channel_id=1, source_target_pairs={{0,16},{8,24},{1,17},{9,25},{2,18},{10,26},{3,19},{11,27},{4,20},{... | collective-permute-start | bytes 786440 | tf_op jit(solution)/shard_map/ppermute | solution.py:783
  10.2 0.6 pad_add_fusion.place_ref
  10.8 1.3 %dynamic_slice.14 = f32[1024]{0:T(1024)} dynamic-slice(f32[4096]{0:T(1024)} %param.17, s32[]{:T(128)S(6)} %select_n.12), dynamic_slice_sizes={1024} | dynamic-slice | bytes 8196 | tf_op jit(solution)/shard_map/dynamic_slice | solution.py:794
  12.1 1.3 %dynamic_slice.15 = f32[1024]{0:T(1024)} dynamic-slice(f32[4096]{0:T(1024)} %param.19, s32[]{:T(128)S(6)} %select_n.12), dynamic_slice_sizes={1024} | dynamic-slice | bytes 8196 | tf_op jit(solution)/shard_map/dynamic_slice | solution.py:795
  13.3 1.5 %multiply_bitcast_fusion.rest_0_.rates_ref = f32[16,1024]{1,0:T(8,128)} fusion(f32[4096,16]{0,1:T(8,128)} %param.18, s32[]{:T(128)S(6)} %select_n.12), kind=kLoop, calls=%fused_computation | loop fusion | flops 16384 | bytes 131076 | tf_op jit(solution)/shard_map/transpose | solution.py:792
  14.8 0.0 copy-done
  14.8 0.8 %constant_dynamic-slice_fusion.rest_1_.cols_ref = bf16[256,1024]{1,0:T(8,128)(2,1)} fusion(bf16[256,4096]{1,0:T(8,128)(2,1)S(1)} %copy-done, s32[]{:T(128)S(6)} %select_n.12), kind=kLoop, calls=%fused_computation.2 | loop fusion | bytes 1048580 | tf_op jit(solution)/shard_map/dynamic_slice | solution.py:793
  15.7 0.0 collective-permute-done.3.far_ref
  15.7 0.0 copy-start.7
  15.7 0.0 collective-permute-done.1.swap_ref
  15.7 4.1 %collective-permute-done.2.near_ref = bf16[2,2,128,256]{3,2,1,0:T(8,128)(2,1)} collective-permute-done((bf16[2,2,128,256]{3,2,1,0:T(8,128)(2,1)}, bf16[2,2,128,256]{3,2,1,0:T(8,128)(2,1)}, u32[]{:S(2)}, u32[]{:S(2)}) %collective-permute-start.2) | collective-permute-done | bytes 262176 | tf_op jit(solution)/shard_map/ppermute | solution.py:783
  19.7 0.0 collective-permute-done.theirs_ref
  19.7 0.0 copy-start.6
  19.7 0.0 copy-done.7
  19.7 1.0 %copy-done.6 = bf16[128,4096]{1,0:T(8,128)(2,1)} copy-done((bf16[128,4096]{1,0:T(8,128)(2,1)}, bf16[128,4096]{1,0:T(8,128)(2,1)S(1)}, u32[]{:S(2)}) %copy-start.6) | copy-done | bytes 1048600
  20.7 8.0 %attend.1 = (bf16[1,256,1024]{2,1,0:T(8,128)(2,1)}, bf16[1,256,1024]{2,1,0:T(8,128)(2,1)}, f32[288,256]{1,0:T(8,128)}) custom-call(s32[2]{0:T(128)} %pad_add_fusion.place_ref, s32[1,16]{1,0:T(1,128)} %doc_ref.1, bf16[128,4096]{1,0:T(8,128)(2,1)} %bitcast.31, bf16[128,4096]{1,0:T(8,128)(2,1)} %copy-done.6, ...), custom_call_target="tpu_custom_call" | custom-call | flops 5000000000 | bytes 4194304 | tf_op jit(solution)/shard_map/attend/pallas_call | solution.py:236
  28.7 0.1 collective-permute-start.7
  28.8 2.5 %collective-permute-start.5 = (bf16[256,1024]{1,0:T(8,128)(2,1)}, bf16[256,1024]{1,0:T(8,128)(2,1)S(1)}, u32[]{:S(2)}, u32[]{:S(2)}) collective-permute-start(bf16[256,1024]{1,0:T(8,128)(2,1)} %bitcast.21), channel_id=1, source_target_pairs={{0,16},{8,24},{16,0},{24,8},{1,17},{9,25},{17,1},{25,9},{2,18},{10... | collective-permute-start | bytes 1572872 | tf_op jit(solution)/shard_map/ppermute | solution.py:801
  31.4 0.2 collective-permute-start.6
  31.5 0.3 collective-permute-start.4
  31.9 0.0 collective-permute-done.7.theirs_ref
  31.9 0.0 copy-start.5
  31.9 0.7 copy-done.5
  32.6 1.7 %low_and_maps.1.low_ref.map_ref = bf16[288,256]{1,0:T(8,128)(2,1)} custom-call(f32[288,256]{1,0:T(8,128)} %get-tuple-element.28.mine_ref, f32[288,256]{1,0:T(8,128)} %copy-done.5), custom_call_target="tpu_custom_call" | custom-call | flops 1 | bytes 1 | tf_op jit(solution)/shard_map/low_and_maps/pallas_call | solution.py:274
  34.3 1.2 %collective-permute-start.8 = (bf16[288,256]{1,0:T(8,128)(2,1)}, bf16[288,256]{1,0:T(8,128)(2,1)S(1)}, u32[]{:S(2)}, u32[]{:S(2)}) collective-permute-start(bf16[288,256]{1,0:T(8,128)(2,1)} %low_and_maps.1.low_ref.map_ref), channel_id=1, source_target_pairs={{0,16},{8,24},{16,0},{24,8},{1,17},{9,25},{17,1},{25,9},{2,18},{10... | collective-permute-start | bytes 442376 | tf_op jit(solution)/shard_map/ppermute | solution.py:803
  35.5 9.1 %scan_own.1 = (bf16[512,1024]{1,0:T(8,128)(2,1)}, bf16[512,1024]{1,0:T(8,128)(2,1)}, f32[4,32,128]{2,1,0:T(8,128)}, f32[16,1024]{1,0:T(8,128)}, f32[1,1024]{1,0:T(1,128)}) custom-call(s32[2]{0:T(128)} %pad_add_fusion.place_ref, bf16[1,256,1024]{2,1,0:T(8,128)(2,1)} %get-tuple-element.25.stayed_ref.stream_ref, bf16[288,256]{1,0:T(8,128)(2,1)} %low_and_maps.1.low_ref.map_ref, ...), custom_call_target="tpu_custom_call" | custom-call | flops 4000000000 | bytes 2097152 | tf_op jit(solution)/shard_map/scan_own/pallas_call | solution.py:561
  44.7 0.0 collective-permute-done.5
  44.7 0.0 copy-start.3
  44.7 0.0 collective-permute-done.6.got_stayed_ref
  44.7 0.0 copy-start.4
  44.7 0.0 collective-permute-done.4.got_sent_ref
  44.7 0.8 %copy-done.4 = bf16[1,256,1024]{2,1,0:T(8,128)(2,1)} copy-done((bf16[1,256,1024]{2,1,0:T(8,128)(2,1)}, bf16[1,256,1024]{2,1,0:T(8,128)(2,1)S(1)}, u32[]{:S(2)}) %copy-start.4) | copy-done | bytes 524312
  45.5 2.2 %join_heads.1.rest_2_ = bf16[128,4096]{1,0:T(8,128)(2,1)} custom-call(bf16[1,256,1024]{2,1,0:T(8,128)(2,1)} %get-tuple-element.24.sent_ref, bf16[1,256,1024]{2,1,0:T(8,128)(2,1)} %get-tuple-element.25.stayed_ref.stream_ref, bf16[1,256,1024]{2,1,0:T(8,128)(2,1)} %collective-permute-done.4.got_sent_ref, bf16[1,256,1024]{2,1,0:T(8,128)(2,1)} %copy-done.4), custom_call_target="tpu_custom_call" | custom-call | tf_op jit(solution)/shard_map/join_heads/pallas_call | solution.py:90
  47.7 0.0 collective-permute-done.8
  47.7 0.0 copy-start.2
  47.7 0.0 copy-done.3
  47.7 0.6 copy-done.2
  48.4 6.6 %step_sizes.1 = (bf16[256,1024]{1,0:T(8,128)(2,1)}, bf16[512,1024]{1,0:T(8,128)(2,1)}, f32[4,32,128]{2,1,0:T(8,128)}, bf16[8,144,128]{2,1,0:T(8,128)(2,1)}) custom-call(s32[2]{0:T(128)} %pad_add_fusion.place_ref, bf16[1,256,1024]{2,1,0:T(8,128)(2,1)} %bitcast.19, bf16[1,288,256]{2,1,0:T(8,128)(2,1)} %bitcast.17, ...), custom_call_target="tpu_custom_call", output_to_operand_aliasing={{1}: (10, {}), {2}: (11, {})} | custom-call | tf_op jit(solution)/shard_map/step_sizes/pallas_call | solution.py:401
  55.0 5.8 %all-to-all-start = ((bf16[8,144,128]{2,1,0:T(8,128)(2,1)}), bf16[8,144,128]{2,1,0:T(8,128)(2,1)S(1)}, u32[]{:S(2)}, u32[]{:S(2)}) async-start(bf16[8,144,128]{2,1,0:T(8,128)(2,1)} %get-tuple-element.39), calls=%async_computation | async-start | bytes 589824 | tf_op jit(solution)/shard_map/all_to_all | solution.py:814
  60.8 8.0 %scan_others.1 = (bf16[512,1024]{1,0:T(8,128)(2,1)}, f32[1,16,1024]{2,1,0:T(8,128)}) custom-call(s32[2]{0:T(128)} %pad_add_fusion.place_ref, bf16[1,256,1024]{2,1,0:T(8,128)(2,1)} %bitcast.20, bf16[256,1024]{1,0:T(8,128)(2,1)} %get-tuple-element.33.steps_ref, f32[4,32,128]{2,1,0:T(8,128)} %get-tuple-element.34.maps_ref, ...), custom_call_target="tpu_custom_call", output_to_operand_aliasing={{0}: (6, {})} | custom-call | flops 4000000000 | bytes 2097152 | tf_op jit(solution)/shard_map/scan_others/pallas_call | solution.py:627
  68.8 1.6 %all-to-all-done.carries_ref = bf16[8,144,128]{2,1,0:T(8,128)(2,1)S(1)} async-done(((bf16[8,144,128]{2,1,0:T(8,128)(2,1)}), bf16[8,144,128]{2,1,0:T(8,128)(2,1)S(1)}, u32[]{:S(2)}, u32[]{:S(2)}) %all-to-all-start) | async-done | bytes 294944 | tf_op jit(solution)/shard_map/all_to_all | solution.py:814
  70.4 0.7 copy-done.1
  71.1 9.2 %add_carried.1 = bf16[512,1024]{1,0:T(8,128)(2,1)} custom-call(s32[2]{0:T(128)} %pad_add_fusion.place_ref, bf16[512,1024]{1,0:T(8,128)(2,1)} %get-tuple-element.36.part_ref, bf16[512,1024]{1,0:T(8,128)(2,1)} %get-tuple-element.37.sums_ref, f32[4,32,128]{2,1,0:T(8,128)} %get-tuple-element.34.maps_ref, f32[16,1024]{1,0:T(8,128)} %get-tuple-element.29.rest_0_.last_own_ref, ...), custom_call_target="tpu_custom_call" | custom-call | tf_op jit(solution)/shard_map/add_carried/pallas_call | solution.py:732
  (1 shorter events, 0.0 us)
Async XLA Ops:
  0.6 14.2 %copy-start = (bf16[256,4096]{1,0:T(8,128)(2,1)S(1)}, bf16[256,4096]{1,0:T(8,128)(2,1)}, u32[]{:S(2)}) copy-start(bf16[256,4096]{1,0:T(8,128)(2,1)} %param.16) | copy-start | bytes 6291460
  2.7 17.0 %collective-permute-start = (bf16[128,4096]{1,0:T(8,128)(2,1)}, bf16[128,4096]{1,0:T(8,128)(2,1)S(1)}, u32[]{:S(2)}, u32[]{:S(2)}) collective-permute-start(bf16[128,4096]{1,0:T(8,128)(2,1)} %bitcast.30), channel_id=1, source_target_pairs={{0,8},{8,0},{16,24},{24,16},{1,9},{9,1},{17,25},{25,17},{2,10},{10... | collective-permute-start | bytes 3145736 | tf_op jit(solution)/shard_map/ppermute | solution.py:787
  3.3 12.4 %collective-permute-start.3 = (bf16[2,2,128,256]{3,2,1,0:T(8,128)(2,1)}, bf16[2,2,128,256]{3,2,1,0:T(8,128)(2,1)S(1)}, u32[]{:S(2)}, u32[]{:S(2)}) collective-permute-start(bf16[2,2,128,256]{3,2,1,0:T(8,128)(2,1)} %get-tuple-element.23), channel_id=1, source_target_pairs={{0,24},{8,16},{1,25},{9,17},{2,26},{10,18},{3,27},{11,19},{4,28},{... | collective-permute-start | bytes 786440 | tf_op jit(solution)/shard_map/ppermute | solution.py:784
  7.8 7.9 %collective-permute-start.1 = (bf16[2,2,128,256]{3,2,1,0:T(8,128)(2,1)}, bf16[2,2,128,256]{3,2,1,0:T(8,128)(2,1)}, u32[]{:S(2)}, u32[]{:S(2)}) collective-permute-start(bf16[2,2,128,256]{3,2,1,0:T(8,128)(2,1)} %get-tuple-element.23), channel_id=1, source_target_pairs={{0,8},{8,0},{16,24},{24,16},{1,9},{9,1},{17,25},{25,17},{2,10},{10... | collective-permute-start | bytes 786440 | tf_op jit(solution)/shard_map/ppermute | solution.py:785
  7.9 11.8 %collective-permute-start.2 = (bf16[2,2,128,256]{3,2,1,0:T(8,128)(2,1)}, bf16[2,2,128,256]{3,2,1,0:T(8,128)(2,1)}, u32[]{:S(2)}, u32[]{:S(2)}) collective-permute-start(bf16[2,2,128,256]{3,2,1,0:T(8,128)(2,1)} %get-tuple-element.21.own_ref), channel_id=1, source_target_pairs={{0,16},{8,24},{1,17},{9,25},{2,18},{10,26},{3,19},{11,27},{4,20},{... | collective-permute-start | bytes 786440 | tf_op jit(solution)/shard_map/ppermute | solution.py:783
  15.7 4.1 %copy-start.7 = (bf16[2,2,128,256]{3,2,1,0:T(8,128)(2,1)}, bf16[2,2,128,256]{3,2,1,0:T(8,128)(2,1)S(1)}, u32[]{:S(2)}) copy-start(bf16[2,2,128,256]{3,2,1,0:T(8,128)(2,1)S(1)} %collective-permute-done.3.far_ref) | copy-start | bytes 786436
  19.7 1.0 %copy-start.6 = (bf16[128,4096]{1,0:T(8,128)(2,1)}, bf16[128,4096]{1,0:T(8,128)(2,1)S(1)}, u32[]{:S(2)}) copy-start(bf16[128,4096]{1,0:T(8,128)(2,1)S(1)} %collective-permute-done.theirs_ref) | copy-start | bytes 3145732
  28.7 3.1 %collective-permute-start.7 = (f32[288,256]{1,0:T(8,128)}, f32[288,256]{1,0:T(8,128)S(1)}, u32[]{:S(2)}, u32[]{:S(2)}) collective-permute-start(f32[288,256]{1,0:T(8,128)} %get-tuple-element.28.mine_ref), channel_id=1, source_target_pairs={{0,8},{8,0},{16,24},{24,16},{1,9},{9,1},{17,25},{25,17},{2,10},{10... | collective-permute-start | bytes 884744 | tf_op jit(solution)/shard_map/ppermute | solution.py:802
  28.8 15.8 %collective-permute-start.5 = (bf16[256,1024]{1,0:T(8,128)(2,1)}, bf16[256,1024]{1,0:T(8,128)(2,1)S(1)}, u32[]{:S(2)}, u32[]{:S(2)}) collective-permute-start(bf16[256,1024]{1,0:T(8,128)(2,1)} %bitcast.21), channel_id=1, source_target_pairs={{0,16},{8,24},{16,0},{24,8},{1,17},{9,25},{17,1},{25,9},{2,18},{10... | collective-permute-start | bytes 1572872 | tf_op jit(solution)/shard_map/ppermute | solution.py:801
  31.4 13.3 %collective-permute-start.6 = (bf16[1,256,1024]{2,1,0:T(8,128)(2,1)}, bf16[1,256,1024]{2,1,0:T(8,128)(2,1)S(1)}, u32[]{:S(2)}, u32[]{:S(2)}) collective-permute-start(bf16[1,256,1024]{2,1,0:T(8,128)(2,1)} %get-tuple-element.25.stayed_ref.stream_ref), channel_id=1, source_target_pairs={{0,8},{8,0},{16,24},{24,16},{1,9},{9,1},{17,25},{25,17},{2,10},{10... | collective-permute-start | bytes 1572872 | tf_op jit(solution)/shard_map/ppermute | solution.py:805
  31.5 13.2 %collective-permute-start.4 = (bf16[1,256,1024]{2,1,0:T(8,128)(2,1)}, bf16[1,256,1024]{2,1,0:T(8,128)(2,1)}, u32[]{:S(2)}, u32[]{:S(2)}) collective-permute-start(bf16[1,256,1024]{2,1,0:T(8,128)(2,1)} %get-tuple-element.24.sent_ref), channel_id=1, source_target_pairs={{0,8},{8,0},{16,24},{24,16},{1,9},{9,1},{17,25},{25,17},{2,10},{10... | collective-permute-start | bytes 1572872 | tf_op jit(solution)/shard_map/ppermute | solution.py:804
  31.9 0.7 copy-start.5
  34.3 13.4 %collective-permute-start.8 = (bf16[288,256]{1,0:T(8,128)(2,1)}, bf16[288,256]{1,0:T(8,128)(2,1)S(1)}, u32[]{:S(2)}, u32[]{:S(2)}) collective-permute-start(bf16[288,256]{1,0:T(8,128)(2,1)} %low_and_maps.1.low_ref.map_ref), channel_id=1, source_target_pairs={{0,16},{8,24},{16,0},{24,8},{1,17},{9,25},{17,1},{25,9},{2,18},{10... | collective-permute-start | bytes 442376 | tf_op jit(solution)/shard_map/ppermute | solution.py:803
  44.7 3.1 %copy-start.3 = (bf16[256,1024]{1,0:T(8,128)(2,1)}, bf16[256,1024]{1,0:T(8,128)(2,1)S(1)}, u32[]{:S(2)}) copy-start(bf16[256,1024]{1,0:T(8,128)(2,1)S(1)} %collective-permute-done.5) | copy-start | bytes 1572868
  44.7 0.8 %copy-start.4 = (bf16[1,256,1024]{2,1,0:T(8,128)(2,1)}, bf16[1,256,1024]{2,1,0:T(8,128)(2,1)S(1)}, u32[]{:S(2)}) copy-start(bf16[1,256,1024]{2,1,0:T(8,128)(2,1)S(1)} %collective-permute-done.6.got_stayed_ref) | copy-start | bytes 1572868
  47.7 0.7 copy-start.2
  55.0 15.5 %all-to-all-start = ((bf16[8,144,128]{2,1,0:T(8,128)(2,1)}), bf16[8,144,128]{2,1,0:T(8,128)(2,1)S(1)}, u32[]{:S(2)}, u32[]{:S(2)}) async-start(bf16[8,144,128]{2,1,0:T(8,128)(2,1)} %get-tuple-element.39), calls=%async_computation | async-start | bytes 589824 | tf_op jit(solution)/shard_map/all_to_all | solution.py:814
  70.4 0.7 copy-start.1

commit v7 on v6

--- a/solution.py
+++ b/solution.py
@@ -22,6 +22,7 @@
 
 masked_fill = -1e30
 params = pltpu.CompilerParams(vmem_limit_bytes=60 << 20)
+less = pltpu.CompilerParams(vmem_limit_bytes=16 << 20)
 
 
 def split(value):
@@ -94,7 +95,7 @@
             (rows // CORES, (others + 1) * CORES * width), sent.dtype
         ),
         scratch_shapes=[pltpu.SemaphoreType.DMA((CORES * (others + 1),))],
-        compiler_params=params,
+        compiler_params=less,
         name="join_heads",
     )(sent, stayed, got_sent, got_stayed)
 

time: 80.9 us -> 80.4 us (level)
  transfers between devices with their start and end apart: 10 -> 10, of which waited for: 2 -> 3; matrix products, arithmetic and copies ran while one was open for 7% -> 7% of each run, Pallas kernels for 26% -> 26%
where the time goes in v7:
time: 80.4 us; the launch traced here: 79.8 us
  Pallas kernels  46.8 us (58%)
  starting transfers between devices  17.6 us (22%)
  local copies, waits for them, and re-layouts  6.44 us (8%)
  waiting for transfers between devices  6.16 us (8%)
  other arithmetic  2.08 us (3%)
    pallas_call x1, Pallas kernels, add_carried(): pl.pallas_call(carried_kernel, grid_spec=pltpu.PrefetchScalarGridSpec(num...  9.17 us
    pallas_call x1, Pallas kernels, scan_own(): pl.pallas_call(own_kernel, grid_spec=pltpu.PrefetchScalarGridSpec(num_sca...  9.14 us
    pallas_call x1, Pallas kernels, attend(): pl.pallas_call(functools.partial(attend_kernel, chips=chips), grid_spec=p...  8.03 us
    pallas_call x1, Pallas kernels, scan_others(): pl.pallas_call(others_kernel, grid_spec=pltpu.PrefetchScalarGridSpec(num_...  8.01 us
    pallas_call x1, Pallas kernels, step_sizes(): pl.pallas_call(step_kernel, grid_spec=pltpu.PrefetchScalarGridSpec(num_sc...  6.58 us
    all_to_all x1, starting transfers between devices, local(): lax.all_to_all(carry, 'chan', split_axis=0, concat_axis=0, tiled=True)  5.82 us
    ppermute x1, starting transfers between devices, local(): from_far = lax.ppermute(theirs, 'seq', far)  4.54 us
    ppermute x1, waiting for transfers between devices, local(): from_near = lax.ppermute(own, 'seq', near)  4.03 us
  transfers between devices with their start and end apart: 10, of which 3 were waited for; matrix products, arithmetic and copies ran while one was open for 7% of the time, Pallas kernels for 26%

profile of v7, /device:TPU:0, one launch (start us, length us, event | category | flops | bytes accessed | tf_op | source)
XLA Modules:
  0.0 79.8 jit_solution(13559731608698188619)
XLA Ops:
  0.6 0.0 copy-start
  0.6 2.1 %select_heads.1 = (bf16[2,2,128,256]{3,2,1,0:T(8,128)(2,1)}, bf16[2,2,128,256]{3,2,1,0:T(8,128)(2,1)}) custom-call(bf16[128,1024]{1,0:T(8,128)(2,1)} %bitcast.20, bf16[128,1024]{1,0:T(8,128)(2,1)} %bitcast.21), custom_call_target="tpu_custom_call" | custom-call | tf_op jit(solution)/shard_map/select_heads/pallas_call | solution.py:62
  2.7 0.5 collective-permute-start
  3.3 4.5 %collective-permute-start.3 = (bf16[2,2,128,256]{3,2,1,0:T(8,128)(2,1)}, bf16[2,2,128,256]{3,2,1,0:T(8,128)(2,1)S(1)}, u32[]{:S(2)}, u32[]{:S(2)}) collective-permute-start(bf16[2,2,128,256]{3,2,1,0:T(8,128)(2,1)} %get-tuple-element.23), channel_id=1, source_target_pairs={{0,24},{8,16},{1,25},{9,17},{2,26},{10,18},{3,27},{11,19},{4,28},{... | collective-permute-start | bytes 786440 | tf_op jit(solution)/shard_map/ppermute | solution.py:785
  7.8 0.1 collective-permute-start.1
  7.9 2.3 %collective-permute-start.2 = (bf16[2,2,128,256]{3,2,1,0:T(8,128)(2,1)}, bf16[2,2,128,256]{3,2,1,0:T(8,128)(2,1)}, u32[]{:S(2)}, u32[]{:S(2)}) collective-permute-start(bf16[2,2,128,256]{3,2,1,0:T(8,128)(2,1)} %get-tuple-element.21.own_ref), channel_id=1, source_target_pairs={{0,16},{8,24},{1,17},{9,25},{2,18},{10,26},{3,19},{11,27},{4,20},{... | collective-permute-start | bytes 786440 | tf_op jit(solution)/shard_map/ppermute | solution.py:784
  10.2 0.6 pad_add_fusion.place_ref
  10.8 1.3 %dynamic_slice.14 = f32[1024]{0:T(1024)} dynamic-slice(f32[4096]{0:T(1024)} %param.17, s32[]{:T(128)S(6)} %select_n.12), dynamic_slice_sizes={1024} | dynamic-slice | bytes 8196 | tf_op jit(solution)/shard_map/dynamic_slice | solution.py:795
  12.1 1.3 %dynamic_slice.15 = f32[1024]{0:T(1024)} dynamic-slice(f32[4096]{0:T(1024)} %param.19, s32[]{:T(128)S(6)} %select_n.12), dynamic_slice_sizes={1024} | dynamic-slice | bytes 8196 | tf_op jit(solution)/shard_map/dynamic_slice | solution.py:796
  13.4 1.5 %multiply_bitcast_fusion.rest_0_.rates_ref = f32[16,1024]{1,0:T(8,128)} fusion(f32[4096,16]{0,1:T(8,128)} %param.18, s32[]{:T(128)S(6)} %select_n.12), kind=kLoop, calls=%fused_computation | loop fusion | flops 16384 | bytes 131076 | tf_op jit(solution)/shard_map/transpose | solution.py:793
  14.9 0.0 copy-done
  14.9 0.8 %constant_dynamic-slice_fusion.rest_1_.cols_ref = bf16[256,1024]{1,0:T(8,128)(2,1)} fusion(bf16[256,4096]{1,0:T(8,128)(2,1)S(1)} %copy-done, s32[]{:T(128)S(6)} %select_n.12), kind=kLoop, calls=%fused_computation.2 | loop fusion | bytes 1048580 | tf_op jit(solution)/shard_map/dynamic_slice | solution.py:794
  15.7 0.0 collective-permute-done.3.far_ref
  15.7 0.0 copy-start.7
  15.7 0.0 collective-permute-done.1.swap_ref
  15.7 4.0 %collective-permute-done.2.near_ref = bf16[2,2,128,256]{3,2,1,0:T(8,128)(2,1)} collective-permute-done((bf16[2,2,128,256]{3,2,1,0:T(8,128)(2,1)}, bf16[2,2,128,256]{3,2,1,0:T(8,128)(2,1)}, u32[]{:S(2)}, u32[]{:S(2)}) %collective-permute-start.2) | collective-permute-done | bytes 262176 | tf_op jit(solution)/shard_map/ppermute | solution.py:784
  19.7 0.0 collective-permute-done.theirs_ref
  19.7 0.0 copy-start.6
  19.7 0.0 copy-done.7
  19.7 1.0 %copy-done.6 = bf16[128,4096]{1,0:T(8,128)(2,1)} copy-done((bf16[128,4096]{1,0:T(8,128)(2,1)}, bf16[128,4096]{1,0:T(8,128)(2,1)S(1)}, u32[]{:S(2)}) %copy-start.6) | copy-done | bytes 1048600
  20.7 8.0 %attend.1 = (bf16[1,256,1024]{2,1,0:T(8,128)(2,1)}, bf16[1,256,1024]{2,1,0:T(8,128)(2,1)}, f32[288,256]{1,0:T(8,128)}) custom-call(s32[2]{0:T(128)} %pad_add_fusion.place_ref, s32[1,16]{1,0:T(1,128)} %doc_ref.1, bf16[128,4096]{1,0:T(8,128)(2,1)} %bitcast.29, bf16[128,4096]{1,0:T(8,128)(2,1)} %copy-done.6, ...), custom_call_target="tpu_custom_call" | custom-call | flops 5000000000 | bytes 4194304 | tf_op jit(solution)/shard_map/attend/pallas_call | solution.py:237
  28.7 0.1 collective-permute-start.7
  28.8 2.5 %collective-permute-start.5 = (bf16[256,1024]{1,0:T(8,128)(2,1)}, bf16[256,1024]{1,0:T(8,128)(2,1)}, u32[]{:S(2)}, u32[]{:S(2)}) collective-permute-start(bf16[256,1024]{1,0:T(8,128)(2,1)} %bitcast.15), channel_id=1, source_target_pairs={{0,16},{8,24},{16,0},{24,8},{1,17},{9,25},{17,1},{25,9},{2,18},{10... | collective-permute-start | bytes 1572872 | tf_op jit(solution)/shard_map/ppermute | solution.py:802
  31.4 0.2 collective-permute-start.6
  31.5 0.3 collective-permute-start.4
  31.9 0.0 collective-permute-done.7.theirs_ref
  31.9 0.0 copy-start.5
  31.9 0.7 copy-done.5
  32.6 1.7 %low_and_maps.1.low_ref.map_ref = bf16[288,256]{1,0:T(8,128)(2,1)} custom-call(f32[288,256]{1,0:T(8,128)} %get-tuple-element.28.mine_ref, f32[288,256]{1,0:T(8,128)} %copy-done.5), custom_call_target="tpu_custom_call" | custom-call | flops 1 | bytes 1 | tf_op jit(solution)/shard_map/low_and_maps/pallas_call | solution.py:275
  34.3 0.0 copy-start.1
  34.3 0.0 copy-start.2
  34.3 1.2 %collective-permute-start.8 = (bf16[288,256]{1,0:T(8,128)(2,1)}, bf16[288,256]{1,0:T(8,128)(2,1)S(1)}, u32[]{:S(2)}, u32[]{:S(2)}) collective-permute-start(bf16[288,256]{1,0:T(8,128)(2,1)} %low_and_maps.1.low_ref.map_ref), channel_id=1, source_target_pairs={{0,16},{8,24},{16,0},{24,8},{1,17},{9,25},{17,1},{25,9},{2,18},{10... | collective-permute-start | bytes 442376 | tf_op jit(solution)/shard_map/ppermute | solution.py:804
  35.5 9.1 %scan_own.1 = (bf16[512,1024]{1,0:T(8,128)(2,1)}, bf16[512,1024]{1,0:T(8,128)(2,1)}, f32[4,32,128]{2,1,0:T(8,128)}, f32[16,1024]{1,0:T(8,128)}, f32[1,1024]{1,0:T(1,128)}) custom-call(s32[2]{0:T(128)} %pad_add_fusion.place_ref, bf16[1,256,1024]{2,1,0:T(8,128)(2,1)} %get-tuple-element.25.stayed_ref.stream_ref, bf16[288,256]{1,0:T(8,128)(2,1)} %low_and_maps.1.low_ref.map_ref, ...), custom_call_target="tpu_custom_call" | custom-call | flops 4000000000 | bytes 2097152 | tf_op jit(solution)/shard_map/scan_own/pallas_call | solution.py:562
  44.7 0.0 collective-permute-done.5
  44.7 0.0 collective-permute-done.6.got_stayed_ref
  44.7 0.0 collective-permute-done.4.got_sent_ref
  44.7 0.0 copy-done.1
  44.7 0.0 copy-done.2
  44.7 2.0 %join_heads.1.rest_2_ = bf16[128,4096]{1,0:T(8,128)(2,1)} custom-call(bf16[1,256,1024]{2,1,0:T(8,128)(2,1)S(1)} %copy-done.1, bf16[1,256,1024]{2,1,0:T(8,128)(2,1)S(1)} %copy-done.2, bf16[1,256,1024]{2,1,0:T(8,128)(2,1)} %collective-permute-done.4.got_sent_ref, bf16[1,256,1024]{2,1,0:T(8,128)(2,1)S(1)} %collective-permute-done.6.got_stayed_ref), custom_call_target="tpu_custom_call" | custom-call | tf_op jit(solution)/shard_map/join_heads/pallas_call | solution.py:91
  46.8 0.5 collective-permute-done.8
  47.3 0.0 copy-start.4
  47.3 0.7 copy-done.4
  47.9 6.6 %step_sizes.1 = (bf16[256,1024]{1,0:T(8,128)(2,1)}, bf16[512,1024]{1,0:T(8,128)(2,1)}, f32[4,32,128]{2,1,0:T(8,128)}, bf16[8,144,128]{2,1,0:T(8,128)(2,1)}) custom-call(s32[2]{0:T(128)} %pad_add_fusion.place_ref, bf16[1,256,1024]{2,1,0:T(8,128)(2,1)} %bitcast.11.stream_ref, ...), custom_call_target="tpu_custom_call", output_to_operand_aliasing={{1}: (10, {}), {2}: (11, {})} | custom-call | tf_op jit(solution)/shard_map/step_sizes/pallas_call | solution.py:402
  54.5 5.8 %all-to-all-start = ((bf16[8,144,128]{2,1,0:T(8,128)(2,1)}), bf16[8,144,128]{2,1,0:T(8,128)(2,1)S(1)}, u32[]{:S(2)}, u32[]{:S(2)}) async-start(bf16[8,144,128]{2,1,0:T(8,128)(2,1)} %get-tuple-element.39), calls=%async_computation | async-start | bytes 589824 | tf_op jit(solution)/shard_map/all_to_all | solution.py:815
  60.3 8.0 %scan_others.1 = (bf16[512,1024]{1,0:T(8,128)(2,1)}, f32[1,16,1024]{2,1,0:T(8,128)}) custom-call(s32[2]{0:T(128)} %pad_add_fusion.place_ref, bf16[1,256,1024]{2,1,0:T(8,128)(2,1)} %bitcast.11.stream_ref, bf16[256,1024]{1,0:T(8,128)(2,1)} %get-tuple-element.33.steps_ref, f32[4,32,128]{2,1,0:T(8,128)} %get-tuple-element.34.maps_ref, ...), custom_call_target="tpu_custom_call", output_to_operand_aliasing={{0}: (6, {})} | custom-call | flops 4000000000 | bytes 2097152 | tf_op jit(solution)/shard_map/scan_others/pallas_call | solution.py:628
  68.3 1.6 %all-to-all-done.carries_ref = bf16[8,144,128]{2,1,0:T(8,128)(2,1)S(1)} async-done(((bf16[8,144,128]{2,1,0:T(8,128)(2,1)}), bf16[8,144,128]{2,1,0:T(8,128)(2,1)S(1)}, u32[]{:S(2)}, u32[]{:S(2)}) %all-to-all-start) | async-done | bytes 294944 | tf_op jit(solution)/shard_map/all_to_all | solution.py:815
  70.0 0.7 copy-done.3
  70.7 9.2 %add_carried.1 = bf16[512,1024]{1,0:T(8,128)(2,1)} custom-call(s32[2]{0:T(128)} %pad_add_fusion.place_ref, bf16[512,1024]{1,0:T(8,128)(2,1)} %get-tuple-element.36.part_ref, bf16[512,1024]{1,0:T(8,128)(2,1)} %get-tuple-element.37.sums_ref, f32[4,32,128]{2,1,0:T(8,128)} %get-tuple-element.34.maps_ref, f32[16,1024]{1,0:T(8,128)} %get-tuple-element.29.rest_0_.last_own_ref, ...), custom_call_target="tpu_custom_call" | custom-call | tf_op jit(solution)/shard_map/add_carried/pallas_call | solution.py:733
  (1 shorter events, 0.0 us)
Async XLA Ops:
  0.6 14.2 %copy-start = (bf16[256,4096]{1,0:T(8,128)(2,1)S(1)}, bf16[256,4096]{1,0:T(8,128)(2,1)}, u32[]{:S(2)}) copy-start(bf16[256,4096]{1,0:T(8,128)(2,1)} %param.16) | copy-start | bytes 6291460
  2.7 17.0 %collective-permute-start = (bf16[128,4096]{1,0:T(8,128)(2,1)}, bf16[128,4096]{1,0:T(8,128)(2,1)S(1)}, u32[]{:S(2)}, u32[]{:S(2)}) collective-permute-start(bf16[128,4096]{1,0:T(8,128)(2,1)} %bitcast.28), channel_id=1, source_target_pairs={{0,8},{8,0},{16,24},{24,16},{1,9},{9,1},{17,25},{25,17},{2,10},{10... | collective-permute-start | bytes 3145736 | tf_op jit(solution)/shard_map/ppermute | solution.py:788
  3.3 12.4 %collective-permute-start.3 = (bf16[2,2,128,256]{3,2,1,0:T(8,128)(2,1)}, bf16[2,2,128,256]{3,2,1,0:T(8,128)(2,1)S(1)}, u32[]{:S(2)}, u32[]{:S(2)}) collective-permute-start(bf16[2,2,128,256]{3,2,1,0:T(8,128)(2,1)} %get-tuple-element.23), channel_id=1, source_target_pairs={{0,24},{8,16},{1,25},{9,17},{2,26},{10,18},{3,27},{11,19},{4,28},{... | collective-permute-start | bytes 786440 | tf_op jit(solution)/shard_map/ppermute | solution.py:785
  7.8 7.9 %collective-permute-start.1 = (bf16[2,2,128,256]{3,2,1,0:T(8,128)(2,1)}, bf16[2,2,128,256]{3,2,1,0:T(8,128)(2,1)}, u32[]{:S(2)}, u32[]{:S(2)}) collective-permute-start(bf16[2,2,128,256]{3,2,1,0:T(8,128)(2,1)} %get-tuple-element.23), channel_id=1, source_target_pairs={{0,8},{8,0},{16,24},{24,16},{1,9},{9,1},{17,25},{25,17},{2,10},{10... | collective-permute-start | bytes 786440 | tf_op jit(solution)/shard_map/ppermute | solution.py:786
  7.9 11.8 %collective-permute-start.2 = (bf16[2,2,128,256]{3,2,1,0:T(8,128)(2,1)}, bf16[2,2,128,256]{3,2,1,0:T(8,128)(2,1)}, u32[]{:S(2)}, u32[]{:S(2)}) collective-permute-start(bf16[2,2,128,256]{3,2,1,0:T(8,128)(2,1)} %get-tuple-element.21.own_ref), channel_id=1, source_target_pairs={{0,16},{8,24},{1,17},{9,25},{2,18},{10,26},{3,19},{11,27},{4,20},{... | collective-permute-start | bytes 786440 | tf_op jit(solution)/shard_map/ppermute | solution.py:784
  15.7 4.0 %copy-start.7 = (bf16[2,2,128,256]{3,2,1,0:T(8,128)(2,1)}, bf16[2,2,128,256]{3,2,1,0:T(8,128)(2,1)S(1)}, u32[]{:S(2)}) copy-start(bf16[2,2,128,256]{3,2,1,0:T(8,128)(2,1)S(1)} %collective-permute-done.3.far_ref) | copy-start | bytes 786436
  19.7 1.0 %copy-start.6 = (bf16[128,4096]{1,0:T(8,128)(2,1)}, bf16[128,4096]{1,0:T(8,128)(2,1)S(1)}, u32[]{:S(2)}) copy-start(bf16[128,4096]{1,0:T(8,128)(2,1)S(1)} %collective-permute-done.theirs_ref) | copy-start | bytes 3145732
  28.7 3.1 %collective-permute-start.7 = (f32[288,256]{1,0:T(8,128)}, f32[288,256]{1,0:T(8,128)S(1)}, u32[]{:S(2)}, u32[]{:S(2)}) collective-permute-start(f32[288,256]{1,0:T(8,128)} %get-tuple-element.28.mine_ref), channel_id=1, source_target_pairs={{0,8},{8,0},{16,24},{24,16},{1,9},{9,1},{17,25},{25,17},{2,10},{10... | collective-permute-start | bytes 884744 | tf_op jit(solution)/shard_map/ppermute | solution.py:803
  28.8 15.9 %collective-permute-start.5 = (bf16[256,1024]{1,0:T(8,128)(2,1)}, bf16[256,1024]{1,0:T(8,128)(2,1)}, u32[]{:S(2)}, u32[]{:S(2)}) collective-permute-start(bf16[256,1024]{1,0:T(8,128)(2,1)} %bitcast.15), channel_id=1, source_target_pairs={{0,16},{8,24},{16,0},{24,8},{1,17},{9,25},{17,1},{25,9},{2,18},{10... | collective-permute-start | bytes 1572872 | tf_op jit(solution)/shard_map/ppermute | solution.py:802
  31.4 13.3 %collective-permute-start.6 = (bf16[1,256,1024]{2,1,0:T(8,128)(2,1)}, bf16[1,256,1024]{2,1,0:T(8,128)(2,1)S(1)}, u32[]{:S(2)}, u32[]{:S(2)}) collective-permute-start(bf16[1,256,1024]{2,1,0:T(8,128)(2,1)} %get-tuple-element.25.stayed_ref.stream_ref), channel_id=1, source_target_pairs={{0,8},{8,0},{16,24},{24,16},{1,9},{9,1},{17,25},{25,17},{2,10},{10... | collective-permute-start | bytes 1572872 | tf_op jit(solution)/shard_map/ppermute | solution.py:806
  31.5 13.2 %collective-permute-start.4 = (bf16[1,256,1024]{2,1,0:T(8,128)(2,1)}, bf16[1,256,1024]{2,1,0:T(8,128)(2,1)}, u32[]{:S(2)}, u32[]{:S(2)}) collective-permute-start(bf16[1,256,1024]{2,1,0:T(8,128)(2,1)} %get-tuple-element.24.sent_ref), channel_id=1, source_target_pairs={{0,8},{8,0},{16,24},{24,16},{1,9},{9,1},{17,25},{25,17},{2,10},{10... | collective-permute-start | bytes 1572872 | tf_op jit(solution)/shard_map/ppermute | solution.py:805
  31.9 0.7 copy-start.5
  34.3 10.4 %copy-start.1 = (bf16[1,256,1024]{2,1,0:T(8,128)(2,1)S(1)}, bf16[1,256,1024]{2,1,0:T(8,128)(2,1)}, u32[]{:S(2)}) copy-start(bf16[1,256,1024]{2,1,0:T(8,128)(2,1)} %get-tuple-element.24.sent_ref) | copy-start | bytes 1572868
  34.3 10.4 %copy-start.2 = (bf16[1,256,1024]{2,1,0:T(8,128)(2,1)S(1)}, bf16[1,256,1024]{2,1,0:T(8,128)(2,1)}, u32[]{:S(2)}) copy-start(bf16[1,256,1024]{2,1,0:T(8,128)(2,1)} %get-tuple-element.25.stayed_ref.stream_ref) | copy-start | bytes 1572868
  34.3 12.9 %collective-permute-start.8 = (bf16[288,256]{1,0:T(8,128)(2,1)}, bf16[288,256]{1,0:T(8,128)(2,1)S(1)}, u32[]{:S(2)}, u32[]{:S(2)}) collective-permute-start(bf16[288,256]{1,0:T(8,128)(2,1)} %low_and_maps.1.low_ref.map_ref), channel_id=1, source_target_pairs={{0,16},{8,24},{16,0},{24,8},{1,17},{9,25},{17,1},{25,9},{2,18},{10... | collective-permute-start | bytes 442376 | tf_op jit(solution)/shard_map/ppermute | solution.py:804
  47.3 0.7 copy-start.4
  54.5 15.5 %all-to-all-start = ((bf16[8,144,128]{2,1,0:T(8,128)(2,1)}), bf16[8,144,128]{2,1,0:T(8,128)(2,1)S(1)}, u32[]{:S(2)}, u32[]{:S(2)}) async-start(bf16[8,144,128]{2,1,0:T(8,128)(2,1)} %get-tuple-element.39), calls=%async_computation | async-start | bytes 589824 | tf_op jit(solution)/shard_map/all_to_all | solution.py:815
  70.0 0.7 copy-start.3

commit v8 on v7

--- a/solution.py
+++ b/solution.py
@@ -275,7 +275,7 @@
     return pl.pallas_call(
         low_kernel,
         out_shape=jax.ShapeDtypeStruct(mine.shape, jnp.bfloat16),
-        compiler_params=params,
+        compiler_params=less,
         cost_estimate=pl.CostEstimate(flops=1, bytes_accessed=1, transcendentals=0),
         name="low_and_maps",
     )(mine, theirs)

time: 80.4 us -> 80.5 us (level)
  Pallas kernels: 46.8 us -> 45.1 us
  waiting for transfers between devices: 6.16 us -> 7.45 us
    pallas_call x1, Pallas kernels: 1.74 us -> 0.03 us  [low_and_maps(): pl.pallas_call(low_kernel, out_shape=jax.ShapeDtypeStruct(mine.shape, jnp...]
    ppermute x1, waiting for transfers between devices: 0.01 us -> 1.13 us  [local(): lax.ppermute(sent[step], 'seq', onward(step + 1))]
    unnamed x16 -> x18, local copies, waits for them, and re-layouts: 3.06 us -> 3.33 us
  transfers between devices with their start and end apart: 10 -> 10, of which waited for: 3 -> 4; matrix products, arithmetic and copies ran while one was open for 7% -> 7% of each run, Pallas kernels for 26% -> 24%
where the time goes in v8:
time: 80.5 us; the launch traced here: 79.8 us
  Pallas kernels  45.1 us (56%)
  starting transfers between devices  17.7 us (22%)
  waiting for transfers between devices  7.45 us (9%)
  local copies, waits for them, and re-layouts  6.73 us (8%)
  other arithmetic  2.13 us (3%)
    pallas_call x1, Pallas kernels, add_carried(): pl.pallas_call(carried_kernel, grid_spec=pltpu.PrefetchScalarGridSpec(num...  9.17 us
    pallas_call x1, Pallas kernels, scan_own(): pl.pallas_call(own_kernel, grid_spec=pltpu.PrefetchScalarGridSpec(num_sca...  9.15 us
    pallas_call x1, Pallas kernels, attend(): pl.pallas_call(functools.partial(attend_kernel, chips=chips), grid_spec=p...  8.03 us
    pallas_call x1, Pallas kernels, scan_others(): pl.pallas_call(others_kernel, grid_spec=pltpu.PrefetchScalarGridSpec(num_...  8.02 us
    pallas_call x1, Pallas kernels, step_sizes(): pl.pallas_call(step_kernel, grid_spec=pltpu.PrefetchScalarGridSpec(num_sc...  6.6 us
    all_to_all x1, starting transfers between devices, local(): lax.all_to_all(carry, 'chan', split_axis=0, concat_axis=0, tiled=True)  5.82 us
    ppermute x1, starting transfers between devices, local(): from_far = lax.ppermute(theirs, 'seq', far)  4.54 us
    ppermute x1, waiting for transfers between devices, local(): from_near = lax.ppermute(own, 'seq', near)  3.97 us
  transfers between devices with their start and end apart: 10, of which 4 were waited for; matrix products, arithmetic and copies ran while one was open for 7% of the time, Pallas kernels for 24%

profile of v8, /device:TPU:0, one launch (start us, length us, event | category | flops | bytes accessed | tf_op | source)
XLA Modules:
  0.0 79.8 jit_solution(9549483467898056165)
XLA Ops:
  0.6 0.0 copy-start
  0.6 2.1 %select_heads.1 = (bf16[2,2,128,256]{3,2,1,0:T(8,128)(2,1)}, bf16[2,2,128,256]{3,2,1,0:T(8,128)(2,1)}) custom-call(bf16[128,1024]{1,0:T(8,128)(2,1)} %bitcast.20, bf16[128,1024]{1,0:T(8,128)(2,1)} %bitcast.21), custom_call_target="tpu_custom_call" | custom-call | tf_op jit(solution)/shard_map/select_heads/pallas_call | solution.py:62
  2.7 0.5 collective-permute-start
  3.3 4.5 %collective-permute-start.3 = (bf16[2,2,128,256]{3,2,1,0:T(8,128)(2,1)}, bf16[2,2,128,256]{3,2,1,0:T(8,128)(2,1)S(1)}, u32[]{:S(2)}, u32[]{:S(2)}) collective-permute-start(bf16[2,2,128,256]{3,2,1,0:T(8,128)(2,1)} %get-tuple-element.23), channel_id=1, source_target_pairs={{0,24},{8,16},{1,25},{9,17},{2,26},{10,18},{3,27},{11,19},{4,28},{... | collective-permute-start | bytes 786440 | tf_op jit(solution)/shard_map/ppermute | solution.py:785
  7.8 0.1 collective-permute-start.1
  7.9 2.3 %collective-permute-start.2 = (bf16[2,2,128,256]{3,2,1,0:T(8,128)(2,1)}, bf16[2,2,128,256]{3,2,1,0:T(8,128)(2,1)}, u32[]{:S(2)}, u32[]{:S(2)}) collective-permute-start(bf16[2,2,128,256]{3,2,1,0:T(8,128)(2,1)} %get-tuple-element.21.own_ref), channel_id=1, source_target_pairs={{0,16},{8,24},{1,17},{9,25},{2,18},{10,26},{3,19},{11,27},{4,20},{... | collective-permute-start | bytes 786440 | tf_op jit(solution)/shard_map/ppermute | solution.py:784
  10.2 0.7 pad_add_fusion.place_ref
  10.9 1.3 %dynamic_slice.14 = f32[1024]{0:T(1024)} dynamic-slice(f32[4096]{0:T(1024)} %param.17, s32[]{:T(128)S(6)} %select_n.12), dynamic_slice_sizes={1024} | dynamic-slice | bytes 8196 | tf_op jit(solution)/shard_map/dynamic_slice | solution.py:795
  12.2 1.3 %dynamic_slice.15 = f32[1024]{0:T(1024)} dynamic-slice(f32[4096]{0:T(1024)} %param.19, s32[]{:T(128)S(6)} %select_n.12), dynamic_slice_sizes={1024} | dynamic-slice | bytes 8196 | tf_op jit(solution)/shard_map/dynamic_slice | solution.py:796
  13.4 1.5 %multiply_bitcast_fusion.rest_0_.rates_ref = f32[16,1024]{1,0:T(8,128)} fusion(f32[4096,16]{0,1:T(8,128)} %param.18, s32[]{:T(128)S(6)} %select_n.12), kind=kLoop, calls=%fused_computation | loop fusion | flops 16384 | bytes 131076 | tf_op jit(solution)/shard_map/transpose | solution.py:793
  14.9 0.0 copy-done
  14.9 0.8 %constant_dynamic-slice_fusion.rest_1_.cols_ref = bf16[256,1024]{1,0:T(8,128)(2,1)} fusion(bf16[256,4096]{1,0:T(8,128)(2,1)S(1)} %copy-done, s32[]{:T(128)S(6)} %select_n.12), kind=kLoop, calls=%fused_computation.2 | loop fusion | bytes 1048580 | tf_op jit(solution)/shard_map/dynamic_slice | solution.py:794
  15.8 0.0 collective-permute-done.3.far_ref
  15.8 0.0 copy-start.8
  15.8 0.0 collective-permute-done.1.swap_ref
  15.8 4.0 %collective-permute-done.2.near_ref = bf16[2,2,128,256]{3,2,1,0:T(8,128)(2,1)} collective-permute-done((bf16[2,2,128,256]{3,2,1,0:T(8,128)(2,1)}, bf16[2,2,128,256]{3,2,1,0:T(8,128)(2,1)}, u32[]{:S(2)}, u32[]{:S(2)}) %collective-permute-start.2) | collective-permute-done | bytes 262176 | tf_op jit(solution)/shard_map/ppermute | solution.py:784
  19.7 0.0 collective-permute-done.theirs_ref
  19.7 0.0 copy-start.7
  19.7 0.0 copy-done.8
  19.7 1.0 %copy-done.7 = bf16[128,4096]{1,0:T(8,128)(2,1)} copy-done((bf16[128,4096]{1,0:T(8,128)(2,1)}, bf16[128,4096]{1,0:T(8,128)(2,1)S(1)}, u32[]{:S(2)}) %copy-start.7) | copy-done | bytes 1048600
  20.7 8.0 %attend.1 = (bf16[1,256,1024]{2,1,0:T(8,128)(2,1)}, bf16[1,256,1024]{2,1,0:T(8,128)(2,1)}, f32[288,256]{1,0:T(8,128)}) custom-call(s32[2]{0:T(128)} %pad_add_fusion.place_ref, s32[1,16]{1,0:T(1,128)} %doc_ref.1, bf16[128,4096]{1,0:T(8,128)(2,1)} %bitcast.29, bf16[128,4096]{1,0:T(8,128)(2,1)} %copy-done.7, ...), custom_call_target="tpu_custom_call" | custom-call | flops 5000000000 | bytes 4194304 | tf_op jit(solution)/shard_map/attend/pallas_call | solution.py:237
  28.7 0.1 collective-permute-start.7
  28.8 2.5 %collective-permute-start.5 = (bf16[256,1024]{1,0:T(8,128)(2,1)}, bf16[256,1024]{1,0:T(8,128)(2,1)}, u32[]{:S(2)}, u32[]{:S(2)}) collective-permute-start(bf16[256,1024]{1,0:T(8,128)(2,1)} %bitcast.15), channel_id=1, source_target_pairs={{0,16},{8,24},{16,0},{24,8},{1,17},{9,25},{17,1},{25,9},{2,18},{10... | collective-permute-start | bytes 1572872 | tf_op jit(solution)/shard_map/ppermute | solution.py:802
  31.4 0.2 collective-permute-start.6
  31.5 0.3 collective-permute-start.4
  31.9 0.0 collective-permute-done.7.theirs_ref
  31.9 0.0 copy-start.3
  31.9 1.0 %copy-done.3 = f32[288,256]{1,0:T(8,128)S(1)} copy-done((f32[288,256]{1,0:T(8,128)S(1)}, f32[288,256]{1,0:T(8,128)}, u32[]{:S(2)}) %copy-start.3) | copy-done | bytes 294936
  32.9 0.0 copy-start.4
  32.9 0.0 copy-start.1
  32.9 0.0 copy-start.2
  32.9 1.3 %collective-permute-start.8 = (bf16[288,256]{1,0:T(8,128)(2,1)S(1)}, bf16[288,256]{1,0:T(8,128)(2,1)S(1)}, u32[]{:S(2)}, u32[]{:S(2)}) collective-permute-start(bf16[288,256]{1,0:T(8,128)(2,1)S(1)} %low_and_maps.1.low_ref.map_ref), channel_id=1, source_target_pairs={{0,16},{8,24},{16,0},{24,8},{1,17},{9,25},{17,1},{25,9},{2,18},{10... | collective-permute-start | bytes 442376 | tf_op jit(solution)/shard_map/ppermute | solution.py:804
  34.2 0.0 copy-done.4
  34.2 9.2 %scan_own.1 = (bf16[512,1024]{1,0:T(8,128)(2,1)}, bf16[512,1024]{1,0:T(8,128)(2,1)}, f32[4,32,128]{2,1,0:T(8,128)}, f32[16,1024]{1,0:T(8,128)}, f32[1,1024]{1,0:T(1,128)}) custom-call(s32[2]{0:T(128)} %pad_add_fusion.place_ref, bf16[1,256,1024]{2,1,0:T(8,128)(2,1)} %get-tuple-element.25.stayed_ref.stream_ref, bf16[288,256]{1,0:T(8,128)(2,1)} %copy-done.4, ...), custom_call_target="tpu_custom_call" | custom-call | flops 4000000000 | bytes 2097152 | tf_op jit(solution)/shard_map/scan_own/pallas_call | solution.py:562
  43.3 1.1 %collective-permute-done.5 = bf16[256,1024]{1,0:T(8,128)(2,1)} collective-permute-done((bf16[256,1024]{1,0:T(8,128)(2,1)}, bf16[256,1024]{1,0:T(8,128)(2,1)}, u32[]{:S(2)}, u32[]{:S(2)}) %collective-permute-start.5) | collective-permute-done | bytes 524320 | tf_op jit(solution)/shard_map/ppermute | solution.py:802
  44.5 0.0 collective-permute-done.6.got_stayed_ref
  44.5 0.0 collective-permute-done.4.got_sent_ref
  44.5 0.0 copy-done.1
  44.5 0.0 copy-done.2
  44.5 2.0 %join_heads.1.rest_2_ = bf16[128,4096]{1,0:T(8,128)(2,1)} custom-call(bf16[1,256,1024]{2,1,0:T(8,128)(2,1)S(1)} %copy-done.1, bf16[1,256,1024]{2,1,0:T(8,128)(2,1)S(1)} %copy-done.2, bf16[1,256,1024]{2,1,0:T(8,128)(2,1)} %collective-permute-done.4.got_sent_ref, bf16[1,256,1024]{2,1,0:T(8,128)(2,1)S(1)} %collective-permute-done.6.got_stayed_ref), custom_call_target="tpu_custom_call" | custom-call | tf_op jit(solution)/shard_map/join_heads/pallas_call | solution.py:91
  46.5 0.7 collective-permute-done.8
  47.3 0.7 copy-done.6
  47.9 6.6 %step_sizes.1 = (bf16[256,1024]{1,0:T(8,128)(2,1)}, bf16[512,1024]{1,0:T(8,128)(2,1)}, f32[4,32,128]{2,1,0:T(8,128)}, bf16[8,144,128]{2,1,0:T(8,128)(2,1)}) custom-call(s32[2]{0:T(128)} %pad_add_fusion.place_ref, bf16[1,256,1024]{2,1,0:T(8,128)(2,1)} %bitcast.11.stream_ref, ...), custom_call_target="tpu_custom_call", output_to_operand_aliasing={{1}: (10, {}), {2}: (11, {})} | custom-call | tf_op jit(solution)/shard_map/step_sizes/pallas_call | solution.py:402
  54.5 5.8 %all-to-all-start = ((bf16[8,144,128]{2,1,0:T(8,128)(2,1)}), bf16[8,144,128]{2,1,0:T(8,128)(2,1)S(1)}, u32[]{:S(2)}, u32[]{:S(2)}) async-start(bf16[8,144,128]{2,1,0:T(8,128)(2,1)} %get-tuple-element.39), calls=%async_computation | async-start | bytes 589824 | tf_op jit(solution)/shard_map/all_to_all | solution.py:815
  60.3 8.0 %scan_others.1 = (bf16[512,1024]{1,0:T(8,128)(2,1)}, f32[1,16,1024]{2,1,0:T(8,128)}) custom-call(s32[2]{0:T(128)} %pad_add_fusion.place_ref, bf16[1,256,1024]{2,1,0:T(8,128)(2,1)} %bitcast.11.stream_ref, bf16[256,1024]{1,0:T(8,128)(2,1)} %get-tuple-element.33.steps_ref, f32[4,32,128]{2,1,0:T(8,128)} %get-tuple-element.34.maps_ref, ...), custom_call_target="tpu_custom_call", output_to_operand_aliasing={{0}: (6, {})} | custom-call | flops 4000000000 | bytes 2097152 | tf_op jit(solution)/shard_map/scan_others/pallas_call | solution.py:628
  68.3 1.6 %all-to-all-done.carries_ref = bf16[8,144,128]{2,1,0:T(8,128)(2,1)S(1)} async-done(((bf16[8,144,128]{2,1,0:T(8,128)(2,1)}), bf16[8,144,128]{2,1,0:T(8,128)(2,1)S(1)}, u32[]{:S(2)}, u32[]{:S(2)}) %all-to-all-start) | async-done | bytes 294944 | tf_op jit(solution)/shard_map/all_to_all | solution.py:815
  70.0 0.7 copy-done.5
  70.7 9.2 %add_carried.1 = bf16[512,1024]{1,0:T(8,128)(2,1)} custom-call(s32[2]{0:T(128)} %pad_add_fusion.place_ref, bf16[512,1024]{1,0:T(8,128)(2,1)} %get-tuple-element.36.part_ref, bf16[512,1024]{1,0:T(8,128)(2,1)} %get-tuple-element.37.sums_ref, f32[4,32,128]{2,1,0:T(8,128)} %get-tuple-element.34.maps_ref, f32[16,1024]{1,0:T(8,128)} %get-tuple-element.29.rest_0_.last_own_ref, ...), custom_call_target="tpu_custom_call" | custom-call | tf_op jit(solution)/shard_map/add_carried/pallas_call | solution.py:733
  (3 shorter events, 0.0 us)
Async XLA Ops:
  0.6 14.3 %copy-start = (bf16[256,4096]{1,0:T(8,128)(2,1)S(1)}, bf16[256,4096]{1,0:T(8,128)(2,1)}, u32[]{:S(2)}) copy-start(bf16[256,4096]{1,0:T(8,128)(2,1)} %param.16) | copy-start | bytes 6291460
  2.7 17.0 %collective-permute-start = (bf16[128,4096]{1,0:T(8,128)(2,1)}, bf16[128,4096]{1,0:T(8,128)(2,1)S(1)}, u32[]{:S(2)}, u32[]{:S(2)}) collective-permute-start(bf16[128,4096]{1,0:T(8,128)(2,1)} %bitcast.28), channel_id=1, source_target_pairs={{0,8},{8,0},{16,24},{24,16},{1,9},{9,1},{17,25},{25,17},{2,10},{10... | collective-permute-start | bytes 3145736 | tf_op jit(solution)/shard_map/ppermute | solution.py:788
  3.3 12.5 %collective-permute-start.3 = (bf16[2,2,128,256]{3,2,1,0:T(8,128)(2,1)}, bf16[2,2,128,256]{3,2,1,0:T(8,128)(2,1)S(1)}, u32[]{:S(2)}, u32[]{:S(2)}) collective-permute-start(bf16[2,2,128,256]{3,2,1,0:T(8,128)(2,1)} %get-tuple-element.23), channel_id=1, source_target_pairs={{0,24},{8,16},{1,25},{9,17},{2,26},{10,18},{3,27},{11,19},{4,28},{... | collective-permute-start | bytes 786440 | tf_op jit(solution)/shard_map/ppermute | solution.py:785
  7.8 8.0 %collective-permute-start.1 = (bf16[2,2,128,256]{3,2,1,0:T(8,128)(2,1)}, bf16[2,2,128,256]{3,2,1,0:T(8,128)(2,1)}, u32[]{:S(2)}, u32[]{:S(2)}) collective-permute-start(bf16[2,2,128,256]{3,2,1,0:T(8,128)(2,1)} %get-tuple-element.23), channel_id=1, source_target_pairs={{0,8},{8,0},{16,24},{24,16},{1,9},{9,1},{17,25},{25,17},{2,10},{10... | collective-permute-start | bytes 786440 | tf_op jit(solution)/shard_map/ppermute | solution.py:786
  7.9 11.8 %collective-permute-start.2 = (bf16[2,2,128,256]{3,2,1,0:T(8,128)(2,1)}, bf16[2,2,128,256]{3,2,1,0:T(8,128)(2,1)}, u32[]{:S(2)}, u32[]{:S(2)}) collective-permute-start(bf16[2,2,128,256]{3,2,1,0:T(8,128)(2,1)} %get-tuple-element.21.own_ref), channel_id=1, source_target_pairs={{0,16},{8,24},{1,17},{9,25},{2,18},{10,26},{3,19},{11,27},{4,20},{... | collective-permute-start | bytes 786440 | tf_op jit(solution)/shard_map/ppermute | solution.py:784
  15.8 4.0 %copy-start.8 = (bf16[2,2,128,256]{3,2,1,0:T(8,128)(2,1)}, bf16[2,2,128,256]{3,2,1,0:T(8,128)(2,1)S(1)}, u32[]{:S(2)}) copy-start(bf16[2,2,128,256]{3,2,1,0:T(8,128)(2,1)S(1)} %collective-permute-done.3.far_ref) | copy-start | bytes 786436
  19.7 1.0 %copy-start.7 = (bf16[128,4096]{1,0:T(8,128)(2,1)}, bf16[128,4096]{1,0:T(8,128)(2,1)S(1)}, u32[]{:S(2)}) copy-start(bf16[128,4096]{1,0:T(8,128)(2,1)S(1)} %collective-permute-done.theirs_ref) | copy-start | bytes 3145732
  28.7 3.1 %collective-permute-start.7 = (f32[288,256]{1,0:T(8,128)}, f32[288,256]{1,0:T(8,128)S(1)}, u32[]{:S(2)}, u32[]{:S(2)}) collective-permute-start(f32[288,256]{1,0:T(8,128)} %get-tuple-element.28.mine_ref), channel_id=1, source_target_pairs={{0,8},{8,0},{16,24},{24,16},{1,9},{9,1},{17,25},{25,17},{2,10},{10... | collective-permute-start | bytes 884744 | tf_op jit(solution)/shard_map/ppermute | solution.py:803
  28.8 15.6 %collective-permute-start.5 = (bf16[256,1024]{1,0:T(8,128)(2,1)}, bf16[256,1024]{1,0:T(8,128)(2,1)}, u32[]{:S(2)}, u32[]{:S(2)}) collective-permute-start(bf16[256,1024]{1,0:T(8,128)(2,1)} %bitcast.15), channel_id=1, source_target_pairs={{0,16},{8,24},{16,0},{24,8},{1,17},{9,25},{17,1},{25,9},{2,18},{10... | collective-permute-start | bytes 1572872 | tf_op jit(solution)/shard_map/ppermute | solution.py:802
  31.4 13.1 %collective-permute-start.6 = (bf16[1,256,1024]{2,1,0:T(8,128)(2,1)}, bf16[1,256,1024]{2,1,0:T(8,128)(2,1)S(1)}, u32[]{:S(2)}, u32[]{:S(2)}) collective-permute-start(bf16[1,256,1024]{2,1,0:T(8,128)(2,1)} %get-tuple-element.25.stayed_ref.stream_ref), channel_id=1, source_target_pairs={{0,8},{8,0},{16,24},{24,16},{1,9},{9,1},{17,25},{25,17},{2,10},{10... | collective-permute-start | bytes 1572872 | tf_op jit(solution)/shard_map/ppermute | solution.py:806
  31.5 12.9 %collective-permute-start.4 = (bf16[1,256,1024]{2,1,0:T(8,128)(2,1)}, bf16[1,256,1024]{2,1,0:T(8,128)(2,1)}, u32[]{:S(2)}, u32[]{:S(2)}) collective-permute-start(bf16[1,256,1024]{2,1,0:T(8,128)(2,1)} %get-tuple-element.24.sent_ref), channel_id=1, source_target_pairs={{0,8},{8,0},{16,24},{24,16},{1,9},{9,1},{17,25},{25,17},{2,10},{10... | collective-permute-start | bytes 1572872 | tf_op jit(solution)/shard_map/ppermute | solution.py:805
  31.9 1.0 %copy-start.3 = (f32[288,256]{1,0:T(8,128)S(1)}, f32[288,256]{1,0:T(8,128)}, u32[]{:S(2)}) copy-start(f32[288,256]{1,0:T(8,128)} %get-tuple-element.28.mine_ref) | copy-start | bytes 884740
  32.9 1.3 %copy-start.4 = (bf16[288,256]{1,0:T(8,128)(2,1)}, bf16[288,256]{1,0:T(8,128)(2,1)S(1)}, u32[]{:S(2)}) copy-start(bf16[288,256]{1,0:T(8,128)(2,1)S(1)} %low_and_maps.1.low_ref.map_ref) | copy-start | bytes 442372
  32.9 11.6 %copy-start.1 = (bf16[1,256,1024]{2,1,0:T(8,128)(2,1)S(1)}, bf16[1,256,1024]{2,1,0:T(8,128)(2,1)}, u32[]{:S(2)}) copy-start(bf16[1,256,1024]{2,1,0:T(8,128)(2,1)} %get-tuple-element.24.sent_ref) | copy-start | bytes 1572868
  32.9 11.6 %copy-start.2 = (bf16[1,256,1024]{2,1,0:T(8,128)(2,1)S(1)}, bf16[1,256,1024]{2,1,0:T(8,128)(2,1)}, u32[]{:S(2)}) copy-start(bf16[1,256,1024]{2,1,0:T(8,128)(2,1)} %get-tuple-element.25.stayed_ref.stream_ref) | copy-start | bytes 1572868
  32.9 14.3 %collective-permute-start.8 = (bf16[288,256]{1,0:T(8,128)(2,1)S(1)}, bf16[288,256]{1,0:T(8,128)(2,1)S(1)}, u32[]{:S(2)}, u32[]{:S(2)}) collective-permute-start(bf16[288,256]{1,0:T(8,128)(2,1)S(1)} %low_and_maps.1.low_ref.map_ref), channel_id=1, source_target_pairs={{0,16},{8,24},{16,0},{24,8},{1,17},{9,25},{17,1},{25,9},{2,18},{10... | collective-permute-start | bytes 442376 | tf_op jit(solution)/shard_map/ppermute | solution.py:804
  47.3 0.7 copy-start.6
  54.5 15.5 %all-to-all-start = ((bf16[8,144,128]{2,1,0:T(8,128)(2,1)}), bf16[8,144,128]{2,1,0:T(8,128)(2,1)S(1)}, u32[]{:S(2)}, u32[]{:S(2)}) async-start(bf16[8,144,128]{2,1,0:T(8,128)(2,1)} %get-tuple-element.39), calls=%async_computation | async-start | bytes 589824 | tf_op jit(solution)/shard_map/all_to_all | solution.py:815
  70.0 0.7 copy-start.5

commit v9 on v8

--- a/solution.py
+++ b/solution.py
@@ -268,7 +268,8 @@
 
 
 def low_kernel(mine_ref, theirs_ref, out_ref):
-    out_ref[...] = (mine_ref[...] + theirs_ref[...]).astype(jnp.bfloat16)
+    total = mine_ref[...] + theirs_ref[...].astype(jnp.float32)
+    out_ref[...] = total.astype(jnp.bfloat16)
 
 
 def low_and_maps(mine, theirs):
@@ -800,7 +801,7 @@
         (rates, cols, bias, gain),
     )
     come = [lax.ppermute(sent[step], "seq", onward(step + 1)) for step in range(chips - 1)]
-    low_own = low_and_maps(part, lax.ppermute(part, "seq", swap))
+    low_own = low_and_maps(part, lax.ppermute(part.astype(jnp.bfloat16), "seq", swap))
     low_come = [lax.ppermute(low_own, "seq", onward(step + 1)) for step in range(chips - 1)]
     got_sent = lax.ppermute(sent, "seq", swap)
     got_stayed = lax.ppermute(stayed, "seq", swap)

time: 80.5 us -> 80.6 us (level)
  starting transfers between devices: 17.7 us -> 16.6 us
  other arithmetic: 2.13 us -> 3.11 us
    ppermute x1, waiting for transfers between devices: 0.01 us -> 1.36 us  [local(): lax.ppermute(part.astype(jnp.bfloat16), 'seq', swap)]
    ppermute x1, waiting for transfers between devices: 1.13 us -> 0.01 us  [local(): lax.ppermute(sent[step], 'seq', onward(step + 1))]
    ppermute x1, starting transfers between devices: 1.27 us -> 0.15 us  [local(): lax.ppermute(low_own, 'seq', onward(step + 1))]
    convert_element_type x0 -> x1, other arithmetic: none -> 0.98 us  [local(): part.astype(jnp.bfloat16)]
  transfers between devices with their start and end apart: 10 -> 10, of which waited for: 4 -> 3; matrix products, arithmetic and copies ran while one was open for 7% -> 8% of each run, Pallas kernels for 24% -> 24%
where the time goes in v9:
time: 80.6 us; the launch traced here: 80 us
  Pallas kernels  45.1 us (56%)
  starting transfers between devices  16.6 us (21%)
  local copies, waits for them, and re-layouts  7.2 us (9%)
  waiting for transfers between devices  7.2 us (9%)
  other arithmetic  3.11 us (4%)
    pallas_call x1, Pallas kernels, add_carried(): pl.pallas_call(carried_kernel, grid_spec=pltpu.PrefetchScalarGridSpec(num...  9.17 us
    pallas_call x1, Pallas kernels, scan_own(): pl.pallas_call(own_kernel, grid_spec=pltpu.PrefetchScalarGridSpec(num_sca...  9.15 us
    pallas_call x1, Pallas kernels, attend(): pl.pallas_call(functools.partial(attend_kernel, chips=chips), grid_spec=p...  8.03 us
    pallas_call x1, Pallas kernels, scan_others(): pl.pallas_call(others_kernel, grid_spec=pltpu.PrefetchScalarGridSpec(num_...  8.02 us
    pallas_call x1, Pallas kernels, step_sizes(): pl.pallas_call(step_kernel, grid_spec=pltpu.PrefetchScalarGridSpec(num_sc...  6.6 us
    all_to_all x1, starting transfers between devices, local(): lax.all_to_all(carry, 'chan', split_axis=0, concat_axis=0, tiled=True)  5.82 us
    ppermute x1, starting transfers between devices, local(): from_far = lax.ppermute(theirs, 'seq', far)  4.54 us
    ppermute x1, waiting for transfers between devices, local(): from_near = lax.ppermute(own, 'seq', near)  3.97 us
  transfers between devices with their start and end apart: 10, of which 3 were waited for; matrix products, arithmetic and copies ran while one was open for 8% of the time, Pallas kernels for 24%

profile of v9, /device:TPU:0, one launch (start us, length us, event | category | flops | bytes accessed | tf_op | source)
XLA Modules:
  0.0 80.0 jit_solution(7835670748827556116)
XLA Ops:
  0.6 0.0 copy-start
  0.6 2.1 %select_heads.1 = (bf16[2,2,128,256]{3,2,1,0:T(8,128)(2,1)}, bf16[2,2,128,256]{3,2,1,0:T(8,128)(2,1)}) custom-call(bf16[128,1024]{1,0:T(8,128)(2,1)} %bitcast.20, bf16[128,1024]{1,0:T(8,128)(2,1)} %bitcast.21), custom_call_target="tpu_custom_call" | custom-call | tf_op jit(solution)/shard_map/select_heads/pallas_call | solution.py:62
  2.7 0.5 collective-permute-start
  3.3 4.5 %collective-permute-start.3 = (bf16[2,2,128,256]{3,2,1,0:T(8,128)(2,1)}, bf16[2,2,128,256]{3,2,1,0:T(8,128)(2,1)S(1)}, u32[]{:S(2)}, u32[]{:S(2)}) collective-permute-start(bf16[2,2,128,256]{3,2,1,0:T(8,128)(2,1)} %get-tuple-element.23), channel_id=1, source_target_pairs={{0,24},{8,16},{1,25},{9,17},{2,26},{10,18},{3,27},{11,19},{4,28},{... | collective-permute-start | bytes 786440 | tf_op jit(solution)/shard_map/ppermute | solution.py:786
  7.8 0.1 collective-permute-start.1
  7.9 2.3 %collective-permute-start.2 = (bf16[2,2,128,256]{3,2,1,0:T(8,128)(2,1)}, bf16[2,2,128,256]{3,2,1,0:T(8,128)(2,1)}, u32[]{:S(2)}, u32[]{:S(2)}) collective-permute-start(bf16[2,2,128,256]{3,2,1,0:T(8,128)(2,1)} %get-tuple-element.21.own_ref), channel_id=1, source_target_pairs={{0,16},{8,24},{1,17},{9,25},{2,18},{10,26},{3,19},{11,27},{4,20},{... | collective-permute-start | bytes 786440 | tf_op jit(solution)/shard_map/ppermute | solution.py:785
  10.2 0.7 pad_add_fusion.place_ref
  10.9 1.3 %dynamic_slice.14 = f32[1024]{0:T(1024)} dynamic-slice(f32[4096]{0:T(1024)} %param.17, s32[]{:T(128)S(6)} %select_n.12), dynamic_slice_sizes={1024} | dynamic-slice | bytes 8196 | tf_op jit(solution)/shard_map/dynamic_slice | solution.py:796
  12.2 1.3 %dynamic_slice.15 = f32[1024]{0:T(1024)} dynamic-slice(f32[4096]{0:T(1024)} %param.19, s32[]{:T(128)S(6)} %select_n.12), dynamic_slice_sizes={1024} | dynamic-slice | bytes 8196 | tf_op jit(solution)/shard_map/dynamic_slice | solution.py:797
  13.4 1.5 %multiply_bitcast_fusion.rest_0_.rates_ref = f32[16,1024]{1,0:T(8,128)} fusion(f32[4096,16]{0,1:T(8,128)} %param.18, s32[]{:T(128)S(6)} %select_n.12), kind=kLoop, calls=%fused_computation | loop fusion | flops 16384 | bytes 131076 | tf_op jit(solution)/shard_map/transpose | solution.py:794
  14.9 0.0 copy-done
  14.9 0.8 %constant_dynamic-slice_fusion.rest_1_.cols_ref = bf16[256,1024]{1,0:T(8,128)(2,1)} fusion(bf16[256,4096]{1,0:T(8,128)(2,1)S(1)} %copy-done, s32[]{:T(128)S(6)} %select_n.12), kind=kLoop, calls=%fused_computation.2 | loop fusion | bytes 1048580 | tf_op jit(solution)/shard_map/dynamic_slice | solution.py:795
  15.8 0.0 collective-permute-done.3.far_ref
  15.8 0.0 copy-start.8
  15.8 0.0 collective-permute-done.1.swap_ref
  15.8 4.0 %collective-permute-done.2.near_ref = bf16[2,2,128,256]{3,2,1,0:T(8,128)(2,1)} collective-permute-done((bf16[2,2,128,256]{3,2,1,0:T(8,128)(2,1)}, bf16[2,2,128,256]{3,2,1,0:T(8,128)(2,1)}, u32[]{:S(2)}, u32[]{:S(2)}) %collective-permute-start.2) | collective-permute-done | bytes 262176 | tf_op jit(solution)/shard_map/ppermute | solution.py:785
  19.7 0.0 collective-permute-done.theirs_ref
  19.7 0.0 copy-done.8
  19.7 1.0 %copy-done.7 = bf16[128,4096]{1,0:T(8,128)(2,1)} copy-done((bf16[128,4096]{1,0:T(8,128)(2,1)}, bf16[128,4096]{1,0:T(8,128)(2,1)S(1)}, u32[]{:S(2)}) %copy-start.7) | copy-done | bytes 1048600
  20.7 8.0 %attend.1 = (bf16[1,256,1024]{2,1,0:T(8,128)(2,1)}, bf16[1,256,1024]{2,1,0:T(8,128)(2,1)}, f32[288,256]{1,0:T(8,128)}) custom-call(s32[2]{0:T(128)} %pad_add_fusion.place_ref, s32[1,16]{1,0:T(1,128)} %doc_ref.1, bf16[128,4096]{1,0:T(8,128)(2,1)} %bitcast.29, bf16[128,4096]{1,0:T(8,128)(2,1)} %copy-done.7, ...), custom_call_target="tpu_custom_call" | custom-call | flops 5000000000 | bytes 4194304 | tf_op jit(solution)/shard_map/attend/pallas_call | solution.py:237
  28.7 2.5 %collective-permute-start.5 = (bf16[256,1024]{1,0:T(8,128)(2,1)}, bf16[256,1024]{1,0:T(8,128)(2,1)}, u32[]{:S(2)}, u32[]{:S(2)}) collective-permute-start(bf16[256,1024]{1,0:T(8,128)(2,1)} %bitcast.15), channel_id=1, source_target_pairs={{0,16},{8,24},{16,0},{24,8},{1,17},{9,25},{17,1},{25,9},{2,18},{10... | collective-permute-start | bytes 1572872 | tf_op jit(solution)/shard_map/ppermute | solution.py:803
  31.3 0.0 collective-permute-start.6
  31.3 0.5 collective-permute-start.4
  31.8 1.0 %convert_element_type.3 = bf16[288,256]{1,0:T(8,128)(2,1)S(1)} convert(f32[288,256]{1,0:T(8,128)} %get-tuple-element.28.mine_ref) | non-fusion elementwise | flops 73728 | bytes 442368 | tf_op jit(solution)/shard_map/convert_element_type | solution.py:804
  32.8 0.1 collective-permute-start.7
  32.9 1.4 %collective-permute-done.7.theirs_ref = bf16[288,256]{1,0:T(8,128)(2,1)S(1)} collective-permute-done((bf16[288,256]{1,0:T(8,128)(2,1)S(1)}, bf16[288,256]{1,0:T(8,128)(2,1)S(1)}, u32[]{:S(2)}, u32[]{:S(2)}) %collective-permute-start.7) | collective-permute-done | bytes 147488 | tf_op jit(solution)/shard_map/ppermute | solution.py:804
  34.2 1.0 %copy-done.1 = f32[288,256]{1,0:T(8,128)S(1)} copy-done((f32[288,256]{1,0:T(8,128)S(1)}, f32[288,256]{1,0:T(8,128)}, u32[]{:S(2)}) %copy-start.1) | copy-done | bytes 294936
  35.2 0.0 copy-start.4
  35.2 0.0 copy-start.2
  35.2 0.0 copy-start.3
  35.2 0.1 collective-permute-start.8
  35.4 0.5 copy-done.4
  35.9 9.1 %scan_own.1 = (bf16[512,1024]{1,0:T(8,128)(2,1)}, bf16[512,1024]{1,0:T(8,128)(2,1)}, f32[4,32,128]{2,1,0:T(8,128)}, f32[16,1024]{1,0:T(8,128)}, f32[1,1024]{1,0:T(1,128)}) custom-call(s32[2]{0:T(128)} %pad_add_fusion.place_ref, bf16[1,256,1024]{2,1,0:T(8,128)(2,1)} %get-tuple-element.25.stayed_ref.stream_ref, bf16[288,256]{1,0:T(8,128)(2,1)} %copy-done.4, ...), custom_call_target="tpu_custom_call" | custom-call | flops 4000000000 | bytes 2097152 | tf_op jit(solution)/shard_map/scan_own/pallas_call | solution.py:563
  45.0 0.0 collective-permute-done.5
  45.0 0.0 collective-permute-done.6.got_stayed_ref
  45.0 0.0 collective-permute-done.4.got_sent_ref
  45.1 0.0 copy-done.2
  45.1 0.0 copy-done.3
  45.1 2.0 %join_heads.1.rest_2_ = bf16[128,4096]{1,0:T(8,128)(2,1)} custom-call(bf16[1,256,1024]{2,1,0:T(8,128)(2,1)S(1)} %copy-done.2, bf16[1,256,1024]{2,1,0:T(8,128)(2,1)S(1)} %copy-done.3, bf16[1,256,1024]{2,1,0:T(8,128)(2,1)} %collective-permute-done.4.got_sent_ref, bf16[1,256,1024]{2,1,0:T(8,128)(2,1)S(1)} %collective-permute-done.6.got_stayed_ref), custom_call_target="tpu_custom_call" | custom-call | tf_op jit(solution)/shard_map/join_heads/pallas_call | solution.py:91
  47.1 0.0 collective-permute-done.8
  47.1 0.0 copy-start.6
  47.1 0.6 copy-done.6
  47.8 6.6 %step_sizes.1 = (bf16[256,1024]{1,0:T(8,128)(2,1)}, bf16[512,1024]{1,0:T(8,128)(2,1)}, f32[4,32,128]{2,1,0:T(8,128)}, bf16[8,144,128]{2,1,0:T(8,128)(2,1)}) custom-call(s32[2]{0:T(128)} %pad_add_fusion.place_ref, bf16[1,256,1024]{2,1,0:T(8,128)(2,1)} %bitcast.11.stream_ref, ...), custom_call_target="tpu_custom_call", output_to_operand_aliasing={{1}: (10, {}), {2}: (11, {})} | custom-call | tf_op jit(solution)/shard_map/step_sizes/pallas_call | solution.py:403
  54.4 5.8 %all-to-all-start = ((bf16[8,144,128]{2,1,0:T(8,128)(2,1)}), bf16[8,144,128]{2,1,0:T(8,128)(2,1)S(1)}, u32[]{:S(2)}, u32[]{:S(2)}) async-start(bf16[8,144,128]{2,1,0:T(8,128)(2,1)} %get-tuple-element.39), calls=%async_computation | async-start | bytes 589824 | tf_op jit(solution)/shard_map/all_to_all | solution.py:816
  60.2 8.0 %scan_others.1 = (bf16[512,1024]{1,0:T(8,128)(2,1)}, f32[1,16,1024]{2,1,0:T(8,128)}) custom-call(s32[2]{0:T(128)} %pad_add_fusion.place_ref, bf16[1,256,1024]{2,1,0:T(8,128)(2,1)} %bitcast.11.stream_ref, bf16[256,1024]{1,0:T(8,128)(2,1)} %get-tuple-element.33.steps_ref, f32[4,32,128]{2,1,0:T(8,128)} %get-tuple-element.34.maps_ref, ...), custom_call_target="tpu_custom_call", output_to_operand_aliasing={{0}: (6, {})} | custom-call | flops 4000000000 | bytes 2097152 | tf_op jit(solution)/shard_map/scan_others/pallas_call | solution.py:629
  68.2 1.9 %all-to-all-done.carries_ref = bf16[8,144,128]{2,1,0:T(8,128)(2,1)S(1)} async-done(((bf16[8,144,128]{2,1,0:T(8,128)(2,1)}), bf16[8,144,128]{2,1,0:T(8,128)(2,1)S(1)}, u32[]{:S(2)}, u32[]{:S(2)}) %all-to-all-start) | async-done | bytes 294944 | tf_op jit(solution)/shard_map/all_to_all | solution.py:816
  70.1 0.7 copy-done.5
  70.8 9.2 %add_carried.1 = bf16[512,1024]{1,0:T(8,128)(2,1)} custom-call(s32[2]{0:T(128)} %pad_add_fusion.place_ref, bf16[512,1024]{1,0:T(8,128)(2,1)} %get-tuple-element.36.part_ref, bf16[512,1024]{1,0:T(8,128)(2,1)} %get-tuple-element.37.sums_ref, f32[4,32,128]{2,1,0:T(8,128)} %get-tuple-element.34.maps_ref, f32[16,1024]{1,0:T(8,128)} %get-tuple-element.29.rest_0_.last_own_ref, ...), custom_call_target="tpu_custom_call" | custom-call | tf_op jit(solution)/shard_map/add_carried/pallas_call | solution.py:734
  (4 shorter events, 0.0 us)
Async XLA Ops:
  0.6 14.3 %copy-start = (bf16[256,4096]{1,0:T(8,128)(2,1)S(1)}, bf16[256,4096]{1,0:T(8,128)(2,1)}, u32[]{:S(2)}) copy-start(bf16[256,4096]{1,0:T(8,128)(2,1)} %param.16) | copy-start | bytes 6291460
  2.7 17.0 %collective-permute-start = (bf16[128,4096]{1,0:T(8,128)(2,1)}, bf16[128,4096]{1,0:T(8,128)(2,1)S(1)}, u32[]{:S(2)}, u32[]{:S(2)}) collective-permute-start(bf16[128,4096]{1,0:T(8,128)(2,1)} %bitcast.28), channel_id=1, source_target_pairs={{0,8},{8,0},{16,24},{24,16},{1,9},{9,1},{17,25},{25,17},{2,10},{10... | collective-permute-start | bytes 3145736 | tf_op jit(solution)/shard_map/ppermute | solution.py:789
  3.3 12.5 %collective-permute-start.3 = (bf16[2,2,128,256]{3,2,1,0:T(8,128)(2,1)}, bf16[2,2,128,256]{3,2,1,0:T(8,128)(2,1)S(1)}, u32[]{:S(2)}, u32[]{:S(2)}) collective-permute-start(bf16[2,2,128,256]{3,2,1,0:T(8,128)(2,1)} %get-tuple-element.23), channel_id=1, source_target_pairs={{0,24},{8,16},{1,25},{9,17},{2,26},{10,18},{3,27},{11,19},{4,28},{... | collective-permute-start | bytes 786440 | tf_op jit(solution)/shard_map/ppermute | solution.py:786
  7.8 8.0 %collective-permute-start.1 = (bf16[2,2,128,256]{3,2,1,0:T(8,128)(2,1)}, bf16[2,2,128,256]{3,2,1,0:T(8,128)(2,1)}, u32[]{:S(2)}, u32[]{:S(2)}) collective-permute-start(bf16[2,2,128,256]{3,2,1,0:T(8,128)(2,1)} %get-tuple-element.23), channel_id=1, source_target_pairs={{0,8},{8,0},{16,24},{24,16},{1,9},{9,1},{17,25},{25,17},{2,10},{10... | collective-permute-start | bytes 786440 | tf_op jit(solution)/shard_map/ppermute | solution.py:787
  7.9 11.8 %collective-permute-start.2 = (bf16[2,2,128,256]{3,2,1,0:T(8,128)(2,1)}, bf16[2,2,128,256]{3,2,1,0:T(8,128)(2,1)}, u32[]{:S(2)}, u32[]{:S(2)}) collective-permute-start(bf16[2,2,128,256]{3,2,1,0:T(8,128)(2,1)} %get-tuple-element.21.own_ref), channel_id=1, source_target_pairs={{0,16},{8,24},{1,17},{9,25},{2,18},{10,26},{3,19},{11,27},{4,20},{... | collective-permute-start | bytes 786440 | tf_op jit(solution)/shard_map/ppermute | solution.py:785
  15.8 4.0 %copy-start.8 = (bf16[2,2,128,256]{3,2,1,0:T(8,128)(2,1)}, bf16[2,2,128,256]{3,2,1,0:T(8,128)(2,1)S(1)}, u32[]{:S(2)}) copy-start(bf16[2,2,128,256]{3,2,1,0:T(8,128)(2,1)S(1)} %collective-permute-done.3.far_ref) | copy-start | bytes 786436
  19.7 1.0 %copy-start.7 = (bf16[128,4096]{1,0:T(8,128)(2,1)}, bf16[128,4096]{1,0:T(8,128)(2,1)S(1)}, u32[]{:S(2)}) copy-start(bf16[128,4096]{1,0:T(8,128)(2,1)S(1)} %collective-permute-done.theirs_ref) | copy-start | bytes 3145732
  28.7 16.3 %collective-permute-start.5 = (bf16[256,1024]{1,0:T(8,128)(2,1)}, bf16[256,1024]{1,0:T(8,128)(2,1)}, u32[]{:S(2)}, u32[]{:S(2)}) collective-permute-start(bf16[256,1024]{1,0:T(8,128)(2,1)} %bitcast.15), channel_id=1, source_target_pairs={{0,16},{8,24},{16,0},{24,8},{1,17},{9,25},{17,1},{25,9},{2,18},{10... | collective-permute-start | bytes 1572872 | tf_op jit(solution)/shard_map/ppermute | solution.py:803
  31.3 13.8 %collective-permute-start.6 = (bf16[1,256,1024]{2,1,0:T(8,128)(2,1)}, bf16[1,256,1024]{2,1,0:T(8,128)(2,1)S(1)}, u32[]{:S(2)}, u32[]{:S(2)}) collective-permute-start(bf16[1,256,1024]{2,1,0:T(8,128)(2,1)} %get-tuple-element.25.stayed_ref.stream_ref), channel_id=1, source_target_pairs={{0,8},{8,0},{16,24},{24,16},{1,9},{9,1},{17,25},{25,17},{2,10},{10... | collective-permute-start | bytes 1572872 | tf_op jit(solution)/shard_map/ppermute | solution.py:807
  31.3 13.8 %collective-permute-start.4 = (bf16[1,256,1024]{2,1,0:T(8,128)(2,1)}, bf16[1,256,1024]{2,1,0:T(8,128)(2,1)}, u32[]{:S(2)}, u32[]{:S(2)}) collective-permute-start(bf16[1,256,1024]{2,1,0:T(8,128)(2,1)} %get-tuple-element.24.sent_ref), channel_id=1, source_target_pairs={{0,8},{8,0},{16,24},{24,16},{1,9},{9,1},{17,25},{25,17},{2,10},{10... | collective-permute-start | bytes 1572872 | tf_op jit(solution)/shard_map/ppermute | solution.py:806
  32.8 1.4 %collective-permute-start.7 = (bf16[288,256]{1,0:T(8,128)(2,1)S(1)}, bf16[288,256]{1,0:T(8,128)(2,1)S(1)}, u32[]{:S(2)}, u32[]{:S(2)}) collective-permute-start(bf16[288,256]{1,0:T(8,128)(2,1)S(1)} %convert_element_type.3), channel_id=1, source_target_pairs={{0,8},{8,0},{16,24},{24,16},{1,9},{9,1},{17,25},{25,17},{2,10},{10... | collective-permute-start | bytes 442376 | tf_op jit(solution)/shard_map/ppermute | solution.py:804
  34.2 1.0 %copy-start.1 = (f32[288,256]{1,0:T(8,128)S(1)}, f32[288,256]{1,0:T(8,128)}, u32[]{:S(2)}) copy-start(f32[288,256]{1,0:T(8,128)} %get-tuple-element.28.mine_ref) | copy-start | bytes 884740
  35.2 0.7 copy-start.4
  35.2 9.8 %copy-start.2 = (bf16[1,256,1024]{2,1,0:T(8,128)(2,1)S(1)}, bf16[1,256,1024]{2,1,0:T(8,128)(2,1)}, u32[]{:S(2)}) copy-start(bf16[1,256,1024]{2,1,0:T(8,128)(2,1)} %get-tuple-element.24.sent_ref) | copy-start | bytes 1572868
  35.2 9.8 %copy-start.3 = (bf16[1,256,1024]{2,1,0:T(8,128)(2,1)S(1)}, bf16[1,256,1024]{2,1,0:T(8,128)(2,1)}, u32[]{:S(2)}) copy-start(bf16[1,256,1024]{2,1,0:T(8,128)(2,1)} %get-tuple-element.25.stayed_ref.stream_ref) | copy-start | bytes 1572868
  35.2 11.9 %collective-permute-start.8 = (bf16[288,256]{1,0:T(8,128)(2,1)S(1)}, bf16[288,256]{1,0:T(8,128)(2,1)S(1)}, u32[]{:S(2)}, u32[]{:S(2)}) collective-permute-start(bf16[288,256]{1,0:T(8,128)(2,1)S(1)} %low_and_maps.1.low_ref.map_ref), channel_id=1, source_target_pairs={{0,16},{8,24},{16,0},{24,8},{1,17},{9,25},{17,1},{25,9},{2,18},{10... | collective-permute-start | bytes 442376 | tf_op jit(solution)/shard_map/ppermute | solution.py:805
  47.1 0.7 copy-start.6
  54.4 15.7 %all-to-all-start = ((bf16[8,144,128]{2,1,0:T(8,128)(2,1)}), bf16[8,144,128]{2,1,0:T(8,128)(2,1)S(1)}, u32[]{:S(2)}, u32[]{:S(2)}) async-start(bf16[8,144,128]{2,1,0:T(8,128)(2,1)} %get-tuple-element.39), calls=%async_computation | async-start | bytes 589824 | tf_op jit(solution)/shard_map/all_to_all | solution.py:816
  70.1 0.7 copy-start.5

commit v10 on v7

--- a/solution.py
+++ b/solution.py
@@ -694,7 +694,7 @@
         ).astype(jnp.bfloat16)
     last = sums_ref[rows - NS :, :].astype(jnp.float32)[NS - 1 :, :]
     state_ref[...] = jnp.exp2(rates_ref[...] * last) * state
-    chunk, several = CORES * LANES, 4
+    chunk, several = CORES * LANES, 8
 
     def some(index, nothing):
         near = pl.ds(pl.multiple_of(index * NS, NS), NS)
@@ -709,8 +709,9 @@
                     out_of = spread_ref[near, n * LANES : (n + 1) * LANES]
                     out_of = jnp.concatenate([out_of] * (chunk // LANES), axis=1)
                     terms.append(decay * begin_ref[n * NS : (n + 1) * NS, lanes] * out_of)
-                four = (terms[0] + terms[1]) + (terms[2] + terms[3])
-                total = total + four.astype(jnp.float32)
+                while len(terms) > 1:
+                    terms = [one + two for one, two in zip(terms[::2], terms[1::2])]
+                total = total + terms[0].astype(jnp.float32)
             out_ref[near, lanes] = total.astype(jnp.bfloat16)
         return nothing
 

time: 80.4 us -> 80.4 us (level)
  no operation moved by 1% of the time
where the time goes in v10:
time: 80.4 us; the launch traced here: 79.8 us
  Pallas kernels  46.8 us (58%)
  starting transfers between devices  17.6 us (22%)
  local copies, waits for them, and re-layouts  6.44 us (8%)
  waiting for transfers between devices  6.16 us (8%)
  other arithmetic  2.08 us (3%)
    pallas_call x1, Pallas kernels, add_carried(): pl.pallas_call(carried_kernel, grid_spec=pltpu.PrefetchScalarGridSpec(num...  9.16 us
    pallas_call x1, Pallas kernels, scan_own(): pl.pallas_call(own_kernel, grid_spec=pltpu.PrefetchScalarGridSpec(num_sca...  9.14 us
    pallas_call x1, Pallas kernels, attend(): pl.pallas_call(functools.partial(attend_kernel, chips=chips), grid_spec=p...  8.03 us
    pallas_call x1, Pallas kernels, scan_others(): pl.pallas_call(others_kernel, grid_spec=pltpu.PrefetchScalarGridSpec(num_...  8.01 us
    pallas_call x1, Pallas kernels, step_sizes(): pl.pallas_call(step_kernel, grid_spec=pltpu.PrefetchScalarGridSpec(num_sc...  6.58 us
    all_to_all x1, starting transfers between devices, local(): lax.all_to_all(carry, 'chan', split_axis=0, concat_axis=0, tiled=True)  5.82 us
    ppermute x1, starting transfers between devices, local(): from_far = lax.ppermute(theirs, 'seq', far)  4.54 us
    ppermute x1, waiting for transfers between devices, local(): from_near = lax.ppermute(own, 'seq', near)  4.03 us
  transfers between devices with their start and end apart: 10, of which 3 were waited for; matrix products, arithmetic and copies ran while one was open for 7% of the time, Pallas kernels for 26%

profile of v10, /device:TPU:0, one launch (start us, length us, event | category | flops | bytes accessed | tf_op | source)
XLA Modules:
  0.0 79.8 jit_solution(6773829084150866059)
XLA Ops:
  0.6 0.0 copy-start
  0.6 2.1 %select_heads.1 = (bf16[2,2,128,256]{3,2,1,0:T(8,128)(2,1)}, bf16[2,2,128,256]{3,2,1,0:T(8,128)(2,1)}) custom-call(bf16[128,1024]{1,0:T(8,128)(2,1)} %bitcast.20, bf16[128,1024]{1,0:T(8,128)(2,1)} %bitcast.21), custom_call_target="tpu_custom_call" | custom-call | tf_op jit(solution)/shard_map/select_heads/pallas_call | solution.py:62
  2.7 0.5 collective-permute-start
  3.3 4.5 %collective-permute-start.3 = (bf16[2,2,128,256]{3,2,1,0:T(8,128)(2,1)}, bf16[2,2,128,256]{3,2,1,0:T(8,128)(2,1)S(1)}, u32[]{:S(2)}, u32[]{:S(2)}) collective-permute-start(bf16[2,2,128,256]{3,2,1,0:T(8,128)(2,1)} %get-tuple-element.23), channel_id=1, source_target_pairs={{0,24},{8,16},{1,25},{9,17},{2,26},{10,18},{3,27},{11,19},{4,28},{... | collective-permute-start | bytes 786440 | tf_op jit(solution)/shard_map/ppermute | solution.py:786
  7.8 0.1 collective-permute-start.1
  7.9 2.3 %collective-permute-start.2 = (bf16[2,2,128,256]{3,2,1,0:T(8,128)(2,1)}, bf16[2,2,128,256]{3,2,1,0:T(8,128)(2,1)}, u32[]{:S(2)}, u32[]{:S(2)}) collective-permute-start(bf16[2,2,128,256]{3,2,1,0:T(8,128)(2,1)} %get-tuple-element.21.own_ref), channel_id=1, source_target_pairs={{0,16},{8,24},{1,17},{9,25},{2,18},{10,26},{3,19},{11,27},{4,20},{... | collective-permute-start | bytes 786440 | tf_op jit(solution)/shard_map/ppermute | solution.py:785
  10.2 0.6 pad_add_fusion.place_ref
  10.8 1.3 %dynamic_slice.14 = f32[1024]{0:T(1024)} dynamic-slice(f32[4096]{0:T(1024)} %param.17, s32[]{:T(128)S(6)} %select_n.12), dynamic_slice_sizes={1024} | dynamic-slice | bytes 8196 | tf_op jit(solution)/shard_map/dynamic_slice | solution.py:796
  12.1 1.3 %dynamic_slice.15 = f32[1024]{0:T(1024)} dynamic-slice(f32[4096]{0:T(1024)} %param.19, s32[]{:T(128)S(6)} %select_n.12), dynamic_slice_sizes={1024} | dynamic-slice | bytes 8196 | tf_op jit(solution)/shard_map/dynamic_slice | solution.py:797
  13.4 1.5 %multiply_bitcast_fusion.rest_0_.rates_ref = f32[16,1024]{1,0:T(8,128)} fusion(f32[4096,16]{0,1:T(8,128)} %param.18, s32[]{:T(128)S(6)} %select_n.12), kind=kLoop, calls=%fused_computation | loop fusion | flops 16384 | bytes 131076 | tf_op jit(solution)/shard_map/transpose | solution.py:794
  14.9 0.0 copy-done
  14.9 0.8 %constant_dynamic-slice_fusion.rest_1_.cols_ref = bf16[256,1024]{1,0:T(8,128)(2,1)} fusion(bf16[256,4096]{1,0:T(8,128)(2,1)S(1)} %copy-done, s32[]{:T(128)S(6)} %select_n.12), kind=kLoop, calls=%fused_computation.2 | loop fusion | bytes 1048580 | tf_op jit(solution)/shard_map/dynamic_slice | solution.py:795
  15.7 0.0 collective-permute-done.3.far_ref
  15.7 0.0 copy-start.7
  15.7 0.0 collective-permute-done.1.swap_ref
  15.7 4.0 %collective-permute-done.2.near_ref = bf16[2,2,128,256]{3,2,1,0:T(8,128)(2,1)} collective-permute-done((bf16[2,2,128,256]{3,2,1,0:T(8,128)(2,1)}, bf16[2,2,128,256]{3,2,1,0:T(8,128)(2,1)}, u32[]{:S(2)}, u32[]{:S(2)}) %collective-permute-start.2) | collective-permute-done | bytes 262176 | tf_op jit(solution)/shard_map/ppermute | solution.py:785
  19.7 0.0 collective-permute-done.theirs_ref
  19.7 0.0 copy-start.6
  19.7 0.0 copy-done.7
  19.7 1.0 %copy-done.6 = bf16[128,4096]{1,0:T(8,128)(2,1)} copy-done((bf16[128,4096]{1,0:T(8,128)(2,1)}, bf16[128,4096]{1,0:T(8,128)(2,1)S(1)}, u32[]{:S(2)}) %copy-start.6) | copy-done | bytes 1048600
  20.7 8.0 %attend.1 = (bf16[1,256,1024]{2,1,0:T(8,128)(2,1)}, bf16[1,256,1024]{2,1,0:T(8,128)(2,1)}, f32[288,256]{1,0:T(8,128)}) custom-call(s32[2]{0:T(128)} %pad_add_fusion.place_ref, s32[1,16]{1,0:T(1,128)} %doc_ref.1, bf16[128,4096]{1,0:T(8,128)(2,1)} %bitcast.29, bf16[128,4096]{1,0:T(8,128)(2,1)} %copy-done.6, ...), custom_call_target="tpu_custom_call" | custom-call | flops 5000000000 | bytes 4194304 | tf_op jit(solution)/shard_map/attend/pallas_call | solution.py:237
  28.7 0.1 collective-permute-start.7
  28.8 2.5 %collective-permute-start.5 = (bf16[256,1024]{1,0:T(8,128)(2,1)}, bf16[256,1024]{1,0:T(8,128)(2,1)}, u32[]{:S(2)}, u32[]{:S(2)}) collective-permute-start(bf16[256,1024]{1,0:T(8,128)(2,1)} %bitcast.15), channel_id=1, source_target_pairs={{0,16},{8,24},{16,0},{24,8},{1,17},{9,25},{17,1},{25,9},{2,18},{10... | collective-permute-start | bytes 1572872 | tf_op jit(solution)/shard_map/ppermute | solution.py:803
  31.4 0.2 collective-permute-start.6
  31.5 0.3 collective-permute-start.4
  31.9 0.0 collective-permute-done.7.theirs_ref
  31.9 0.0 copy-start.5
  31.9 0.7 copy-done.5
  32.6 1.7 %low_and_maps.1.low_ref.map_ref = bf16[288,256]{1,0:T(8,128)(2,1)} custom-call(f32[288,256]{1,0:T(8,128)} %get-tuple-element.28.mine_ref, f32[288,256]{1,0:T(8,128)} %copy-done.5), custom_call_target="tpu_custom_call" | custom-call | flops 1 | bytes 1 | tf_op jit(solution)/shard_map/low_and_maps/pallas_call | solution.py:275
  34.3 0.0 copy-start.1
  34.3 0.0 copy-start.2
  34.3 1.2 %collective-permute-start.8 = (bf16[288,256]{1,0:T(8,128)(2,1)}, bf16[288,256]{1,0:T(8,128)(2,1)S(1)}, u32[]{:S(2)}, u32[]{:S(2)}) collective-permute-start(bf16[288,256]{1,0:T(8,128)(2,1)} %low_and_maps.1.low_ref.map_ref), channel_id=1, source_target_pairs={{0,16},{8,24},{16,0},{24,8},{1,17},{9,25},{17,1},{25,9},{2,18},{10... | collective-permute-start | bytes 442376 | tf_op jit(solution)/shard_map/ppermute | solution.py:805
  35.5 9.1 %scan_own.1 = (bf16[512,1024]{1,0:T(8,128)(2,1)}, bf16[512,1024]{1,0:T(8,128)(2,1)}, f32[4,32,128]{2,1,0:T(8,128)}, f32[16,1024]{1,0:T(8,128)}, f32[1,1024]{1,0:T(1,128)}) custom-call(s32[2]{0:T(128)} %pad_add_fusion.place_ref, bf16[1,256,1024]{2,1,0:T(8,128)(2,1)} %get-tuple-element.25.stayed_ref.stream_ref, bf16[288,256]{1,0:T(8,128)(2,1)} %low_and_maps.1.low_ref.map_ref, ...), custom_call_target="tpu_custom_call" | custom-call | flops 4000000000 | bytes 2097152 | tf_op jit(solution)/shard_map/scan_own/pallas_call | solution.py:562
  44.7 0.0 collective-permute-done.5
  44.7 0.0 collective-permute-done.6.got_stayed_ref
  44.7 0.0 collective-permute-done.4.got_sent_ref
  44.7 0.0 copy-done.1
  44.7 0.0 copy-done.2
  44.7 2.0 %join_heads.1.rest_2_ = bf16[128,4096]{1,0:T(8,128)(2,1)} custom-call(bf16[1,256,1024]{2,1,0:T(8,128)(2,1)S(1)} %copy-done.1, bf16[1,256,1024]{2,1,0:T(8,128)(2,1)S(1)} %copy-done.2, bf16[1,256,1024]{2,1,0:T(8,128)(2,1)} %collective-permute-done.4.got_sent_ref, bf16[1,256,1024]{2,1,0:T(8,128)(2,1)S(1)} %collective-permute-done.6.got_stayed_ref), custom_call_target="tpu_custom_call" | custom-call | tf_op jit(solution)/shard_map/join_heads/pallas_call | solution.py:91
  46.8 0.5 collective-permute-done.8
  47.3 0.0 copy-start.4
  47.3 0.7 copy-done.4
  47.9 6.6 %step_sizes.1 = (bf16[256,1024]{1,0:T(8,128)(2,1)}, bf16[512,1024]{1,0:T(8,128)(2,1)}, f32[4,32,128]{2,1,0:T(8,128)}, bf16[8,144,128]{2,1,0:T(8,128)(2,1)}) custom-call(s32[2]{0:T(128)} %pad_add_fusion.place_ref, bf16[1,256,1024]{2,1,0:T(8,128)(2,1)} %bitcast.11.stream_ref, ...), custom_call_target="tpu_custom_call", output_to_operand_aliasing={{1}: (10, {}), {2}: (11, {})} | custom-call | tf_op jit(solution)/shard_map/step_sizes/pallas_call | solution.py:402
  54.5 5.8 %all-to-all-start = ((bf16[8,144,128]{2,1,0:T(8,128)(2,1)}), bf16[8,144,128]{2,1,0:T(8,128)(2,1)S(1)}, u32[]{:S(2)}, u32[]{:S(2)}) async-start(bf16[8,144,128]{2,1,0:T(8,128)(2,1)} %get-tuple-element.39), calls=%async_computation | async-start | bytes 589824 | tf_op jit(solution)/shard_map/all_to_all | solution.py:816
  60.3 8.0 %scan_others.1 = (bf16[512,1024]{1,0:T(8,128)(2,1)}, f32[1,16,1024]{2,1,0:T(8,128)}) custom-call(s32[2]{0:T(128)} %pad_add_fusion.place_ref, bf16[1,256,1024]{2,1,0:T(8,128)(2,1)} %bitcast.11.stream_ref, bf16[256,1024]{1,0:T(8,128)(2,1)} %get-tuple-element.33.steps_ref, f32[4,32,128]{2,1,0:T(8,128)} %get-tuple-element.34.maps_ref, ...), custom_call_target="tpu_custom_call", output_to_operand_aliasing={{0}: (6, {})} | custom-call | flops 4000000000 | bytes 2097152 | tf_op jit(solution)/shard_map/scan_others/pallas_call | solution.py:628
  68.3 1.6 %all-to-all-done.carries_ref = bf16[8,144,128]{2,1,0:T(8,128)(2,1)S(1)} async-done(((bf16[8,144,128]{2,1,0:T(8,128)(2,1)}), bf16[8,144,128]{2,1,0:T(8,128)(2,1)S(1)}, u32[]{:S(2)}, u32[]{:S(2)}) %all-to-all-start) | async-done | bytes 294944 | tf_op jit(solution)/shard_map/all_to_all | solution.py:816
  70.0 0.7 copy-done.3
  70.7 9.2 %add_carried.1 = bf16[512,1024]{1,0:T(8,128)(2,1)} custom-call(s32[2]{0:T(128)} %pad_add_fusion.place_ref, bf16[512,1024]{1,0:T(8,128)(2,1)} %get-tuple-element.36.part_ref, bf16[512,1024]{1,0:T(8,128)(2,1)} %get-tuple-element.37.sums_ref, f32[4,32,128]{2,1,0:T(8,128)} %get-tuple-element.34.maps_ref, f32[16,1024]{1,0:T(8,128)} %get-tuple-element.29.rest_0_.last_own_ref, ...), custom_call_target="tpu_custom_call" | custom-call | tf_op jit(solution)/shard_map/add_carried/pallas_call | solution.py:734
  (1 shorter events, 0.0 us)
Async XLA Ops:
  0.6 14.2 %copy-start = (bf16[256,4096]{1,0:T(8,128)(2,1)S(1)}, bf16[256,4096]{1,0:T(8,128)(2,1)}, u32[]{:S(2)}) copy-start(bf16[256,4096]{1,0:T(8,128)(2,1)} %param.16) | copy-start | bytes 6291460
  2.7 17.0 %collective-permute-start = (bf16[128,4096]{1,0:T(8,128)(2,1)}, bf16[128,4096]{1,0:T(8,128)(2,1)S(1)}, u32[]{:S(2)}, u32[]{:S(2)}) collective-permute-start(bf16[128,4096]{1,0:T(8,128)(2,1)} %bitcast.28), channel_id=1, source_target_pairs={{0,8},{8,0},{16,24},{24,16},{1,9},{9,1},{17,25},{25,17},{2,10},{10... | collective-permute-start | bytes 3145736 | tf_op jit(solution)/shard_map/ppermute | solution.py:789
  3.3 12.4 %collective-permute-start.3 = (bf16[2,2,128,256]{3,2,1,0:T(8,128)(2,1)}, bf16[2,2,128,256]{3,2,1,0:T(8,128)(2,1)S(1)}, u32[]{:S(2)}, u32[]{:S(2)}) collective-permute-start(bf16[2,2,128,256]{3,2,1,0:T(8,128)(2,1)} %get-tuple-element.23), channel_id=1, source_target_pairs={{0,24},{8,16},{1,25},{9,17},{2,26},{10,18},{3,27},{11,19},{4,28},{... | collective-permute-start | bytes 786440 | tf_op jit(solution)/shard_map/ppermute | solution.py:786
  7.8 7.9 %collective-permute-start.1 = (bf16[2,2,128,256]{3,2,1,0:T(8,128)(2,1)}, bf16[2,2,128,256]{3,2,1,0:T(8,128)(2,1)}, u32[]{:S(2)}, u32[]{:S(2)}) collective-permute-start(bf16[2,2,128,256]{3,2,1,0:T(8,128)(2,1)} %get-tuple-element.23), channel_id=1, source_target_pairs={{0,8},{8,0},{16,24},{24,16},{1,9},{9,1},{17,25},{25,17},{2,10},{10... | collective-permute-start | bytes 786440 | tf_op jit(solution)/shard_map/ppermute | solution.py:787
  7.9 11.8 %collective-permute-start.2 = (bf16[2,2,128,256]{3,2,1,0:T(8,128)(2,1)}, bf16[2,2,128,256]{3,2,1,0:T(8,128)(2,1)}, u32[]{:S(2)}, u32[]{:S(2)}) collective-permute-start(bf16[2,2,128,256]{3,2,1,0:T(8,128)(2,1)} %get-tuple-element.21.own_ref), channel_id=1, source_target_pairs={{0,16},{8,24},{1,17},{9,25},{2,18},{10,26},{3,19},{11,27},{4,20},{... | collective-permute-start | bytes 786440 | tf_op jit(solution)/shard_map/ppermute | solution.py:785
  15.7 4.0 %copy-start.7 = (bf16[2,2,128,256]{3,2,1,0:T(8,128)(2,1)}, bf16[2,2,128,256]{3,2,1,0:T(8,128)(2,1)S(1)}, u32[]{:S(2)}) copy-start(bf16[2,2,128,256]{3,2,1,0:T(8,128)(2,1)S(1)} %collective-permute-done.3.far_ref) | copy-start | bytes 786436
  19.7 1.0 %copy-start.6 = (bf16[128,4096]{1,0:T(8,128)(2,1)}, bf16[128,4096]{1,0:T(8,128)(2,1)S(1)}, u32[]{:S(2)}) copy-start(bf16[128,4096]{1,0:T(8,128)(2,1)S(1)} %collective-permute-done.theirs_ref) | copy-start | bytes 3145732
  28.7 3.1 %collective-permute-start.7 = (f32[288,256]{1,0:T(8,128)}, f32[288,256]{1,0:T(8,128)S(1)}, u32[]{:S(2)}, u32[]{:S(2)}) collective-permute-start(f32[288,256]{1,0:T(8,128)} %get-tuple-element.28.mine_ref), channel_id=1, source_target_pairs={{0,8},{8,0},{16,24},{24,16},{1,9},{9,1},{17,25},{25,17},{2,10},{10... | collective-permute-start | bytes 884744 | tf_op jit(solution)/shard_map/ppermute | solution.py:804
  28.8 15.9 %collective-permute-start.5 = (bf16[256,1024]{1,0:T(8,128)(2,1)}, bf16[256,1024]{1,0:T(8,128)(2,1)}, u32[]{:S(2)}, u32[]{:S(2)}) collective-permute-start(bf16[256,1024]{1,0:T(8,128)(2,1)} %bitcast.15), channel_id=1, source_target_pairs={{0,16},{8,24},{16,0},{24,8},{1,17},{9,25},{17,1},{25,9},{2,18},{10... | collective-permute-start | bytes 1572872 | tf_op jit(solution)/shard_map/ppermute | solution.py:803
  31.4 13.3 %collective-permute-start.6 = (bf16[1,256,1024]{2,1,0:T(8,128)(2,1)}, bf16[1,256,1024]{2,1,0:T(8,128)(2,1)S(1)}, u32[]{:S(2)}, u32[]{:S(2)}) collective-permute-start(bf16[1,256,1024]{2,1,0:T(8,128)(2,1)} %get-tuple-element.25.stayed_ref.stream_ref), channel_id=1, source_target_pairs={{0,8},{8,0},{16,24},{24,16},{1,9},{9,1},{17,25},{25,17},{2,10},{10... | collective-permute-start | bytes 1572872 | tf_op jit(solution)/shard_map/ppermute | solution.py:807
  31.5 13.2 %collective-permute-start.4 = (bf16[1,256,1024]{2,1,0:T(8,128)(2,1)}, bf16[1,256,1024]{2,1,0:T(8,128)(2,1)}, u32[]{:S(2)}, u32[]{:S(2)}) collective-permute-start(bf16[1,256,1024]{2,1,0:T(8,128)(2,1)} %get-tuple-element.24.sent_ref), channel_id=1, source_target_pairs={{0,8},{8,0},{16,24},{24,16},{1,9},{9,1},{17,25},{25,17},{2,10},{10... | collective-permute-start | bytes 1572872 | tf_op jit(solution)/shard_map/ppermute | solution.py:806
  31.9 0.7 copy-start.5
  34.3 10.4 %copy-start.1 = (bf16[1,256,1024]{2,1,0:T(8,128)(2,1)S(1)}, bf16[1,256,1024]{2,1,0:T(8,128)(2,1)}, u32[]{:S(2)}) copy-start(bf16[1,256,1024]{2,1,0:T(8,128)(2,1)} %get-tuple-element.24.sent_ref) | copy-start | bytes 1572868
  34.3 10.4 %copy-start.2 = (bf16[1,256,1024]{2,1,0:T(8,128)(2,1)S(1)}, bf16[1,256,1024]{2,1,0:T(8,128)(2,1)}, u32[]{:S(2)}) copy-start(bf16[1,256,1024]{2,1,0:T(8,128)(2,1)} %get-tuple-element.25.stayed_ref.stream_ref) | copy-start | bytes 1572868
  34.3 12.9 %collective-permute-start.8 = (bf16[288,256]{1,0:T(8,128)(2,1)}, bf16[288,256]{1,0:T(8,128)(2,1)S(1)}, u32[]{:S(2)}, u32[]{:S(2)}) collective-permute-start(bf16[288,256]{1,0:T(8,128)(2,1)} %low_and_maps.1.low_ref.map_ref), channel_id=1, source_target_pairs={{0,16},{8,24},{16,0},{24,8},{1,17},{9,25},{17,1},{25,9},{2,18},{10... | collective-permute-start | bytes 442376 | tf_op jit(solution)/shard_map/ppermute | solution.py:805
  47.3 0.7 copy-start.4
  54.5 15.5 %all-to-all-start = ((bf16[8,144,128]{2,1,0:T(8,128)(2,1)}), bf16[8,144,128]{2,1,0:T(8,128)(2,1)S(1)}, u32[]{:S(2)}, u32[]{:S(2)}) async-start(bf16[8,144,128]{2,1,0:T(8,128)(2,1)} %get-tuple-element.39), calls=%async_computation | async-start | bytes 589824 | tf_op jit(solution)/shard_map/all_to_all | solution.py:816
  70.0 0.7 copy-start.3
